TPU v7x, 32 devices: a whole 2x2x4 slice. The times are simulated.
32 devices in a mesh: section: 2 (over core), ctx: 4 (over z), tensor: 4 (over y, x).
Axes of the slice: x: 2, y: 2, z: 4, core: 2. Of those that a mesh axis runs over, the one named last changes fastest.
Arguments:
- tokens: bfloat16 [4, 1024, 1536], P(None, 'ctx'), may hold values from -6 to 6
- cotangent: bfloat16 [4, 1024, 1536], P(None, 'ctx'), may hold values from -6 to 6
- seg_ids: int32 [4, 1024], replicated, may hold values from 0 to 1, as said below
- norm_gain: bfloat16 [2, 1536], P('section'), may hold values from 0.099609375 to 1.8984375
- in_zx: bfloat16 [2, 1536, 2, 3072], P('section', 'ctx', None, 'tensor'), may hold values from -0.15625 to 0.15625
- in_bc: bfloat16 [2, 1536, 256], P('section', 'ctx'), may hold values from -0.15625 to 0.15625
- in_dt: bfloat16 [2, 1536, 48], P('section', 'ctx', 'tensor'), may hold values from -0.15625 to 0.15625
- conv_x: bfloat16 [2, 4, 3072], P('section', None, 'tensor'), may hold values from -3 to 3
- conv_xb: bfloat16 [2, 3072], P('section', 'tensor'), may hold values from -3 to 3
- conv_bc: bfloat16 [2, 4, 256], P('section'), may hold values from -3 to 3
- conv_bcb: bfloat16 [2, 256], P('section'), may hold values from -3 to 3
- dt_bias: float32 [2, 48], P('section', 'tensor'), may hold values from -3 to 0
- a_log: float32 [2, 48], P('section', 'tensor'), may hold values from -12 to -1
- skip_gain: float32 [2, 48], P('section', 'tensor'), may hold values from 0.5 to 1.5
- gate_gain: bfloat16 [2, 3072], P('section', 'tensor'), may hold values from 0.099609375 to 1.8984375
- out_w: bfloat16 [2, 3072, 1536], P('section', 'tensor', 'ctx'), may hold values from -0.109375 to 0.109375
Outputs:
- section_outputs: bfloat16 [2, 4, 1024, 1536], P('section', None, 'ctx')
- input_grads: float32 [2, 4, 1024, 1536], P('section', None, 'ctx')
- grad_norm_gain: float32 [2, 1536], P('section')
- grad_in_zx: float32 [2, 1536, 2, 3072], P('section', 'ctx', None, 'tensor')
- grad_in_bc: float32 [2, 1536, 256], P('section', 'ctx')
- grad_in_dt: float32 [2, 1536, 48], P('section', 'ctx', 'tensor')
- grad_conv_x: float32 [2, 4, 3072], P('section', None, 'tensor')
- grad_conv_xb: float32 [2, 3072], P('section', 'tensor')
- grad_conv_bc: float32 [2, 4, 256], P('section')
- grad_conv_bcb: float32 [2, 256], P('section')
- grad_dt_bias: float32 [2, 48], P('section', 'tensor')
- grad_a_log: float32 [2, 48], P('section', 'tensor')
- grad_skip_gain: float32 [2, 48], P('section', 'tensor')
- grad_gate_gain: float32 [2, 3072], P('section', 'tensor')
- grad_out_w: float32 [2, 3072, 1536], P('section', 'tensor', 'ctx')
Inputs may be any that keep to these rules, and one draw needn't show every extreme that they name: `seg_ids`: ids never fall along each micro-batch's 1024 tokens and start at 0 in each; equal ids mark one document. One micro-batch is a single document; in each other one, every aligned block of 512 tokens but the first holds exactly one document start, so its ids run from 0 to 1.
All inputs are finite; a program needn't handle non-finite values.
Results may differ from a plain program's by a relative error of at most 0.0131.
The roundings to bfloat16 on the way count: a program that leaves them out, or rounds other values in their place, can miss the bound.
Values may be sent and summed in bfloat16 or wider, within the bound.
No kernel may reach another device: no remote copies, remote signals or barrier semaphores. Data moves between devices by JAX's collectives and lax.ppermute only.
A program may use at most 256 MiB of HBM per device.

v0:
```python
from functools import partial

import jax
import jax.numpy as jnp
from jax import lax
from jax.sharding import PartitionSpec as P

N = 128
KC = 4
CH = 256
DI = 3072


epsilon = 1e-05
precise = lax.Precision.HIGHEST


def from_behind(block, axis, distance):
    devices = range(lax.axis_size(axis))
    route = [(i - distance, i) for i in devices if i - distance in devices]
    return lax.ppermute(block, axis, route)


def prefix(value, axis, join, neutral, backward):
    count, mine = (lax.axis_size(axis), lax.axis_index(axis))
    pieces = jax.tree.map(lambda part: lax.all_gather(part, axis), value)
    if backward:
        pieces = jax.tree.map(lambda part: part[::-1], pieces)
        mine = count - 1 - mine
    total = jax.tree.map(
        lambda part, zero: jnp.full_like(part, 0) + jnp.asarray(zero, part.dtype), value, neutral
    )

    def hop(position, total):
        longer = join(total, jax.tree.map(lambda part: part[position], pieces))
        return jax.tree.map(lambda new, old: jnp.where(position < mine, new, old), longer, total)

    return lax.fori_loop(0, count - 1, hop, total)


def block_step(decay_rate, carried, inputs):
    state_now, seg_before = carried
    x_block, rate_block, b_block, c_block, seg_block = inputs
    cumulative = jnp.cumsum(rate_block * decay_rate[None, :], axis=0)
    width_block = seg_block.shape[0]
    row_index = lax.broadcasted_iota(jnp.int32, (width_block, width_block), 0)
    col_index = lax.broadcasted_iota(jnp.int32, (width_block, width_block), 1)
    within = (row_index >= col_index) & (seg_block[:, None] == seg_block[None, :])
    within_heads = within[:, :, None]
    spread = cumulative[:, None, :] - cumulative[None, :, :]
    decay = jnp.where(within_heads, jnp.exp(jnp.where(within_heads, spread, 0.0)), 0.0)
    scores = jnp.dot(c_block, b_block.T, precision=precise)
    weights = scores[:, :, None] * decay * rate_block[None, :, :]
    output = jnp.einsum("tsh,shp->thp", weights, x_block, precision=precise)
    entering = jnp.exp(cumulative) * (seg_block == seg_before)[:, None].astype(jnp.float32)
    output = output + entering[:, :, None] * jnp.einsum(
        "tn,hpn->thp", c_block, state_now, precision=precise
    )
    leaving = (
        jnp.exp(cumulative[-1][None, :] - cumulative)
        * (seg_block == seg_block[-1])[:, None].astype(jnp.float32)
        * rate_block
    )
    state_next = entering[-1][:, None, None] * state_now + jnp.einsum(
        "sh,shp,sn->hpn", leaving, x_block, b_block, precision=precise
    )
    return ((state_next, seg_block[-1]), output)


def scan_blocks(x_heads, step_rate, b_part, c_part, seg_own, decay_rate, state_start, seg_start):
    blocks = x_heads.shape[0] // CH

    def to_blocks(value):
        return value.reshape((blocks, CH) + value.shape[1:])

    stepper = jax.checkpoint(partial(block_step, decay_rate))
    final_carry, output = lax.scan(
        stepper,
        (state_start, seg_start),
        (
            to_blocks(x_heads),
            to_blocks(step_rate),
            to_blocks(b_part),
            to_blocks(c_part),
            to_blocks(seg_own),
        ),
    )
    return (output.reshape(x_heads.shape), final_carry[0])


def causal_conv(padded_in, kernel, offset, seg_padded):
    own_rows = padded_in.shape[0] - (KC - 1)
    current = seg_padded[KC - 1 :]
    summed = jnp.zeros((own_rows, padded_in.shape[1]), jnp.float32) + offset[None, :]
    for tap_index in range(KC):
        shifted = padded_in[tap_index : tap_index + own_rows]
        same_doc = (seg_padded[tap_index : tap_index + own_rows] == current).astype(jnp.float32)
        summed = summed + kernel[tap_index][None, :] * shifted * same_doc[:, None]
    return summed


def chain_combine(earlier, later):
    return (earlier[0] * later[0], earlier[1] * later[0][:, None, None] + later[1])


def project_in(layer_in, gain_row, zx_full, bc_full, dt_full):
    inputs_f = layer_in.astype(jnp.float32)
    in_scale = lax.rsqrt(jnp.mean(inputs_f * inputs_f, axis=1) + epsilon)
    normed = (inputs_f * in_scale[:, None] * gain_row[None, :]).astype(jnp.bfloat16)
    model_width = zx_full.shape[0]
    inner_local = zx_full.shape[2]
    joined = jnp.dot(
        normed, zx_full.reshape(model_width, 2 * inner_local), preferred_element_type=jnp.float32
    )
    bc_pre = jnp.dot(normed, bc_full, preferred_element_type=jnp.float32)
    mixed_pre = jnp.concatenate([joined[:, inner_local:], bc_pre], axis=1).astype(jnp.bfloat16)
    step_pre = jnp.dot(normed, dt_full, preferred_element_type=jnp.float32)
    return (inputs_f, in_scale, normed, joined[:, :inner_local], mixed_pre, step_pre)


def mixer_parts(padded_in, step_pre, kernel, offset, bias_row, log_rate, seg_padded, heads_local):
    own_rows = step_pre.shape[0]
    inner_local = padded_in.shape[1] - 2 * N
    head_size = inner_local // heads_local
    conv_out = jax.nn.silu(causal_conv(padded_in, kernel, offset, seg_padded))
    x_heads = conv_out[:, :inner_local].reshape(own_rows, heads_local, head_size)
    b_part = conv_out[:, inner_local : inner_local + N]
    c_part = conv_out[:, inner_local + N :]
    step_rate = jax.nn.softplus(step_pre + bias_row[None, :])
    decay_rate = -jnp.exp(log_rate)
    seg_own = seg_padded[KC - 1 :]
    seg_start = seg_padded[KC - 2]
    local_out, local_state = scan_blocks(
        x_heads,
        step_rate,
        b_part,
        c_part,
        seg_own,
        decay_rate,
        jnp.zeros((heads_local, head_size, N), jnp.float32),
        seg_start,
    )
    carried = jnp.exp(jnp.cumsum(step_rate * decay_rate[None, :], axis=0)) * (seg_own == seg_start)[
        :, None
    ].astype(jnp.float32)
    return (x_heads, c_part, local_out, local_state, carried)


def mixer_tail(parts, state_in, gate_pre, skip_row):
    x_heads, c_part, local_out, local_state, carried = parts
    own_rows = gate_pre.shape[0]
    ssm_out = (
        local_out
        + carried[:, :, None] * jnp.einsum("tn,hpn->thp", c_part, state_in, precision=precise)
        + skip_row[None, :, None] * x_heads
    )
    gate_act = jax.nn.silu(gate_pre)
    gated = ssm_out.reshape(own_rows, gate_pre.shape[1]) * gate_act
    state_out = carried[-1][:, None, None] * state_in + local_state
    return ((gated, state_out), (carried, c_part, gate_act))


def select_batch(array_in, chosen):
    return lax.dynamic_index_in_dim(array_in, chosen, 0, keepdims=False)


def store_batch(buffer, value, chosen, valid):
    return jnp.where(valid, lax.dynamic_update_index_in_dim(buffer, value, chosen, 0), buffer)


def body(
    tokens,
    cotangent,
    seg_ids,
    norm_gain,
    in_zx,
    in_bc,
    in_dt,
    conv_x,
    conv_xb,
    conv_bc,
    conv_bcb,
    dt_bias,
    a_log,
    skip_gain,
    gate_gain,
    out_w,
):
    section_index = lax.axis_index("section")
    ctx_index = lax.axis_index("ctx")
    tensor_index = lax.axis_index("tensor")
    section_count = lax.axis_size("section")
    tensor_count = lax.axis_size("tensor")
    batches = tokens.shape[0]
    token_rows = tokens.shape[1]
    model_width = tokens.shape[2]
    zx_full, bc_full, dt_full, out_full = (
        lax.all_gather(in_zx[0], "ctx", axis=0, tiled=True),
        lax.all_gather(in_bc[0], "ctx", axis=0, tiled=True),
        lax.all_gather(in_dt[0], "ctx", axis=0, tiled=True),
        lax.all_gather(out_w[0], "ctx", axis=1, tiled=True),
    )
    inner_local = zx_full.shape[2]
    heads_local = dt_full.shape[1]
    head_size = inner_local // heads_local
    mixed_width = inner_local + 2 * N
    gain_row = norm_gain[0].astype(jnp.float32)
    kernel = jnp.concatenate([conv_x[0], conv_bc[0]], axis=1).astype(jnp.float32)
    offset = jnp.concatenate([conv_xb[0], conv_bcb[0]]).astype(jnp.float32)
    bias_row = dt_bias[0]
    log_rate = a_log[0]
    skip_row = skip_gain[0]
    gate_row = gate_gain[0].astype(jnp.float32)
    seg_lead = jnp.full((batches, KC - 1), -1, jnp.int32)
    seg_all = jnp.concatenate([seg_lead, seg_ids], axis=1)
    seg_local = lax.dynamic_slice_in_dim(seg_all, ctx_index * token_rows, token_rows + KC - 1, 1)
    chain_start = (
        jnp.ones((heads_local,), jnp.float32),
        jnp.zeros((heads_local, head_size, N), jnp.float32),
    )
    kept_inputs = jnp.zeros((batches, token_rows, model_width), jnp.bfloat16)
    kept_states = jnp.zeros((batches, heads_local, head_size, N), jnp.float32)
    kept_scales = jnp.zeros((batches, token_rows), jnp.float32)
    kept_edges = jnp.zeros((batches, KC - 1, mixed_width), jnp.bfloat16)
    section_store = jnp.zeros((batches, token_rows, model_width), jnp.bfloat16)
    received = jnp.zeros((token_rows, model_width), jnp.bfloat16)
    for tick_number in range(batches + section_count - 1):
        batch_index = tick_number - section_index
        valid = (batch_index >= 0) & (batch_index < batches)
        chosen = jnp.clip(batch_index, 0, batches - 1)
        layer_in = jnp.where(section_index == 0, select_batch(tokens, chosen), received)
        seg_padded = select_batch(seg_local, chosen)
        inputs_f, in_scale, normed, gate_pre, mixed_pre, step_pre = project_in(
            layer_in, gain_row, zx_full, bc_full, dt_full
        )
        edge_rows = from_behind(mixed_pre[token_rows - (KC - 1) :], "ctx", 1)
        padded_in = jnp.concatenate([edge_rows, mixed_pre], axis=0).astype(jnp.float32)
        parts = mixer_parts(
            padded_in, step_pre, kernel, offset, bias_row, log_rate, seg_padded, heads_local
        )
        state_in = prefix((parts[4][-1], parts[3]), "ctx", chain_combine, chain_start, False)[1]
        gated = mixer_tail(parts, state_in, gate_pre, skip_row)[0][0]
        squares = lax.psum(jnp.sum(gated * gated, axis=1), "tensor")
        gate_scale = lax.rsqrt(squares / DI + epsilon)
        gate_normed = (gated * gate_scale[:, None] * gate_row[None, :]).astype(jnp.bfloat16)
        projected = lax.psum(
            jnp.dot(gate_normed, out_full, preferred_element_type=jnp.float32), "tensor"
        )
        layer_out = (inputs_f + projected).astype(jnp.bfloat16)
        kept_inputs = store_batch(kept_inputs, layer_in, chosen, valid)
        kept_states = store_batch(kept_states, state_in, chosen, valid)
        kept_scales = store_batch(kept_scales, gate_scale, chosen, valid)
        kept_edges = store_batch(kept_edges, edge_rows, chosen, valid)
        section_store = store_batch(section_store, layer_out, chosen, valid)
        received = from_behind(layer_out, "section", 1)
    acc_zx = jnp.zeros((model_width, 2 * inner_local), jnp.float32)
    acc_dt = jnp.zeros((model_width, heads_local), jnp.float32)
    acc_out = jnp.zeros((inner_local, model_width), jnp.float32)
    acc_bc = jnp.zeros((model_width, 2 * N), jnp.float32)
    acc_gain = jnp.zeros((model_width,), jnp.float32)
    acc_kernel = jnp.zeros((KC, mixed_width), jnp.float32)
    acc_offset = jnp.zeros((mixed_width,), jnp.float32)
    acc_bias = jnp.zeros((heads_local,), jnp.float32)
    acc_log = jnp.zeros((heads_local,), jnp.float32)
    acc_skip = jnp.zeros((heads_local,), jnp.float32)
    acc_gate = jnp.zeros((inner_local,), jnp.float32)
    grad_store = jnp.zeros((batches, token_rows, model_width), jnp.float32)
    received_grad = jnp.zeros((token_rows, model_width), jnp.bfloat16)
    last_section = section_count - 1
    contract = (((0,), (0,)), ((), ()))
    for tick_number in range(batches + section_count - 1):
        batch_index = batches - 1 - tick_number + (last_section - section_index)
        valid = (batch_index >= 0) & (batch_index < batches)
        chosen = jnp.clip(batch_index, 0, batches - 1)
        out_grad = jnp.where(
            section_index == last_section, select_batch(cotangent, chosen), received_grad
        )
        seg_padded = select_batch(seg_local, chosen)
        inputs_f, in_scale, normed, gate_pre, mixed_pre, step_pre = project_in(
            select_batch(kept_inputs, chosen), gain_row, zx_full, bc_full, dt_full
        )
        padded_in = jnp.concatenate([select_batch(kept_edges, chosen), mixed_pre], axis=0).astype(
            jnp.float32
        )
        state_in = select_batch(kept_states, chosen)
        gate_scale = select_batch(kept_scales, chosen)

        def local_mixer(
            padded_arg,
            gate_arg,
            step_arg,
            state_arg,
            kernel_arg,
            offset_arg,
            bias_arg,
            log_arg,
            skip_arg,
        ):
            return mixer_tail(
                mixer_parts(
                    padded_arg,
                    step_arg,
                    kernel_arg,
                    offset_arg,
                    bias_arg,
                    log_arg,
                    seg_padded,
                    heads_local,
                ),
                state_arg,
                gate_arg,
                skip_arg,
            )

        outputs, pullback, extras = jax.vjp(
            local_mixer,
            padded_in,
            gate_pre,
            step_pre,
            state_in,
            kernel,
            offset,
            bias_row,
            log_rate,
            skip_row,
            has_aux=True,
        )
        gated = outputs[0]
        carried, c_part, gate_act = extras
        gate_normed = (gated * gate_scale[:, None] * gate_row[None, :]).astype(jnp.bfloat16)
        normed_gate_grad = jnp.dot(out_grad, out_full.T, preferred_element_type=jnp.float32)
        out_term = lax.dot_general(
            gate_normed, out_grad, contract, preferred_element_type=jnp.float32
        )
        gate_term = jnp.sum(normed_gate_grad * gated * gate_scale[:, None], axis=0)
        projection = lax.psum(
            jnp.sum(normed_gate_grad * gate_row[None, :] * gated, axis=1), "tensor"
        )
        gated_grad = (
            gate_scale[:, None] * gate_row[None, :] * normed_gate_grad
            - gated * (gate_scale**3 * projection / DI)[:, None]
        )
        out_heads = (gated_grad * gate_act).reshape(token_rows, heads_local, head_size)
        pull_state = jnp.einsum("th,thp,tn->hpn", carried, out_heads, c_part, precision=precise)
        state_after = prefix((carried[-1], pull_state), "ctx", chain_combine, chain_start, True)[1]
        (
            padded_grad,
            gate_grad,
            step_grad,
            unused_state,
            kernel_grad,
            offset_grad,
            bias_grad,
            log_grad,
            skip_grad,
        ) = pullback((gated_grad, state_after))
        edge_grad = from_behind(padded_grad[: KC - 1], "ctx", -1)
        mixed_grad = padded_grad[KC - 1 :].at[token_rows - (KC - 1) :].add(edge_grad)
        zx_grad = jnp.concatenate(
            [gate_grad.astype(jnp.bfloat16), mixed_grad[:, :inner_local].astype(jnp.bfloat16)],
            axis=1,
        )
        bc_grad = mixed_grad[:, inner_local:]
        step_low = step_grad.astype(jnp.bfloat16)
        normed_grad = jnp.dot(
            zx_grad,
            zx_full.reshape(model_width, 2 * inner_local).T,
            preferred_element_type=jnp.float32,
        )
        normed_grad = normed_grad + jnp.dot(step_low, dt_full.T, preferred_element_type=jnp.float32)
        normed_grad = normed_grad + jnp.dot(
            bc_grad, bc_full.astype(jnp.float32).T, precision=precise
        )
        zx_term = lax.dot_general(normed, zx_grad, contract, preferred_element_type=jnp.float32)
        dt_term = lax.dot_general(normed, step_low, contract, preferred_element_type=jnp.float32)
        bc_term = lax.dot_general(normed.astype(jnp.float32), bc_grad, contract, precision=precise)
        normed_grad = lax.psum(normed_grad.astype(jnp.bfloat16), "tensor").astype(jnp.float32)
        normed_x = inputs_f * in_scale[:, None]
        weighted = gain_row[None, :] * normed_grad
        input_grad = out_grad.astype(jnp.float32) + in_scale[:, None] * (
            weighted - normed_x * jnp.mean(weighted * normed_x, axis=1)[:, None]
        )
        norm_term = jnp.sum(normed_grad * normed_x, axis=0)
        sent_grad = input_grad.astype(jnp.bfloat16)
        grad_store = store_batch(
            grad_store,
            jnp.where(section_index == 0, input_grad, sent_grad.astype(jnp.float32)),
            chosen,
            valid,
        )
        acc_zx = jnp.where(valid, acc_zx + zx_term, acc_zx)
        acc_dt = jnp.where(valid, acc_dt + dt_term, acc_dt)
        acc_out = jnp.where(valid, acc_out + out_term, acc_out)
        acc_bc = jnp.where(valid, acc_bc + bc_term, acc_bc)
        acc_gain = jnp.where(valid, acc_gain + norm_term, acc_gain)
        acc_kernel = jnp.where(valid, acc_kernel + kernel_grad, acc_kernel)
        acc_offset = jnp.where(valid, acc_offset + offset_grad, acc_offset)
        acc_bias = jnp.where(valid, acc_bias + bias_grad, acc_bias)
        acc_log = jnp.where(valid, acc_log + log_grad, acc_log)
        acc_skip = jnp.where(valid, acc_skip + skip_grad, acc_skip)
        acc_gate = jnp.where(valid, acc_gate + gate_term, acc_gate)
        received_grad = from_behind(sent_grad, "section", -1)
    zx_sum, dt_sum, out_sum = (
        lax.psum_scatter(
            acc_zx.reshape(model_width, 2, inner_local).astype(jnp.bfloat16),
            "ctx",
            scatter_dimension=0,
            tiled=True,
        ).astype(jnp.float32),
        lax.psum_scatter(
            acc_dt.astype(jnp.bfloat16), "ctx", scatter_dimension=0, tiled=True
        ).astype(jnp.float32),
        lax.psum_scatter(
            acc_out.astype(jnp.bfloat16), "ctx", scatter_dimension=1, tiled=True
        ).astype(jnp.float32),
    )
    first_tensor = (tensor_index == 0).astype(jnp.float32)

    def widen(piece):
        full_shape = piece.shape[:-1] + (piece.shape[-1] * tensor_count,)
        return lax.dynamic_update_slice_in_dim(
            jnp.zeros(full_shape, jnp.float32),
            piece,
            tensor_index * piece.shape[-1],
            piece.ndim - 1,
        )

    def narrow(full_array):
        own_width = full_array.shape[-1] // tensor_count
        return lax.dynamic_slice_in_dim(
            full_array, tensor_index * own_width, own_width, full_array.ndim - 1
        )

    sums = lax.psum(
        (
            acc_bc,
            acc_gain * first_tensor,
            acc_kernel[:, inner_local:],
            acc_offset[inner_local:],
            widen(acc_kernel[:, :inner_local]),
            widen(acc_offset[:inner_local]),
            widen(acc_bias),
            widen(acc_log),
            widen(acc_skip),
            widen(acc_gate),
        ),
        ("ctx", "tensor"),
    )
    rows_own = in_bc.shape[1]
    bc_rows = lax.dynamic_slice_in_dim(sums[0], ctx_index * rows_own, rows_own, 0)
    return (
        section_store[None],
        grad_store[None],
        sums[1][None],
        zx_sum[None],
        bc_rows[None],
        dt_sum[None],
        narrow(sums[4])[None],
        narrow(sums[5])[None],
        sums[2][None],
        sums[3][None],
        narrow(sums[6])[None],
        narrow(sums[7])[None],
        narrow(sums[8])[None],
        narrow(sums[9])[None],
        out_sum[None],
    )


def solution(mesh):
    return jax.shard_map(
        body,
        mesh=mesh,
        in_specs=(
            P(None, "ctx", None),
            P(None, "ctx", None),
            P(),
            P("section", None),
            P("section", "ctx", None, "tensor"),
            P("section", "ctx", None),
            P("section", "ctx", "tensor"),
            P("section", None, "tensor"),
            P("section", "tensor"),
            P("section", None, None),
            P("section", None),
            P("section", "tensor"),
            P("section", "tensor"),
            P("section", "tensor"),
            P("section", "tensor"),
            P("section", "tensor", "ctx"),
        ),
        out_specs=(
            P("section", None, "ctx", None),
            P("section", None, "ctx", None),
            P("section", None),
            P("section", "ctx", None, "tensor"),
            P("section", "ctx", None),
            P("section", "ctx", "tensor"),
            P("section", None, "tensor"),
            P("section", "tensor"),
            P("section", None, None),
            P("section", None),
            P("section", "tensor"),
            P("section", "tensor"),
            P("section", "tensor"),
            P("section", "tensor"),
            P("section", "tensor", "ctx"),
        ),
        check_vma=False,
    )
```

profile of v0, /device:TPU:9, one launch (start us, length us, event | category | flops | bytes accessed | tf_op | source)
XLA Modules:
  0.0 2738.0 jit_solution(2189601661663491571)
XLA Ops:
  9.4 10.7 all-gather.2
  28.8 28.1 %all-gather.1 = bf16[1,1536,256]{2,1,0:T(8,128)(2,1)S(1)} all-gather(bf16[1,384,256]{2,1,0:T(8,128)(2,1)S(1)} %copy-done.326), channel_id=3, replica_groups=mesh['section'=2,'ctx'=4,'tensor'=4] {'ctx'}, dimensions={1}, use_global_device_ids=true | all-gather | bytes 983040 | tf_op jit(solution)/shard_map/all_gather | solution.py:199
  58.9 51.4 %all-gather.37.cloned.1.call-done = bf16[1,1536,2,768]{3,2,0,1:T(2,128)(2,1)} async-done(((bf16[1,384,2,768]{3,2,0,1:T(2,128)(2,1)}), bf16[1,1536,2,768]{3,2,0,1:T(2,128)(2,1)}) %all-gather.37.cloned.1.call-update) | async-done | bytes 4718608 | tf_op jit(solution)/shard_map/all_gather | solution.py:198
  138.3 24.0 all-gather.39.cloned.1.call-done
  178.5 34.5 %all-gather.41.cloned.1.call-done = bf16[1,768,1536]{2,1,0:T(8,128)(2,1)} async-done(((bf16[1,768,384]{2,1,0:T(8,128)(2,1)}), bf16[1,768,1536]{2,1,0:T(8,128)(2,1)}) %all-gather.41.cloned.1.call-update) | async-done | bytes 2359312 | tf_op jit(solution)/shard_map/all_gather | solution.py:201
  216.8 61.1 %all-reduce.87.cloned.1.call-done = f32[256,1536]{1,0:T(8,128)} async-done(((f32[256,1536]{1,0:T(8,128)}), f32[256,1536]{1,0:T(8,128)}) %all-reduce.87.cloned.1.call-update) | async-done | bytes 1572880 | tf_op jit(solution)/shard_map/psum | solution.py:246
  336.1 18.5 all-gather.43.cloned.1.call-done
  381.6 61.3 %all-reduce.89.cloned.1.call-done = f32[256,1536]{1,0:T(8,128)} async-done(((f32[256,1536]{1,0:T(8,128)}), f32[256,1536]{1,0:T(8,128)}) %all-reduce.89.cloned.1.call-update) | async-done | bytes 1572880 | tf_op jit(solution)/shard_map/psum | solution.py:246
  499.3 19.2 all-gather.45.cloned.1.call-done
  545.5 61.3 %all-reduce.91.cloned.1.call-done = f32[256,1536]{1,0:T(8,128)} async-done(((f32[256,1536]{1,0:T(8,128)}), f32[256,1536]{1,0:T(8,128)}) %all-reduce.91.cloned.1.call-update) | async-done | bytes 1572880 | tf_op jit(solution)/shard_map/psum | solution.py:246
  663.2 18.0 all-gather.47.cloned.1.call-done
  717.6 51.9 %all-reduce.93.cloned.1.call-done = f32[256,1536]{1,0:T(8,128)} async-done(((f32[256,1536]{1,0:T(8,128)}), f32[256,1536]{1,0:T(8,128)}) %all-reduce.93.cloned.1.call-update) | async-done | bytes 1572880 | tf_op jit(solution)/shard_map/psum | solution.py:246
  952.7 19.2 all-gather.51.cloned.1.call-done
  1094.6 49.3 %all-reduce.97.cloned.1.call-done = bf16[256,1536]{1,0:T(8,128)(2,1)} async-done(((bf16[256,1536]{1,0:T(8,128)(2,1)}), bf16[256,1536]{1,0:T(8,128)(2,1)}) %all-reduce.97.cloned.1.call-update) | async-done | bytes 786448 | tf_op jit(solution)/shard_map/psum | solution.py:377
  1254.7 20.1 all-gather.53.cloned.1.call-done
  1277.5 9.5 while.111
  1412.7 35.4 %all-reduce.99.cloned.1.call-done = bf16[256,1536]{1,0:T(8,128)(2,1)} async-done(((bf16[256,1536]{1,0:T(8,128)(2,1)}), bf16[256,1536]{1,0:T(8,128)(2,1)}) %all-reduce.99.cloned.1.call-update) | async-done | bytes 786448 | tf_op jit(solution)/shard_map/psum | solution.py:377
  1511.6 13.3 all-gather.55.cloned.1.call-done
  1527.7 9.4 while.112
  1663.2 35.1 %all-reduce.101.cloned.1.call-done = bf16[256,1536]{1,0:T(8,128)(2,1)} async-done(((bf16[256,1536]{1,0:T(8,128)(2,1)}), bf16[256,1536]{1,0:T(8,128)(2,1)}) %all-reduce.101.cloned.1.call-update) | async-done | bytes 786448 | tf_op jit(solution)/shard_map/psum | solution.py:377
  1761.5 13.4 all-gather.57.cloned.1.call-done
  1777.7 9.4 while.113
  1913.6 35.2 %all-reduce.103.cloned.1.call-done = bf16[256,1536]{1,0:T(8,128)(2,1)} async-done(((bf16[256,1536]{1,0:T(8,128)(2,1)}), bf16[256,1536]{1,0:T(8,128)(2,1)}) %all-reduce.103.cloned.1.call-update) | async-done | bytes 786448 | tf_op jit(solution)/shard_map/psum | solution.py:377
  2006.6 18.7 all-gather.59.cloned.1.call-done
  2028.1 9.4 while.114
  2163.9 15.6 all-reduce.105.cloned.1.call-done
  2213.2 12.7 copy.559
  2231.6 12.3 all-reduce.95.cloned.1.call-done
  2268.0 111.0 %all-reduce.111.cloned.1.call-done = (f32[1,1536]{1,0:T(1,128)}, f32[4,3072]{1,0:T(4,128)}, f32[3072]{0:T(1024)}, f32[1,4,256]{2,1,0:T(4,128)}, f32[1,256]{1,0:T...) async-done(((f32[1,1536]{1,0:T(1,128)}, f32[4,3072]{1,0:T(4,128)}, f32[3072]{0:T(1024)}, f32[1,4,256]{2,1,0:T(4,128)}, f32[1,256]{1,0:T(1,128)}, ...) | async-done | bytes 85584 | tf_op jit(solution)/shard_map/psum | solution.py:434
  2386.6 116.7 %all-reduce.107.cloned.1.call-done = f32[1536,256]{1,0:T(8,128)} async-done(((f32[1536,256]{1,0:T(8,128)}), f32[1536,256]{1,0:T(8,128)}) %all-reduce.107.cloned.1.call-update) | async-done | bytes 1572880 | tf_op jit(solution)/shard_map/psum | solution.py:434
  2505.1 46.5 %reduce-scatter.9.cloned.1.call-done = bf16[384,768]{1,0:T(8,128)(2,1)} async-done(((bf16[1536,768]{1,0:T(8,128)(2,1)}), bf16[384,768]{1,0:T(8,128)(2,1)}) %reduce-scatter.9.cloned.1.call-update) | async-done | bytes 589840
  2554.0 171.7 %all-reduce.109.cloned.1.call-done = bf16[1536,2,768]{2,1,0:T(2,128)(2,1)} async-done(((bf16[1536,2,768]{2,1,0:T(2,128)(2,1)}), bf16[1536,2,768]{2,1,0:T(2,128)(2,1)}) %all-reduce.109.cloned.1.call-update) | async-done | bytes 4718608
  (2272 shorter events, 1586.6 us)
Async XLA Ops:
  7.2 103.0 %all-gather.37.cloned.1.call-start = ((), (), s32[]{:S(2)}) async-start(), calls=%async_computation.13 | async-start | bytes 5898240 | tf_op jit(solution)/shard_map/all_gather | solution.py:198
  7.9 154.4 %all-gather.39.cloned.1.call-start = ((), (), s32[]{:S(2)}) async-start(), calls=%async_computation.14 | async-start | bytes 1966080 | tf_op jit(solution)/shard_map/all_gather | solution.py:26
  125.0 88.0 %all-gather.41.cloned.1.call-start = ((), (), s32[]{:S(2)}) async-start(), calls=%async_computation.15 | async-start | bytes 2949120 | tf_op jit(solution)/shard_map/all_gather | solution.py:201
  125.7 152.2 %all-reduce.87.cloned.1.call-start = ((), (), s32[]{:S(2)}) async-start(), calls=%async_computation.2 | async-start | bytes 3145728 | tf_op jit(solution)/shard_map/psum | solution.py:246
  216.8 137.8 %all-gather.43.cloned.1.call-start = ((), (), s32[]{:S(2)}) async-start(), calls=%async_computation.16 | async-start | bytes 1966080 | tf_op jit(solution)/shard_map/all_gather | solution.py:26
  318.9 124.0 %all-reduce.89.cloned.1.call-start = ((), (), s32[]{:S(2)}) async-start(), calls=%async_computation.3 | async-start | bytes 3145728 | tf_op jit(solution)/shard_map/psum | solution.py:246
  381.5 137.0 %all-gather.45.cloned.1.call-start = ((), (), s32[]{:S(2)}) async-start(), calls=%async_computation.17 | async-start | bytes 1966080 | tf_op jit(solution)/shard_map/all_gather | solution.py:26
  482.2 124.6 %all-reduce.91.cloned.1.call-start = ((), (), s32[]{:S(2)}) async-start(), calls=%async_computation.4 | async-start | bytes 3145728 | tf_op jit(solution)/shard_map/psum | solution.py:246
  545.5 135.7 %all-gather.47.cloned.1.call-start = ((), (), s32[]{:S(2)}) async-start(), calls=%async_computation.18 | async-start | bytes 1966080 | tf_op jit(solution)/shard_map/all_gather | solution.py:26
  646.1 123.3 %all-reduce.93.cloned.1.call-start = ((), (), s32[]{:S(2)}) async-start(), calls=%async_computation.5 | async-start | bytes 3145728 | tf_op jit(solution)/shard_map/psum | solution.py:246
  708.1 165.9 %all-gather.49.cloned.1.call-start = ((), (), s32[]{:S(2)}) async-start(), calls=%async_computation.19 | async-start | bytes 1966080 | tf_op jit(solution)/shard_map/all_gather | solution.py:26
  794.0 27.2 collective-permute-start.8
  835.9 136.1 %all-gather.51.cloned.1.call-start = ((), (), s32[]{:S(2)}) async-start(), calls=%async_computation.20 | async-start | bytes 1966080 | tf_op jit(solution)/shard_map/all_gather | solution.py:26
  931.4 212.6 %all-reduce.97.cloned.1.call-start = ((), (), s32[]{:S(2)}) async-start(), calls=%async_computation.7 | async-start | bytes 1572864 | tf_op jit(solution)/shard_map/psum | solution.py:377
  1047.9 33.8 %collective-permute-start.9 = (f32[3,1024]{1,0:T(4,128)}, f32[3,1024]{1,0:T(4,128)}, u32[]{:S(2)}, u32[]{:S(2)}) collective-permute-start(f32[3,1024]{1,0:T(4,128)} %pad_add_fusion.9), channel_id=1, source_target_pairs={{4,0},{8,4},{12,8},{5,1},{9,5},{13,9},{6,2},{10,6},{14,10},{7,3},{... | collective-permute-start | bytes 36872 | tf_op jit(solution)/shard_map/ppermute | solution.py:21
  1094.4 180.4 %all-gather.53.cloned.1.call-start = ((), (), s32[]{:S(2)}) async-start(), calls=%async_computation.21 | async-start | bytes 1966080 | tf_op jit(solution)/shard_map/all_gather | solution.py:26
  1236.2 212.0 %all-reduce.99.cloned.1.call-start = ((), (), s32[]{:S(2)}) async-start(), calls=%async_computation.8 | async-start | bytes 1572864 | tf_op jit(solution)/shard_map/psum | solution.py:377
  1351.8 34.1 %collective-permute-start.11 = (f32[3,1024]{1,0:T(4,128)}, f32[3,1024]{1,0:T(4,128)}, u32[]{:S(2)}, u32[]{:S(2)}) collective-permute-start(f32[3,1024]{1,0:T(4,128)} %pad_add_fusion.8), channel_id=1, source_target_pairs={{4,0},{8,4},{12,8},{5,1},{9,5},{13,9},{6,2},{10,6},{14,10},{7,3},{... | collective-permute-start | bytes 36872 | tf_op jit(solution)/shard_map/ppermute | solution.py:21
  1398.6 126.4 %all-gather.55.cloned.1.call-start = ((), (), s32[]{:S(2)}) async-start(), calls=%async_computation.22 | async-start | bytes 1966080 | tf_op jit(solution)/shard_map/all_gather | solution.py:26
  1488.8 209.5 %all-reduce.101.cloned.1.call-start = ((), (), s32[]{:S(2)}) async-start(), calls=%async_computation.9 | async-start | bytes 1572864 | tf_op jit(solution)/shard_map/psum | solution.py:377
  1602.3 33.9 %collective-permute-start.13 = (f32[3,1024]{1,0:T(4,128)}, f32[3,1024]{1,0:T(4,128)}, u32[]{:S(2)}, u32[]{:S(2)}) collective-permute-start(f32[3,1024]{1,0:T(4,128)} %pad_add_fusion.7), channel_id=1, source_target_pairs={{4,0},{8,4},{12,8},{5,1},{9,5},{13,9},{6,2},{10,6},{14,10},{7,3},{... | collective-permute-start | bytes 36872 | tf_op jit(solution)/shard_map/ppermute | solution.py:21
  1648.8 126.1 %all-gather.57.cloned.1.call-start = ((), (), s32[]{:S(2)}) async-start(), calls=%async_computation.23 | async-start | bytes 1966080 | tf_op jit(solution)/shard_map/all_gather | solution.py:26
  1738.8 209.9 %all-reduce.103.cloned.1.call-start = ((), (), s32[]{:S(2)}) async-start(), calls=%async_computation.10 | async-start | bytes 1572864 | tf_op jit(solution)/shard_map/psum | solution.py:377
  1852.5 34.0 %collective-permute-start.15 = (f32[3,1024]{1,0:T(4,128)}, f32[3,1024]{1,0:T(4,128)}, u32[]{:S(2)}, u32[]{:S(2)}) collective-permute-start(f32[3,1024]{1,0:T(4,128)} %pad_add_fusion.6), channel_id=1, source_target_pairs={{4,0},{8,4},{12,8},{5,1},{9,5},{13,9},{6,2},{10,6},{14,10},{7,3},{... | collective-permute-start | bytes 36872 | tf_op jit(solution)/shard_map/ppermute | solution.py:21
  1899.2 126.2 %all-gather.59.cloned.1.call-start = ((), (), s32[]{:S(2)}) async-start(), calls=%async_computation.24 | async-start | bytes 1966080 | tf_op jit(solution)/shard_map/all_gather | solution.py:26
  1989.3 190.2 %all-reduce.105.cloned.1.call-start = ((), (), s32[]{:S(2)}) async-start(), calls=%async_computation.11 | async-start | bytes 1572864 | tf_op jit(solution)/shard_map/psum | solution.py:377
  2129.9 114.0 %all-reduce.95.cloned.1.call-start = ((), (), s32[]{:S(2)}) async-start(), calls=%async_computation.6 | async-start | bytes 3145728 | tf_op jit(solution)/shard_map/psum | solution.py:246
  2137.1 125.7 %reduce-scatter.7.cloned.1.call-start = ((), (), s32[]{:S(2)}) async-start(), calls=%async_computation.25 | async-start | bytes 491520
  2162.2 216.8 %all-reduce.111.cloned.1.call-start = ((), (), s32[]{:S(2)}) async-start(), calls=%async_computation.28 | async-start | bytes 173056 | tf_op jit(solution)/shard_map/psum | solution.py:434
  2182.5 320.8 %all-reduce.107.cloned.1.call-start = ((), (), s32[]{:S(2)}) async-start(), calls=%async_computation.12 | async-start | bytes 3145728 | tf_op jit(solution)/shard_map/psum | solution.py:434
  2186.8 364.7 %reduce-scatter.9.cloned.1.call-start = ((), (), s32[]{:S(2)}) async-start(), calls=%async_computation.26 | async-start | bytes 2949120
  2200.8 525.0 %all-reduce.109.cloned.1.call-start = ((), (), s32[]{:S(2)}) async-start(), calls=%async_computation.27 | async-start | bytes 9437184
  (630 other events, 5019.4 us)
Sparse Core Ops, SparseCore 0:
  9.6 100.5 all-gather.36
  125.1 37.2 all-gather.38
  163.9 49.0 all-gather.40
  216.9 60.9 all-reduce.86
  319.0 35.4 all-gather.42
  381.6 61.1 all-reduce.88
  482.3 36.1 all-gather.44
  545.6 61.1 all-reduce.90
  646.3 34.8 all-gather.46
  708.3 61.1 all-reduce.92
  836.0 35.6 all-gather.48
  931.5 40.4 all-gather.50
  1094.5 49.3 all-reduce.96
  1236.3 38.3 all-gather.52
  1398.7 49.4 all-reduce.98
  1488.9 36.0 all-gather.54
  1649.0 49.3 all-reduce.100
  1738.9 35.9 all-gather.56
  1899.3 49.4 all-reduce.102
  1989.4 35.9 all-gather.58
  2130.0 49.4 all-reduce.104
  2182.9 60.9 all-reduce.94
  2246.1 16.5 reduce-scatter.6
  2271.3 107.5 all-reduce.110
  2384.4 118.8 all-reduce.106
  2505.6 45.9 reduce-scatter.8
  2553.9 171.7 all-reduce.108
where the time goes:
time: 2770 us; the launch traced here: 2740 us
  waiting for transfers between devices  1120 us (40%)
  matrix products  457 us (16%)
  other arithmetic  452 us (16%)
  local copies, waits for them, and re-layouts  443 us (16%)
  blocking collectives  187 us (7%)
  starting transfers between devices  56.2 us (2%)
    psum x5, waiting for transfers between devices, body(): lax.psum(jnp.dot(gate_normed, out_full, preferred_element_type=jnp.float3...  248 us
    psum x2, waiting for transfers between devices, body(): lax.psum((acc_bc, acc_gain * first_tensor, acc_kernel[:, inner_local:], a...  228 us
    unnamed x30, waiting for transfers between devices  220 us
    psum x5, waiting for transfers between devices, body(): lax.psum(normed_grad.astype(jnp.bfloat16), 'tensor').astype(jnp.float32)  171 us
    all_gather x10, waiting for transfers between devices, prefix(): pieces = jax.tree.map(lambda part: lax.all_gather(part, axis), value)  165 us
    another operation x87, other arithmetic  122 us
    another operation x128, local copies, waits for them, and re-layouts  106 us
    dot_general x20, matrix products, block_step(): output = jnp.einsum('tsh,shp->thp', weights, x_block, precision=precise)  104 us
  transfers between devices with their start and end apart: 45, of which 28 were waited for; matrix products, arithmetic and copies ran while one was open for 20% of the time, Pallas kernels for 0%

commit v1 on v0

--- a/solution.py
+++ b/solution.py
@@ -3,16 +3,902 @@
 import jax
 import jax.numpy as jnp
 from jax import lax
+from jax.experimental import pallas as pl
+from jax.experimental.pallas import tpu as pltpu
 from jax.sharding import PartitionSpec as P
 
+bf16 = jnp.bfloat16
+f32 = jnp.float32
+precise = lax.Precision.HIGHEST
+epsilon = 1e-05
 N = 128
 KC = 4
 CH = 256
 DI = 3072
-
-
-epsilon = 1e-05
-precise = lax.Precision.HIGHEST
+HALO = 16
+LANES = 128
+VMEM_BYTES = 48 * 1024 * 1024
+
+M_FWD, M_BWD, M_ENTER, M_LEAVE, M_SEG = 0, 4, 8, 9, 10
+
+
+def mm(a, b):
+    return lax.dot_general(a, b, (((1,), (0,)), ((), ())), preferred_element_type=f32)
+
+
+def mm_nt(a, b, precision=None):
+    return lax.dot_general(a, b, (((1,), (1,)), ((), ())), preferred_element_type=f32, precision=precision)
+
+
+def mm_tn(a, b):
+    return lax.dot_general(a, b, (((0,), (0,)), ((), ())), preferred_element_type=f32)
+
+
+def split(v):
+    high = v.astype(bf16)
+    return high, (v - high.astype(f32)).astype(bf16)
+
+
+def rows_of(selector, values):
+    high, low = split(values)
+    return mm_nt(selector, high) + mm_nt(selector, low)
+
+
+def times_mask(rows, mask):
+    high, low = split(rows)
+    return mm(high, mask) + mm(low, mask)
+
+
+def left_parts(a):
+    high, low = split(a)
+    return jnp.concatenate([high, low, high], axis=1)
+
+
+def right_parts(b, axis):
+    high, low = split(b)
+    return jnp.concatenate([high, high, low], axis=axis)
+
+
+def precise_nt(a, b):
+    return mm_nt(left_parts(a), right_parts(b, 1))
+
+
+def precise_mm(a, b):
+    return mm(left_parts(a), right_parts(b, 0))
+
+
+def head_selector(head_size):
+    row = lax.broadcasted_iota(jnp.int32, (8, LANES), 0)
+    lane = lax.broadcasted_iota(jnp.int32, (8, LANES), 1)
+    return (row == lane // head_size).astype(bf16)
+
+
+def iota2(shape):
+    return lax.broadcasted_iota(jnp.int32, shape, 0), lax.broadcasted_iota(jnp.int32, shape, 1)
+
+
+def sigmoid(v):
+    return 1.0 / (1.0 + jnp.exp(-v))
+
+
+def softplus(v):
+    return jnp.maximum(v, 0.0) + jnp.log1p(jnp.exp(-jnp.abs(v)))
+
+
+def fill_padded(padded, halo_ref, pre_ref, rows):
+    padded[pl.ds(0, HALO), :] = halo_ref[...].astype(f32)
+    padded[pl.ds(HALO, rows), :] = pre_ref[...].astype(f32)
+
+
+def conv_tile(padded, taps_ref, marks, start, count):
+    total = jnp.zeros((count, LANES), f32) + taps_ref[KC : KC + 1, :]
+    for k in range(KC):
+        shifted = padded[pl.ds(start + HALO - KC + 1 + k, count), :]
+        if k == KC - 1:
+            total = total + taps_ref[k : k + 1, :] * shifted
+        else:
+            total = total + taps_ref[k : k + 1, :] * (shifted * marks[start : start + count, M_FWD + k : M_FWD + k + 1])
+    return total
+
+
+TILE = 128
+
+
+def scan_forward_kernel(
+    head_size, rows, pre_ref, halo_ref, taps_ref, marks_ref, seg_ref, step_ref, bias_ref, decay_ref,
+    conv_ref, y_ref, own_state_ref, last_state_ref, cum_ref, rate_ref, cum_rows_ref, step_rows_ref,
+    padded, b_all, b_turned, scores, cum_all, rate_all, step_all,
+):
+    i = pl.program_id(0)
+    chunks = rows // CH
+    fill_padded(padded, halo_ref, pre_ref, rows)
+    for start in range(0, rows, TILE):
+        value = conv_tile(padded, taps_ref, marks_ref, start, TILE)
+        conv_ref[pl.ds(start, TILE), :] = value / (1.0 + jnp.exp(-value))
+
+    @pl.when(i == 0)
+    def _():
+        b_all[...] = conv_ref[...]
+        b_turned[...] = conv_ref[...].T
+        shifted = step_ref[...] + bias_ref[...]
+        rate = softplus(shifted)
+        step_all[...] = shifted
+        rate_all[...] = rate
+        r, c = iota2((CH, CH))
+        tri = (r >= c).astype(f32)
+        for n in range(chunks):
+            part = rate[n * CH : (n + 1) * CH, :] * decay_ref[...]
+            cum_all[pl.ds(n * CH, CH), :] = lax.dot_general(
+                tri, part, (((1,), (0,)), ((), ())), preferred_element_type=f32, precision=precise
+            )
+
+    @pl.when(i == 1)
+    def _():
+        r, c = iota2((CH, CH))
+        for n in range(chunks):
+            here = pl.ds(n * CH, CH)
+            same = marks_ref[here, M_SEG : M_SEG + 1] == seg_ref[0:1, here]
+            value = precise_nt(conv_ref[here, :], b_all[here, :])
+            scores[n] = jnp.where((r >= c) & same, value, 0.0)
+
+    @pl.when(i >= 2)
+    def _():
+        j = i - 2
+        per = LANES // head_size
+        row, lane = iota2((LANES, LANES))
+        widen = (row == per * j + lane // head_size).astype(f32)
+        cum = lax.dot_general(cum_all[...], widen, (((1,), (0,)), ((), ())), preferred_element_type=f32, precision=precise)
+        rate = lax.dot_general(rate_all[...], widen, (((1,), (0,)), ((), ())), preferred_element_type=f32, precision=precise)
+        row8, lane8 = iota2((8, LANES))
+        pick = ((lane8 == per * j + row8) & (row8 < per)).astype(f32)
+        cum_rows = mm_nt(pick, cum_all[...], precise)
+        cum_rows_ref[0] = cum_rows
+        step_rows_ref[0] = mm_nt(pick, step_all[...], precise)
+        cum_ref[...] = cum
+        rate_ref[...] = rate
+        lane_c = lax.broadcasted_iota(jnp.int32, (CH, LANES), 1)
+        states = []
+        for n in range(chunks):
+            here = pl.ds(n * CH, CH)
+            span = slice(n * CH, (n + 1) * CH)
+            scaled = rate[span] * conv_ref[here, :]
+            scaled_parts = right_parts(scaled, 0)
+            out = jnp.zeros((CH, LANES), f32)
+            for h in range(per):
+                spread = cum[span, h * head_size : h * head_size + 1] - cum_rows[h : h + 1, span]
+                value = mm(left_parts(scores[n] * jnp.exp(jnp.minimum(spread, 0.0))), scaled_parts)
+                out = value if per == 1 else jnp.where(lane_c // head_size == h, value, out)
+            y_ref[here, :] = out
+            leave = jnp.exp(cum[(n + 1) * CH - 1 : (n + 1) * CH, :] - cum[span]) * marks_ref[here, M_LEAVE : M_LEAVE + 1]
+            state = precise_mm(b_turned[:, here], scaled * leave)
+            own_state_ref[n] = state
+            states.append(state)
+        total = states[0]
+        for n in range(1, chunks):
+            last = (n + 1) * CH - 1
+            kept = jnp.exp(cum[last : last + 1, :]) * marks_ref[last : last + 1, M_ENTER : M_ENTER + 1]
+            total = kept * total + states[n]
+        last_state_ref[...] = total
+
+
+def call(kernel, held, in_specs, **rest):
+    count = len(held)
+
+    def run(*refs):
+        kernel(*refs[count:])
+
+    made = pl.pallas_call(run, in_specs=[pl.BlockSpec(memory_space=pl.ANY)] * count + in_specs, **rest)
+    return lambda *args: made(*held, *args)
+
+
+def ordered(value, *others):
+    anywhere = pl.BlockSpec(memory_space=pl.ANY)
+    return pl.pallas_call(
+        lambda *refs: None,
+        in_specs=[anywhere] * (1 + len(others)),
+        out_specs=anywhere,
+        out_shape=jax.ShapeDtypeStruct(value.shape, value.dtype),
+        input_output_aliases={0: 0},
+        cost_estimate=cost(0),
+        name="ordered",
+    )(value, *others)
+
+
+def whole(shape):
+    return pl.BlockSpec(shape, lambda i: (0,) * len(shape))
+
+
+def params(limit=VMEM_BYTES):
+    return pltpu.CompilerParams(vmem_limit_bytes=limit, dimension_semantics=("arbitrary",))
+
+
+def cost(microseconds):
+    return pl.CostEstimate(flops=0, bytes_accessed=int(microseconds * 3e6), transcendentals=0)
+
+
+def scan_forward(pre, halo, taps, marks, seg_row, step, bias, decay, head_size, held=()):
+    rows, mixed = pre.shape
+    inner = mixed - 2 * N
+    pairs = inner // LANES
+    chunks = rows // CH
+    steps = pairs + 2
+    column = lambda i: (0, (i + pairs) % steps)
+    pair = lambda i: (0, jnp.maximum(i - 2, 0))
+    return call(
+        partial(scan_forward_kernel, head_size, rows),
+        held,
+        grid=(steps,),
+        in_specs=[
+            pl.BlockSpec((rows, LANES), column),
+            pl.BlockSpec((HALO, LANES), column),
+            pl.BlockSpec((8, LANES), column),
+            whole((rows, LANES)),
+            whole((8, rows)),
+            whole((rows, LANES)),
+            whole((1, LANES)),
+            whole((1, LANES)),
+        ],
+        out_specs=[
+            pl.BlockSpec((rows, LANES), column),
+            pl.BlockSpec((rows, LANES), pair),
+            pl.BlockSpec((chunks, N, LANES), lambda i: (0, 0, jnp.maximum(i - 2, 0))),
+            pl.BlockSpec((N, LANES), pair),
+            pl.BlockSpec((rows, LANES), pair),
+            pl.BlockSpec((rows, LANES), pair),
+            pl.BlockSpec((1, 8, rows), lambda i: (jnp.maximum(i - 2, 0), 0, 0)),
+            pl.BlockSpec((1, 8, rows), lambda i: (jnp.maximum(i - 2, 0), 0, 0)),
+        ],
+        out_shape=[
+            jax.ShapeDtypeStruct((rows, mixed), f32),
+            jax.ShapeDtypeStruct((rows, inner), f32),
+            jax.ShapeDtypeStruct((chunks, N, inner), f32),
+            jax.ShapeDtypeStruct((N, inner), f32),
+            jax.ShapeDtypeStruct((rows, inner), f32),
+            jax.ShapeDtypeStruct((rows, inner), f32),
+            jax.ShapeDtypeStruct((pairs, 8, rows), f32),
+            jax.ShapeDtypeStruct((pairs, 8, rows), f32),
+        ],
+        scratch_shapes=[
+            pltpu.VMEM((rows + HALO, LANES), f32),
+            pltpu.VMEM((rows, LANES), f32),
+            pltpu.VMEM((N, rows), f32),
+            pltpu.VMEM((chunks, CH, CH), f32),
+            pltpu.VMEM((rows, LANES), f32),
+            pltpu.VMEM((rows, LANES), f32),
+            pltpu.VMEM((rows, LANES), f32),
+        ],
+        compiler_params=params(),
+        cost_estimate=cost(15),
+        name="scan_forward",
+    )(pre, halo, taps, marks, seg_row, step, bias, decay)
+
+
+def gate_kernel(
+    chunks, with_grad, y_ref, conv_ref, c_ref, cum_ref, marks_ref, own_state_ref, state_ref, gate_ref, skip_ref, gain_ref,
+    *rest,
+):
+    if with_grad:
+        grad_ref, ssm_ref, gated_ref, entering_ref, sums_ref = rest
+    else:
+        ssm_ref, gated_ref, entering_ref, sums_ref = rest
+    i = pl.program_id(0)
+    state = state_ref[...]
+    for n in range(chunks):
+        here = pl.ds(n * CH, CH)
+        entering_ref[n] = state
+        enter = jnp.exp(cum_ref[here, :]) * marks_ref[here, M_ENTER : M_ENTER + 1]
+        ssm_ref[here, :] = (
+            y_ref[here, :]
+            + enter * precise_mm(c_ref[here, :], state)
+            + skip_ref[...] * conv_ref[here, :]
+        )
+        state = enter[CH - 1 : CH, :] * state + own_state_ref[n]
+    gate = gate_ref[...]
+    gated = ssm_ref[...] * (gate * sigmoid(gate))
+    scaled = gated * gain_ref[...]
+    gated_ref[...] = scaled
+    row = lax.broadcasted_iota(jnp.int32, (8, LANES), 0)
+    sums = rows_of((row == 0).astype(bf16), gated * gated)
+    if with_grad:
+        sums = sums + rows_of((row == 1).astype(bf16), scaled * grad_ref[...])
+
+    @pl.when(i == 0)
+    def _():
+        sums_ref[...] = sums
+
+    @pl.when(i > 0)
+    def _():
+        sums_ref[...] += sums
+
+
+def gate_forward(y, conv, cum, marks, own_state, state_in, gate, skip, gain, grad=None, held=()):
+    rows, inner = y.shape
+    pairs = inner // LANES
+    chunks = rows // CH
+    block = pl.BlockSpec((rows, LANES), lambda i: (0, i))
+    line = pl.BlockSpec((1, LANES), lambda i: (0, i))
+    states = pl.BlockSpec((chunks, N, LANES), lambda i: (0, 0, i))
+    last = conv.shape[1] // LANES - 1
+    in_specs = [
+        block, block, pl.BlockSpec((rows, LANES), lambda i: (0, last)), block, whole((rows, LANES)), states,
+        pl.BlockSpec((N, LANES), lambda i: (0, i)), block, line, line,
+    ]
+    args = [y, conv, conv, cum, marks, own_state, state_in, gate, skip, gain]
+    if grad is not None:
+        in_specs.append(block)
+        args.append(grad)
+    return call(
+        partial(gate_kernel, chunks, grad is not None),
+        held,
+        grid=(pairs,),
+        in_specs=in_specs,
+        out_specs=[block, block, states, whole((8, rows))],
+        out_shape=[
+            jax.ShapeDtypeStruct((rows, inner), f32),
+            jax.ShapeDtypeStruct((rows, inner), f32),
+            jax.ShapeDtypeStruct((chunks, N, inner), f32),
+            jax.ShapeDtypeStruct((8, rows), f32),
+        ],
+        compiler_params=params(),
+        cost_estimate=cost(6),
+        name="gate_forward",
+    )(*args)
+
+
+def gate_backward_kernel(
+    chunks, channels, grad_ref, gate_ref, ssm_ref, conv_ref, c_ref, cum_ref, marks_ref, sums_ref, gain_ref,
+    out_grad_ref, gate_grad_ref, pulled_ref, first_ref, gain_grad_ref, skip_grad_ref, dots_ref,
+    scale_all, shift_all, c_turned,
+):
+    i = pl.program_id(0)
+
+    @pl.when(i == 0)
+    def _():
+        scale = lax.rsqrt(sums_ref[0:1, :] / channels + epsilon)
+        shift = scale * scale * scale * sums_ref[1:2, :] / channels
+        rows = scale.shape[1]
+        scale_all[...] = jnp.broadcast_to(scale, (LANES, rows)).T
+        shift_all[...] = jnp.broadcast_to(shift, (LANES, rows)).T
+        c_turned[...] = c_ref[...].T
+
+    gate = gate_ref[...]
+    sig = sigmoid(gate)
+    act = gate * sig
+    ssm = ssm_ref[...]
+    gated = ssm * act
+    grad = grad_ref[...]
+    scale = scale_all[...]
+    gated_grad = scale * gain_ref[...] * grad - gated * shift_all[...]
+    gain_grad_ref[...] = jnp.sum(grad * gated * scale, axis=0, keepdims=True)
+    out_grad = gated_grad * act
+    out_grad_ref[...] = out_grad
+    skip_grad_ref[...] = jnp.sum(out_grad * conv_ref[...], axis=0, keepdims=True)
+    gate_grad = gated_grad * ssm * (sig * (1.0 + gate * (1.0 - sig)))
+    gate_grad_ref[...] = gate_grad.astype(bf16)
+    row = lax.broadcasted_iota(jnp.int32, (8, LANES), 0)
+    dots = rows_of((row == 0).astype(bf16), gate_grad * gate)
+    kept = []
+    for n in range(chunks):
+        here = pl.ds(n * CH, CH)
+        enter = jnp.exp(cum_ref[here, :]) * marks_ref[here, M_ENTER : M_ENTER + 1]
+        pulled = precise_mm(c_turned[:, here], out_grad_ref[here, :] * enter)
+        pulled_ref[n] = pulled
+        kept.append((enter[CH - 1 : CH, :], pulled))
+    first = kept[-1][1]
+    for last_enter, pulled in kept[-2::-1]:
+        first = last_enter * first + pulled
+    first_ref[...] = first
+
+    @pl.when(i == 0)
+    def _():
+        dots_ref[...] = dots
+
+    @pl.when(i > 0)
+    def _():
+        dots_ref[...] += dots
+
+
+def gate_backward(grad, gate, ssm, conv, cum, marks, sums, gain, channels, held=()):
+    rows, inner = ssm.shape
+    pairs = inner // LANES
+    chunks = rows // CH
+    block = pl.BlockSpec((rows, LANES), lambda i: (0, i))
+    line = pl.BlockSpec((1, LANES), lambda i: (0, i))
+    states = pl.BlockSpec((chunks, N, LANES), lambda i: (0, 0, i))
+    last = conv.shape[1] // LANES - 1
+    return call(
+        partial(gate_backward_kernel, chunks, float(channels)),
+        held,
+        grid=(pairs,),
+        in_specs=[
+            block, block, block, block, pl.BlockSpec((rows, LANES), lambda i: (0, last)), block,
+            whole((rows, LANES)), whole((8, rows)), line,
+        ],
+        out_specs=[block, block, states, pl.BlockSpec((N, LANES), lambda i: (0, i)), line, line, whole((8, rows))],
+        out_shape=[
+            jax.ShapeDtypeStruct((rows, inner), f32),
+            jax.ShapeDtypeStruct((rows, inner), bf16),
+            jax.ShapeDtypeStruct((chunks, N, inner), f32),
+            jax.ShapeDtypeStruct((N, inner), f32),
+            jax.ShapeDtypeStruct((1, inner), f32),
+            jax.ShapeDtypeStruct((1, inner), f32),
+            jax.ShapeDtypeStruct((8, rows), f32),
+        ],
+        scratch_shapes=[pltpu.VMEM((rows, LANES), f32), pltpu.VMEM((rows, LANES), f32), pltpu.VMEM((N, rows), f32)],
+        compiler_params=params(),
+        cost_estimate=cost(7),
+        name="gate_backward",
+    )(grad, gate, ssm, conv, conv, cum, marks, sums, gain)
+
+
+def intra_backward_kernel(
+    head_size, chunks, out_grad_ref, conv_ref, b_ref, c_ref, cum_ref, rate_ref, cum_rows_ref, marks_ref, seg_ref,
+    scaled_grad_ref, rate_rows_ref, b_grad_ref, c_grad_ref,
+    scores, scores_grad,
+):
+    i = pl.program_id(0)
+    per = LANES // head_size
+    r, c = iota2((CH, CH))
+
+    @pl.when(i == 0)
+    def _():
+        for n in range(chunks):
+            here = pl.ds(n * CH, CH)
+            same = marks_ref[here, M_SEG : M_SEG + 1] == seg_ref[0:1, here]
+            value = precise_nt(b_ref[here, :], c_ref[here, :])
+            scores[n] = jnp.where((r <= c) & same, value, 0.0)
+            scores_grad[n] = jnp.zeros((CH, CH), f32)
+
+    from_row = (r >= c).astype(bf16)
+    lane_c = lax.broadcasted_iota(jnp.int32, (CH, LANES), 1)
+    rate_rows_ref[...] = jnp.zeros(rate_rows_ref.shape, f32)
+    for n in range(chunks):
+        here = pl.ds(n * CH, CH)
+        scaled = rate_ref[here, :] * conv_ref[here, :]
+        grad_parts = right_parts(out_grad_ref[here, :], 1)
+        grad_low = grad_parts[:, :LANES]
+        out = jnp.zeros((CH, LANES), f32)
+        for h in range(per):
+            mine = lane_c // head_size == h
+            spread = cum_rows_ref[0, h : h + 1, here] - cum_ref[here, h * head_size : h * head_size + 1]
+            decay = jnp.exp(jnp.minimum(spread, 0.0))
+            weights = scores[n] * decay
+            value = mm(weights.astype(bf16), grad_low)
+            out = jnp.where(mine, value, out)
+            weights_grad = mm_nt(left_parts(jnp.where(mine, scaled, 0.0)), grad_parts)
+            scores_grad[n] += decay * weights_grad
+            flow = mm((weights * weights_grad).astype(bf16), from_row)
+            rate_rows_ref[0, h : h + 1, here] = jnp.sum(jnp.where(r < c, flow, 0.0), axis=0, keepdims=True)
+        scaled_grad_ref[here, :] = out
+
+    @pl.when(i == pl.num_programs(0) - 1)
+    def _():
+        for n in range(chunks):
+            here = pl.ds(n * CH, CH)
+            same = marks_ref[here, M_SEG : M_SEG + 1] == seg_ref[0:1, here]
+            total = jnp.where((r <= c) & same, scores_grad[n], 0.0)
+            b_grad_ref[here, :] = precise_mm(total, c_ref[here, :])
+            c_grad_ref[here, :] = precise_mm(total.T, b_ref[here, :])
+
+
+def intra_backward(out_grad, conv, cum, rate, cum_rows, marks, seg_row, head_size, held=()):
+    rows, inner = out_grad.shape
+    pairs = inner // LANES
+    chunks = rows // CH
+    block = pl.BlockSpec((rows, LANES), lambda i: (0, i))
+    heads = pl.BlockSpec((1, 8, rows), lambda i: (i, 0, 0))
+    return call(
+        partial(intra_backward_kernel, head_size, chunks),
+        held,
+        grid=(pairs,),
+        in_specs=[
+            block, block, pl.BlockSpec((rows, LANES), lambda i: (0, pairs)),
+            pl.BlockSpec((rows, LANES), lambda i: (0, pairs + 1)), block, block, heads,
+            whole((rows, LANES)), whole((8, rows)),
+        ],
+        out_specs=[block, heads, whole((rows, N)), whole((rows, N))],
+        out_shape=[
+            jax.ShapeDtypeStruct((rows, inner), f32),
+            jax.ShapeDtypeStruct((pairs, 8, rows), f32),
+            jax.ShapeDtypeStruct((rows, N), f32),
+            jax.ShapeDtypeStruct((rows, N), f32),
+        ],
+        scratch_shapes=[pltpu.VMEM((chunks, CH, CH), f32), pltpu.VMEM((chunks, CH, CH), f32)],
+        compiler_params=params(),
+        cost_estimate=cost(8),
+        name="intra_backward",
+    )(out_grad, conv, conv, conv, cum, rate, cum_rows, marks, seg_row)
+
+
+def scan_backward_kernel(
+    head_size, rows, pairs, out_grad_ref, scaled_grad_ref, conv_ref, b_ref, c_ref, cum_ref, rate_ref, rate_rows_ref, step_rows_ref,
+    entering_ref, pulled_ref, after_ref, skip_ref, decay_ref, b_intra_ref, c_intra_ref, pre_ref, halo_ref, taps_ref, marks_ref,
+    conv_grad_ref, taps_grad_ref, step_grad_ref, log_grad_ref, bias_grad_ref,
+    padded, b_total, c_total, current,
+):
+    i = pl.program_id(0)
+    chunks = rows // CH
+    fill_padded(padded, halo_ref, pre_ref, rows)
+
+    @pl.when(i == 0)
+    def _():
+        b_total[...] = b_intra_ref[...]
+        c_total[...] = c_intra_ref[...]
+
+    @pl.when(i < pairs)
+    def _():
+        selector = head_selector(head_size)
+        r, c = iota2((CH, CH))
+        from_row = (r >= c).astype(bf16)
+        before = (r < c).astype(bf16)
+        after = after_ref[...]
+        log_total = jnp.zeros((8, 1), f32)
+        bias_total = jnp.zeros((8, 1), f32)
+        decay = decay_ref[0, :, 0:1]
+        for n in reversed(range(chunks)):
+            here = pl.ds(n * CH, CH)
+            last = (n + 1) * CH - 1
+            mark_enter = marks_ref[here, M_ENTER : M_ENTER + 1]
+            mark_leave = marks_ref[here, M_LEAVE : M_LEAVE + 1]
+            cum = cum_ref[here, :]
+            enter = jnp.exp(cum) * mark_enter
+            leave = jnp.exp(cum_ref[last : last + 1, :] - cum) * mark_leave
+            conv = conv_ref[here, :]
+            rate = rate_ref[here, :]
+            scaled = rate * conv
+            out_grad = out_grad_ref[here, :]
+            state = entering_ref[n]
+            state_low = state.astype(bf16)
+            after_low = after.astype(bf16)
+            left = leave * mm(b_ref[here, :].astype(bf16), after_low)
+            scaled_grad = scaled_grad_ref[here, :] + left
+            b_total[here, :] += precise_nt(scaled * leave, after)
+            entered = out_grad * enter
+            c_total[here, :] += precise_nt(entered, state)
+            came = rows_of(selector, entered * mm(c_ref[here, :].astype(bf16), state_low))
+            gone = rows_of(selector, scaled * left)
+            kept = enter[CH - 1 : CH, :]
+            through = jnp.sum(rows_of(selector, kept * (state * after)), axis=1, keepdims=True)
+            log_rate_grad = rate_rows_ref[0, :, here] + times_mask(came, from_row) + times_mask(gone, before) + through
+            direct = rows_of(selector, conv * scaled_grad)
+            shifted = step_rows_ref[0, :, here]
+            step_grad = (direct + log_rate_grad * decay) * sigmoid(shifted)
+            step_grad_ref[0, :, here] = step_grad
+            log_total = log_total + jnp.sum(log_rate_grad * softplus(shifted), axis=1, keepdims=True) * decay
+            bias_total = bias_total + jnp.sum(step_grad, axis=1, keepdims=True)
+            current[here, :] = rate * scaled_grad + skip_ref[...] * out_grad
+            after = kept * after + pulled_ref[n]
+        log_grad_ref[0] = jnp.broadcast_to(log_total, (8, LANES))
+        bias_grad_ref[0] = jnp.broadcast_to(bias_total, (8, LANES))
+
+    @pl.when(i == pairs)
+    def _():
+        current[...] = b_total[...]
+
+    @pl.when(i == pairs + 1)
+    def _():
+        current[...] = c_total[...]
+
+    sums = [jnp.zeros((1, LANES), f32) for _ in range(KC + 1)]
+    for start in range(0, rows, TILE):
+        value = conv_tile(padded, taps_ref, marks_ref, start, TILE)
+        sig = sigmoid(value)
+        grad = current[pl.ds(start, TILE), :] * (sig * (1.0 + value * (1.0 - sig)))
+        conv_grad_ref[pl.ds(start, TILE), :] = grad
+        for k in range(KC):
+            shifted = padded[pl.ds(start + HALO - KC + 1 + k, TILE), :]
+            if k < KC - 1:
+                shifted = shifted * marks_ref[start : start + TILE, M_FWD + k : M_FWD + k + 1]
+            sums[k] = sums[k] + jnp.sum(grad * shifted, axis=0, keepdims=True)
+        sums[KC] = sums[KC] + jnp.sum(grad, axis=0, keepdims=True)
+    taps_grad_ref[...] = jnp.concatenate(sums + [jnp.zeros((8 - KC - 1, LANES), f32)], axis=0)
+
+
+def scan_backward(
+    out_grad, scaled_grad, conv, cum, rate, rate_rows, step_rows, entering, pulled, after, skip, decay_rows,
+    b_intra, c_intra, pre, halo, taps, marks, head_size, held=(),
+):
+    rows, inner = out_grad.shape
+    mixed = pre.shape[1]
+    pairs = inner // LANES
+    chunks = rows // CH
+    steps = pairs + 2
+    own = lambda i: jnp.minimum(i, pairs - 1)
+    block = pl.BlockSpec((rows, LANES), lambda i: (0, own(i)))
+    column = lambda i: (0, i)
+    heads = pl.BlockSpec((1, 8, rows), lambda i: (own(i), 0, 0))
+    few = pl.BlockSpec((1, 8, LANES), lambda i: (own(i), 0, 0))
+    states = pl.BlockSpec((chunks, N, LANES), lambda i: (0, 0, own(i)))
+    return call(
+        partial(scan_backward_kernel, head_size, rows, pairs),
+        held,
+        grid=(steps,),
+        in_specs=[
+            block, block, block, pl.BlockSpec((rows, LANES), lambda i: (0, pairs)),
+            pl.BlockSpec((rows, LANES), lambda i: (0, pairs + 1)), block, block, heads, heads, states, states,
+            pl.BlockSpec((N, LANES), lambda i: (0, own(i))), pl.BlockSpec((1, LANES), lambda i: (0, own(i))), few,
+            whole((rows, N)), whole((rows, N)), pl.BlockSpec((rows, LANES), column), pl.BlockSpec((HALO, LANES), column),
+            pl.BlockSpec((8, LANES), column), whole((rows, LANES)),
+        ],
+        out_specs=[pl.BlockSpec((rows, LANES), column), pl.BlockSpec((8, LANES), column), heads, few, few],
+        out_shape=[
+            jax.ShapeDtypeStruct((rows, mixed), f32),
+            jax.ShapeDtypeStruct((8, mixed), f32),
+            jax.ShapeDtypeStruct((pairs, 8, rows), f32),
+            jax.ShapeDtypeStruct((pairs, 8, LANES), f32),
+            jax.ShapeDtypeStruct((pairs, 8, LANES), f32),
+        ],
+        scratch_shapes=[
+            pltpu.VMEM((rows + HALO, LANES), f32),
+            pltpu.VMEM((rows, N), f32),
+            pltpu.VMEM((rows, N), f32),
+            pltpu.VMEM((rows, LANES), f32),
+        ],
+        compiler_params=params(),
+        cost_estimate=cost(16),
+        name="scan_backward",
+    )(
+        out_grad, scaled_grad, conv, conv, conv, cum, rate, rate_rows, step_rows, entering, pulled, after, skip, decay_rows,
+        b_intra, c_intra, pre, halo, taps, marks,
+    )
+
+
+def conv_backward_kernel(
+    rows, pairs, per, conv_grad_ref, next_ref, taps_ref, marks_ref, pre_ref, gate_dots_ref, step_grad_ref, step_rows_ref,
+    bias_ref, out_ref, map_grad_ref, dots_ref, padded,
+):
+    i = pl.program_id(0)
+    row = lax.broadcasted_iota(jnp.int32, (8, LANES), 0)
+
+    @pl.when(i == 0)
+    def _():
+        dots_ref[...] = gate_dots_ref[...]
+
+    @pl.when(i > 0)
+    def _():
+        padded[pl.ds(0, rows), :] = conv_grad_ref[...]
+        padded[pl.ds(rows, 8), :] = next_ref[...]
+        selector = (row == 0).astype(bf16)
+        for start in range(0, rows, TILE):
+            total = taps_ref[KC - 1 : KC, :] * padded[pl.ds(start, TILE), :]
+            for k in range(KC - 1):
+                shifted = padded[pl.ds(start + KC - 1 - k, TILE), :]
+                total = total + taps_ref[k : k + 1, :] * (
+                    shifted * marks_ref[start : start + TILE, M_BWD + k : M_BWD + k + 1]
+                )
+            out_ref[pl.ds(start, TILE), :] = total.astype(bf16)
+            map_grad_ref[pl.ds(start, TILE), :] = total
+            dots_ref[:, pl.ds(start, TILE)] += rows_of(selector, total * pre_ref[pl.ds(start, TILE), :].astype(f32))
+
+    @pl.when(i == 0)
+    def _():
+        grads = [step_grad_ref[j, 0:per, :] for j in range(pairs)]
+        grads = jnp.concatenate(grads + [jnp.zeros((LANES - per * pairs, rows), f32)], axis=0)
+        out_ref[...] = grads.T.astype(bf16)
+        total = jnp.zeros((1, rows), f32)
+        for j in range(pairs):
+            total = total + jnp.sum(
+                step_grad_ref[j, 0:per, :] * (step_rows_ref[j, 0:per, :] - bias_ref[j, 0:per, 0:1]), axis=0, keepdims=True
+            )
+        dots_ref[0:1, :] += total
+
+
+def conv_backward(conv_grad, next_grad, taps, marks, pre, gate_dots, step_grad, step_rows, bias_rows, head_size, held=()):
+    rows, mixed = pre.shape
+    pairs = (mixed - 2 * N) // LANES
+    steps = pairs + 3
+    column = lambda i: (0, jnp.clip(i - 1, 0, pairs + 1))
+    return call(
+        partial(conv_backward_kernel, rows, pairs, LANES // head_size),
+        held,
+        grid=(steps,),
+        in_specs=[
+            pl.BlockSpec((rows, LANES), column), pl.BlockSpec((8, LANES), column), pl.BlockSpec((8, LANES), column),
+            whole((rows, LANES)), pl.BlockSpec((rows, LANES), column),
+            whole((8, rows)),
+            whole((pairs, 8, rows)), whole((pairs, 8, rows)), whole((pairs, 8, LANES)),
+        ],
+        out_specs=[
+            pl.BlockSpec((rows, LANES), lambda i: (0, i)),
+            pl.BlockSpec((rows, LANES), lambda i: (0, jnp.clip(i - pairs - 1, 0, 1))),
+            whole((8, rows)),
+        ],
+        out_shape=[
+            jax.ShapeDtypeStruct((rows, steps * LANES), bf16),
+            jax.ShapeDtypeStruct((rows, 2 * N), f32),
+            jax.ShapeDtypeStruct((8, rows), f32),
+        ],
+        scratch_shapes=[pltpu.VMEM((rows + 8, LANES), f32)],
+        compiler_params=params(),
+        cost_estimate=cost(6),
+        name="conv_backward",
+    )(conv_grad, next_grad, taps, marks, pre, gate_dots, step_grad, step_rows, bias_rows)
+
+
+def join_kernel(count, width, index_ref, *refs):
+    blocks, out_ref = refs[:count], refs[count]
+    for n in range(count):
+        start = pl.multiple_of((index_ref[0] ^ n) * width, LANES)
+        out_ref[:, pl.ds(start, width)] = blocks[n][...].astype(out_ref.dtype)
+
+
+def join(blocks, index, dtype, first_row, held=()):
+    count = len(blocks)
+    rows, width = blocks[0].shape
+    rows -= first_row
+    size = min(rows, 256)
+    return call(
+        partial(join_kernel, count, width),
+        held,
+        grid=(rows // size,),
+        in_specs=[pl.BlockSpec(memory_space=pltpu.SMEM)]
+        + [pl.BlockSpec((size, width), lambda i: (i + first_row // size, 0))] * count,
+        out_specs=pl.BlockSpec((size, count * width), lambda i: (i, 0)),
+        out_shape=jax.ShapeDtypeStruct((rows, count * width), dtype),
+        compiler_params=params(),
+        cost_estimate=cost(2),
+        name="join",
+    )(index, *blocks)
+
+
+def join_norm_kernel(count, width, index_ref, gain_ref, *refs):
+    blocks, normed_ref, scale_ref = refs[:count], refs[count], refs[count + 1]
+    total = jnp.zeros((blocks[0].shape[0], 1), f32)
+    for n in range(count):
+        value = blocks[n][...].astype(f32)
+        total = total + jnp.sum(value * value, axis=1, keepdims=True)
+    scale = lax.rsqrt(total / (count * width) + epsilon)
+    scale_ref[...] = jnp.broadcast_to(scale, scale_ref.shape)
+    for n in range(count):
+        here = pl.ds(pl.multiple_of((index_ref[0] ^ n) * width, LANES), width)
+        normed_ref[:, here] = (blocks[n][...].astype(f32) * scale * gain_ref[:, here]).astype(bf16)
+
+
+def join_norm(blocks, index, gain, rows, held=()):
+    count = len(blocks)
+    width = blocks[0].shape[1]
+    size = 128
+    block = pl.BlockSpec((size, width), lambda i: (i, 0))
+    return call(
+        partial(join_norm_kernel, count, width),
+        held,
+        grid=(rows // size,),
+        in_specs=[pl.BlockSpec(memory_space=pltpu.SMEM), whole((1, count * width))] + [block] * count,
+        out_specs=[
+            pl.BlockSpec((size, count * width), lambda i: (i, 0)),
+            pl.BlockSpec((size, LANES), lambda i: (i, 0)),
+        ],
+        out_shape=[
+            jax.ShapeDtypeStruct((rows, count * width), bf16),
+            jax.ShapeDtypeStruct((rows, LANES), f32),
+        ],
+        compiler_params=params(),
+        cost_estimate=cost(3),
+        name="join_norm",
+    )(index, gain, *blocks)
+
+
+def input_side_kernel(count, width, own_ref, dots_ref, block_ref, grad_ref, scale_ref, gain_ref, *refs):
+    sent, out_ref, norm_ref = refs[: count - 1], refs[count - 1], refs[count]
+    normed_grad = own_ref[...]
+    for piece in sent:
+        normed_grad = normed_grad + piece[...].astype(f32)
+    scale = scale_ref[:, 0:1]
+    rows = scale.shape[0]
+    mean = jnp.broadcast_to(dots_ref[0:1, :] / width, (LANES, rows)).T[:, 0:1]
+    normed_x = block_ref[...].astype(f32) * scale
+    grad = grad_ref[...].astype(f32) + scale * (gain_ref[...] * normed_grad - normed_x * mean)
+    out_ref[...] = grad.astype(bf16)
+    norm = jnp.sum(normed_grad * normed_x, axis=0, keepdims=True)
+
+    @pl.when(pl.program_id(0) == 0)
+    def _():
+        norm_ref[...] = norm
+
+    @pl.when(pl.program_id(0) > 0)
+    def _():
+        norm_ref[...] += norm
+
+
+def input_gradient(own, sent, dots, block, grad, scale, gain, width, held=()):
+    rows, cols = own.shape
+    size = 128
+    part = pl.BlockSpec((size, cols), lambda i: (i, 0))
+    return call(
+        partial(input_side_kernel, len(sent) + 1, float(width)),
+        held,
+        grid=(rows // size,),
+        in_specs=[
+            part, pl.BlockSpec((8, size), lambda i: (0, i)), part, part, pl.BlockSpec((size, LANES), lambda i: (i, 0)),
+            whole((1, cols)),
+        ]
+        + [part] * len(sent),
+        out_specs=[part, whole((1, cols))],
+        out_shape=[jax.ShapeDtypeStruct((rows, cols), bf16), jax.ShapeDtypeStruct((1, cols), f32)],
+        compiler_params=params(),
+        cost_estimate=cost(3),
+        name="input_gradient",
+    )(own, dots, block, grad, scale, gain, *sent)
+
+
+def join_micro_kernel(count, width, held, places_ref, *refs):
+    out_ref, refs = refs[-1], refs[held:]
+    for n in range(count):
+        start = pl.multiple_of((places_ref[0] ^ n) * width, LANES)
+        out_ref[:, pl.ds(start, width)] = refs[n][...].astype(out_ref.dtype)
+
+
+def join_micro(places, blocks, dtype, held=()):
+    count = len(blocks)
+    rows, width = blocks[0].shape
+    size = rows // 4
+    return pl.pallas_call(
+        partial(join_micro_kernel, count, width, len(held)),
+        grid_spec=pltpu.PrefetchScalarGridSpec(
+            num_scalar_prefetch=1,
+            grid=(4,),
+            in_specs=[pl.BlockSpec(memory_space=pl.ANY)] * len(held)
+            + [pl.BlockSpec((size, width), lambda i, places: (i, 0))] * count,
+            out_specs=pl.BlockSpec((size, count * width), lambda i, places: (places[1] ^ i, 0)),
+        ),
+        out_shape=jax.ShapeDtypeStruct((rows, count * width), dtype),
+        compiler_params=params(),
+        cost_estimate=cost(5),
+        name="join_micro",
+    )(places, *held, *blocks)
+
+
+def join_gathered_kernel(count, width, held, places_ref, *refs):
+    out_ref, blocks_ref = refs[-1], refs[held]
+    for n in range(count):
+        out_ref[:, n * width : (n + 1) * width] = blocks_ref[n].astype(out_ref.dtype)
+
+
+def join_gathered(places, blocks, dtype, held=()):
+    count, rows, width = blocks.shape
+    size = rows // 4
+    return pl.pallas_call(
+        partial(join_gathered_kernel, count, width, len(held)),
+        grid_spec=pltpu.PrefetchScalarGridSpec(
+            num_scalar_prefetch=1,
+            grid=(4,),
+            in_specs=[pl.BlockSpec(memory_space=pl.ANY)] * len(held)
+            + [pl.BlockSpec((count, size, width), lambda i, places: (0, i, 0))],
+            out_specs=pl.BlockSpec((size, count * width), lambda i, places: (places[1] ^ i, 0)),
+        ),
+        out_shape=jax.ShapeDtypeStruct((rows, count * width), dtype),
+        compiler_params=params(),
+        cost_estimate=cost(5),
+        name="join_gathered",
+    )(places, *held, blocks)
+
+
+def place_maps_kernel(count, places_ref, term_ref, normed_ref, *refs):
+    pieces, out_ref = refs[:count], refs[count]
+    rows = pieces[0].shape[0]
+    total = jnp.zeros(out_ref.shape, f32)
+    for n in range(count):
+        here = pl.ds(pl.multiple_of((places_ref[0] ^ n) * rows, 16), rows)
+        total = total + mm_tn(normed_ref[here, :], pieces[n][...])
+    out_ref[...] = total.astype(bf16)
+
+
+def place_maps(index, term, normed, pieces, first_column):
+    count = len(pieces)
+    rows, width = pieces[0].shape
+    depth = normed.shape[1]
+    return pl.pallas_call(
+        partial(place_maps_kernel, count),
+        grid=(width // LANES,),
+        in_specs=[pl.BlockSpec(memory_space=pltpu.SMEM), pl.BlockSpec(memory_space=pl.ANY), whole(normed.shape)]
+        + [pl.BlockSpec((rows, LANES), lambda i: (0, i))] * count,
+        out_specs=pl.BlockSpec((depth, LANES), lambda i: (0, i + first_column // LANES)),
+        out_shape=jax.ShapeDtypeStruct(term.shape, term.dtype),
+        input_output_aliases={1: 0},
+        compiler_params=params(),
+        cost_estimate=cost(3),
+        name="place_maps",
+    )(index, term, normed, *pieces)
 
 
 def from_behind(block, axis, distance):
@@ -467,44 +1353,438 @@
     )
 
 
+def swap_section(value):
+    return lax.ppermute(value, "section", [(0, 1), (1, 0)])
+
+
+def from_partner(value, distance):
+    count = lax.axis_size("tensor")
+    return lax.ppermute(value, "tensor", [(i, i ^ distance) for i in range(count)])
+
+
+def with_partners(value):
+    return [value] + [from_partner(value, k) for k in range(1, lax.axis_size("tensor"))]
+
+
+def sum_over_tensor(value):
+    return sum(with_partners(value)[1:], value)
+
+
+def column_block(value, index, width):
+    return lax.dynamic_slice_in_dim(value, index * width, width, value.ndim - 1)
+
+
+def zero_of(value):
+    return jnp.minimum(jnp.abs(value[(0,) * value.ndim].astype(f32)).astype(jnp.int32), 0)
+
+
+def to_micro(value):
+    section, ctx, tensor = (lax.axis_index(a) for a in ("section", "ctx", "tensor"))
+    count = lax.axis_size("ctx")
+    width = value.shape[2] // lax.axis_size("tensor")
+    came = []
+    for e in range(2):
+        sent = 2 * section + ((ctx & 1) ^ e)
+        piece = lax.dynamic_slice(value, (sent, 0, tensor * width), (1, value.shape[1], width))[0]
+        route = [(s * count + c, (c >> 1) * count + 2 * s + ((c & 1) ^ e)) for s in range(2) for c in range(count)]
+        came.append(lax.ppermute(piece, ("section", "ctx"), route))
+    even = (ctx & 1) == 0
+    return jnp.concatenate([jnp.where(even, came[0], came[1]), jnp.where(even, came[1], came[0])], axis=0)
+
+
+def to_owners(blocks):
+    section, ctx, count = lax.axis_index("section"), lax.axis_index("ctx"), lax.axis_size("ctx")
+    rows = blocks[0].shape[0] // 2
+    pieces = []
+    for e in range(count):
+        half, layer = (ctx ^ e) & 1, (ctx ^ e) >> 1
+        piece = lax.dynamic_slice_in_dim(jnp.where(layer == 0, blocks[0], blocks[1]), half * rows, rows, 0)
+        route = [
+            (s * count + z, ((z ^ e) >> 1) * count + 2 * s + ((z ^ e) & 1)) for s in range(2) for z in range(count)
+        ]
+        pieces.append(lax.ppermute(piece, ("section", "ctx"), route))
+    ordered = []
+    for n in range(count):
+        wanted = ctx ^ n
+        e = ((wanted ^ ctx) & 1) | ((((wanted >> 1) ^ section) & 1) << 1)
+        chosen = pieces[count - 1]
+        for k in range(count - 1):
+            chosen = jnp.where(e == k, pieces[k], chosen)
+        ordered.append(chosen)
+    return jnp.concatenate(ordered, axis=0)
+
+
+def in_halves(own, section):
+    half = own.shape[0] // 2
+    keep = lax.dynamic_slice_in_dim(own, section * half, half, 0)
+    came = swap_section(lax.dynamic_slice_in_dim(own, (1 - section) * half, half, 0))
+    return [jnp.where(section == layer, keep, came) for layer in range(2)]
+
+
+def own_layer(halves, section):
+    keep = jnp.where(section == 0, halves[0], halves[1])
+    came = swap_section(jnp.where(section == 0, halves[1], halves[0]))
+    return jnp.concatenate([jnp.where(section == 0, keep, came), jnp.where(section == 0, came, keep)], axis=0)
+
+
+def token_marks(seg_around, rows):
+    own = seg_around[HALO : HALO + rows]
+    columns = [seg_around[HALO - KC + 1 + k : HALO - KC + 1 + k + rows] == own for k in range(KC)]
+    columns += [seg_around[HALO + KC - 1 - k : HALO + KC - 1 - k + rows] == own for k in range(KC)]
+    chunks = rows // CH
+    before = seg_around[HALO - 1 : HALO - 1 + rows].reshape(chunks, CH)[:, :1]
+    last = own.reshape(chunks, CH)[:, -1:]
+    columns.append((own.reshape(chunks, CH) == before).reshape(rows))
+    columns.append((own.reshape(chunks, CH) == last).reshape(rows))
+    columns = [column.astype(f32) for column in columns] + [own.astype(f32)]
+    marks = jnp.pad(jnp.stack(columns, axis=1), ((0, 0), (0, LANES - len(columns))))
+    return marks, jnp.broadcast_to(own.astype(f32)[None, :], (8, rows))
+
+
+class Layer:
+    pass
+
+
+def lane_row(values):
+    return jnp.pad(values, (0, LANES - values.shape[0]))[None, :]
+
+
+def pair_rows(values, per):
+    pairs = values.shape[0] // per
+    padded = jnp.pad(values.reshape(pairs, per), ((0, 0), (0, 8 - per)))
+    return jnp.broadcast_to(padded[:, :, None], (pairs, 8, LANES))
+
+
+def from_pairs(values, per):
+    return values[:, :per, 0].reshape(-1)
+
+
+def unpack(pack, heads, head_size, inner, width):
+    layer = Layer()
+    layer.taps = jnp.concatenate([pack[: KC + 1, : inner + 2 * N], jnp.zeros((8 - KC - 1, inner + 2 * N), f32)], axis=0)
+    layer.norm_gain = pack[KC + 1 : KC + 2, :width]
+    layer.gate_gain = pack[KC + 2 : KC + 3, :inner]
+    small = pack[KC + 3, : 3 * heads].reshape(3, heads)
+    per = LANES // head_size
+    decay = -jnp.exp(small[1])
+    layer.bias_lanes, layer.decay_lanes = lane_row(small[0]), lane_row(decay)
+    layer.bias_rows, layer.decay_rows = pair_rows(small[0], per), pair_rows(decay, per)
+    layer.skip = jnp.repeat(small[2], head_size)[None, :]
+    return layer
+
+
+transposed = (((0,), (0,)), ((), ()))
+across = (((1,), (1,)), ((), ()))
+
+
+def project(layer, marks, seg_row, head_size, held=()):
+    layer.pre = jnp.dot(layer.normed, layer.mix[:, LANES:], preferred_element_type=f32).astype(bf16)
+    step = jnp.dot(layer.normed, layer.mix[:, :LANES], preferred_element_type=f32)
+    layer.halo = lax.ppermute(layer.pre[-HALO:], "section", [(0, 1)])
+    (layer.conv, layer.y, layer.own_state, last_state, layer.cum, layer.rate, layer.cum_rows, layer.step_rows) = scan_forward(
+        layer.pre, layer.halo, layer.taps, marks, seg_row, step, layer.bias_lanes, layer.decay_lanes, head_size, held
+    )
+    layer.state_in = lax.ppermute(last_state, "section", [(0, 1)])
+
+
+def gate(layer, marks, grad=None):
+    layer.gate = jnp.dot(layer.normed, layer.gate_weight, preferred_element_type=f32)
+    layer.ssm, layer.gained, layer.entering, sums = gate_forward(
+        layer.y, layer.conv, layer.cum, marks, layer.own_state, layer.state_in, layer.gate, layer.skip, layer.gate_gain, grad
+    )
+    return sum_over_tensor(sums)
+
+
+def gate_side(layer, grad, sums, marks, channels, held=()):
+    (layer.out_grad, layer.gate_grad, layer.pulled, first, layer.gain_grad, layer.skip_grad, layer.gate_dots) = gate_backward(
+        grad, layer.gate, layer.ssm, layer.conv, layer.cum, marks, sums, layer.gate_gain, channels, held
+    )
+    layer.after = lax.ppermute(first, "section", [(1, 0)])
+
+
+def scan_side(layer, marks, seg_row, head_size, held_intra=(), held_scan=(), held_conv=(), after_intra=None, late_held=None):
+    per = LANES // head_size
+    scaled_grad, rate_rows, b_intra, c_intra = intra_backward(
+        layer.out_grad, layer.conv, layer.cum, layer.rate, layer.cum_rows, marks, seg_row, head_size, held_intra
+    )
+    if after_intra is not None:
+        held_conv = (*held_conv, *after_intra(rate_rows))
+    conv_grad, layer.taps_grad, step_grad, log_grad, bias_grad = scan_backward(
+        layer.out_grad, scaled_grad, layer.conv, layer.cum, layer.rate, rate_rows, layer.step_rows, layer.entering,
+        layer.pulled, layer.after, layer.skip, layer.decay_rows, b_intra, c_intra, layer.pre, layer.halo,
+        layer.taps, marks, head_size, held_scan,
+    )
+    next_grad = lax.ppermute(conv_grad[:8], "section", [(1, 0)])
+    if late_held is not None:
+        held_conv = (*held_conv, *late_held(conv_grad))
+    layer.mix_grad, layer.map_grad, dots = conv_backward(
+        conv_grad, next_grad, layer.taps, marks, layer.pre, layer.gate_dots, step_grad, layer.step_rows,
+        layer.bias_rows, head_size, held_conv,
+    )
+    layer.dots = sum_over_tensor(dots)
+    heads = layer.skip_grad.shape[1] // head_size
+    layer.small = jnp.concatenate([
+        from_pairs(bias_grad, per), from_pairs(log_grad, per), layer.skip_grad.reshape(heads, head_size).sum(axis=1)
+    ])
+
+
+def scatter_rows(term):
+    return lax.psum_scatter(term, ("ctx", "section"), scatter_dimension=0, tiled=True)
+
+
+def whole_micro_body(
+    tokens, cotangent, seg_ids, norm_gain, in_zx, in_bc, in_dt, conv_x, conv_xb, conv_bc, conv_bcb, dt_bias, a_log,
+    skip_gain, gate_gain, out_w,
+):
+    section, ctx, tensor = (lax.axis_index(a) for a in ("section", "ctx", "tensor"))
+    tensors, ctxs = lax.axis_size("tensor"), lax.axis_size("ctx")
+    width = tokens.shape[2]
+    own_width = width // tensors
+    inner = conv_x.shape[2]
+    heads = dt_bias.shape[1]
+    head_size = inner // heads
+    mixed = inner + 2 * N
+    channels = inner * tensors
+    rows = seg_ids.shape[1] // 2
+    index = tensor.astype(jnp.int32).reshape(1)
+
+    def block_rows(weight, b):
+        return lax.dynamic_slice_in_dim(weight, b * own_width, own_width, 0)
+
+    def gather_rows(half):
+        return lax.all_gather(half, ("ctx", "section"), axis=0, tiled=True)
+
+    own_mix = jnp.concatenate([jnp.pad(in_dt[0], ((0, 0), (0, LANES - heads))), in_zx[0, :, 1], in_bc[0]], axis=1)
+    mix_halves = in_halves(own_mix, section)
+    mix_first = gather_rows(mix_halves[0])
+    token_block = to_micro(tokens)
+    rest_halves = in_halves(jnp.concatenate([in_zx[0, :, 0], out_w[0].T], axis=1), section)
+
+    def line(values):
+        return jnp.pad(values.astype(f32), (0, width - values.shape[0]))[None, :]
+
+    own_pack = jnp.concatenate(
+        [line(jnp.concatenate([conv_x[0, k], conv_bc[0, k]])) for k in range(KC)]
+        + [
+            line(jnp.concatenate([conv_xb[0], conv_bcb[0]])), line(norm_gain[0]), line(gate_gain[0]),
+            line(jnp.concatenate([dt_bias[0], a_log[0], skip_gain[0]])),
+        ],
+        axis=0,
+    )
+    other_pack = swap_section(own_pack)
+    first, second = (
+        unpack(jnp.where(section == n, own_pack, other_pack), heads, head_size, inner, width) for n in range(2)
+    )
+    seg_mine = lax.dynamic_index_in_dim(seg_ids, ctx, 0, keepdims=False)
+    seg_around = jnp.concatenate([jnp.full((HALO,), -1, jnp.int32), seg_mine, jnp.full((HALO,), -2, jnp.int32)])
+    seg_around = lax.dynamic_slice_in_dim(seg_around, section * rows, rows + 2 * HALO, 0)
+    marks, seg_row = token_marks(seg_around, rows)
+
+    first.block = token_block
+    first.gate_weight = gather_rows(ordered(rest_halves[0][:, :inner], token_block))
+    first.normed, first.in_scale = join_norm(with_partners(first.block), index, first.norm_gain, rows)
+    first.out_turned = gather_rows(ordered(rest_halves[0][:, inner:], first.normed))
+    first.mix = mix_first
+    project(first, marks, seg_row, head_size)
+    second.mix = gather_rows(ordered(mix_halves[1], first.pre))
+    rest_second = gather_rows(ordered(rest_halves[1], first.conv))
+    second.gate_weight, second.out_turned = rest_second[:, :inner], rest_second[:, inner:]
+    cot_block = to_micro(ordered(cotangent, first.pre))
+    sums_first = gate(first, marks)
+
+    def gate_low(layer, sums):
+        layer.gated = (layer.gained * lax.rsqrt(sums[0] / channels + epsilon)[:, None]).astype(bf16)
+
+    def blocks_of(total, dtype):
+        parts = [column_block(total, tensor ^ n, own_width) for n in range(tensors)]
+        return [parts[0]] + [part.astype(dtype) for part in parts[1:]]
+
+    def out_terms(layer, dtype):
+        return blocks_of(lax.dot_general(layer.gated, layer.out_turned, across, preferred_element_type=f32), dtype)
+
+    gate_low(first, sums_first)
+    terms = out_terms(first, f32)
+    projected = sum([from_partner(terms[n], n) for n in range(1, tensors)], terms[0])
+    second.block = (first.block.astype(f32) + projected).astype(bf16)
+
+    second.normed, second.in_scale = join_norm(with_partners(second.block), index, second.norm_gain, rows)
+    project(second, marks, seg_row, head_size)
+    cot_full = join(with_partners(ordered(cot_block, second.pre)), index, bf16, 0)
+    grad_second = jnp.dot(cot_full, second.out_turned, preferred_element_type=f32)
+    sums_second = gate(second, marks, grad_second)
+
+    def input_terms(layer):
+        total = lax.dot_general(layer.gate_grad, layer.gate_weight, across, preferred_element_type=f32)
+        total = total + lax.dot_general(layer.mix_grad, layer.mix, across, preferred_element_type=f32)
+        return blocks_of(total, bf16)
+
+    def send_terms(layer, terms):
+        return [from_partner(ordered(terms[n], layer.dots), n) for n in range(1, tensors)]
+
+    def input_side(layer, own, sent, out_grad_block, held=()):
+        return input_gradient(
+            own, sent, layer.dots, layer.block, out_grad_block, layer.in_scale,
+            column_block(layer.norm_gain, tensor, own_width), width, held,
+        )
+
+    def rest_term(layer, out_grad, *others):
+        low = [
+            lax.dot_general(layer.normed, ordered(layer.gate_grad, *others), transposed, preferred_element_type=f32).astype(bf16),
+            lax.dot_general(out_grad, layer.gated, transposed, preferred_element_type=f32).astype(bf16),
+        ]
+        return jnp.concatenate(low, axis=1)
+
+    def share(layer, *others):
+        count = rows // tensors
+        map_grad = ordered(layer.map_grad, *others)
+
+        def part(b):
+            return lax.dynamic_slice_in_dim(map_grad, b * count, count, 0)
+
+        total = sum([from_partner(part(tensor ^ k), k) for k in range(1, tensors)], part(tensor))
+        layer.map_share = total.astype(bf16)
+
+    def mix_start(layer):
+        return lax.dot_general(layer.normed, layer.mix_grad, transposed, preferred_element_type=f32).astype(bf16)
+
+    def mix_term(layer, started, *others):
+        pieces = [ordered(piece, *others) for piece in with_partners(layer.map_share)]
+        return place_maps(index, started, layer.normed, pieces, LANES + inner)
+
+    def small_pack(layer, norm_grad):
+        def row(values):
+            return jnp.pad(values, (0, mixed - values.shape[0]))[None, :]
+
+        return jnp.concatenate(
+            [layer.taps_grad, row(layer.gain_grad[0]), row(layer.small), row(norm_grad[0]), jnp.zeros((5, mixed), f32)], axis=0
+        )
+
+    gate_low(second, sums_second)
+    out_second = lax.dot_general(second.gated, second.out_turned, across, preferred_element_type=f32).astype(bf16)
+    result = lax.psum_scatter(out_second, "tensor", scatter_dimension=1, tiled=True)
+    gate_side(second, grad_second, sums_second, marks, channels, (out_second,))
+    rest_term_second = rest_term(second, cot_full)
+    rest_sum_second = scatter_rows(rest_term_second)
+    scan_side(second, marks, seg_row, head_size, held_scan=(rest_term_second,), held_conv=(result,))
+    terms = input_terms(second)
+    sent = send_terms(second, terms)
+    middle_block, norm_second = input_side(second, terms[0], sent, cot_block)
+    share(second, *sent)
+    result = (second.block.astype(f32) + ordered(result, second.dots).astype(f32)).astype(bf16)
+    output_pieces = to_owners([second.block, result])
+    mix_started = mix_start(second)
+    middle = join(with_partners(middle_block), index, bf16, 0, (mix_started, output_pieces))
+    mix_term_second = mix_term(second, mix_started, rest_sum_second, middle)
+    mix_sum_second = scatter_rows(mix_term_second)
+
+    grad_first = jnp.dot(middle, first.out_turned, preferred_element_type=f32)
+    crossed = jnp.sum(grad_first * first.gained, axis=1)
+    crossed = sum_over_tensor(jnp.broadcast_to(crossed[None, :], (8, rows)))
+    sums_first = jnp.concatenate([sums_first[:1], crossed[:1], sums_first[2:]], axis=0)
+    gate_side(first, grad_first, sums_first, marks, channels)
+    outputs = lax.all_gather(ordered(output_pieces, first.out_grad), "tensor", axis=0, tiled=False)
+    rest_terms = []
+
+    def after_scan(conv_grad):
+        rest_terms.append(rest_term(first, middle, conv_grad))
+        return rest_terms
+
+    scan_side(
+        first, marks, seg_row, head_size, held_intra=(mix_term_second,), held_conv=(rest_sum_second, mix_sum_second), late_held=after_scan,
+    )
+    rest_sum_first = scatter_rows(rest_terms[0])
+    terms = input_terms(first)
+    sent = send_terms(first, terms)
+    share(first, first.dots)
+    last_block, norm_first = input_side(first, terms[0], sent, middle_block, (outputs,))
+    grad_pieces = to_owners([last_block, middle_block])
+    grads = with_partners(grad_pieces)
+    mix_sum_first = scatter_rows(mix_term(first, mix_start(first), rest_sum_first, grad_pieces))
+    places = jnp.stack([tensor, ctx]).astype(jnp.int32)
+    outputs = join_gathered(places, outputs, bf16, (last_block,))
+
+    rest_sum = own_layer([rest_sum_first, rest_sum_second], section).astype(f32)
+    mix_sum = own_layer([mix_sum_first, mix_sum_second], section).astype(f32)
+    bc_sum = mix_sum[:, LANES + inner :]
+    pack_first, pack_second = ordered(small_pack(first, norm_first), grads[1]), small_pack(second, norm_second)
+    pack = jnp.where(section == 0, pack_first, pack_second) + swap_section(
+        jnp.where(section == 0, pack_second, pack_first)
+    )
+    pack = sum(
+        [lax.ppermute(pack, "ctx", [(c, (c + d) % ctxs) for c in range(ctxs)]) for d in range(1, ctxs)], pack
+    )
+    shared = with_partners(jnp.concatenate([pack[:8, inner:], jnp.broadcast_to(pack[10:11, :own_width], (8, own_width))], axis=1))
+    taps_bc = sum([piece[:, : 2 * N] for piece in shared[1:]], shared[0][:, : 2 * N])
+    norm = join([piece[:, 2 * N :] for piece in shared], index, f32, 0)[0]
+    small = pack[9, : 3 * heads].reshape(3, heads)
+    zx_sum = jnp.stack([rest_sum[:, :inner], mix_sum[:, LANES : LANES + inner]], axis=1)
+    out_sum = rest_sum[:, inner:].T
+    input_grads = join_micro(places, grads, f32, (outputs,))
+    return (
+        outputs.reshape(1, ctxs, -1, width),
+        input_grads.reshape(1, ctxs, -1, width),
+        norm[None],
+        zx_sum[None],
+        bc_sum[None],
+        mix_sum[:, :heads][None],
+        pack[:KC, :inner][None],
+        pack[KC, :inner][None],
+        taps_bc[:KC][None],
+        taps_bc[KC][None],
+        small[0][None],
+        small[1][None],
+        small[2][None],
+        pack[8, :inner][None],
+        out_sum[None],
+    )
+
+
+def fits(shape, batches):
+    return shape["ctx"] == batches == 4 and shape["section"] == 2 and shape["tensor"] & (shape["tensor"] - 1) == 0
+
+
 def solution(mesh):
-    return jax.shard_map(
-        body,
-        mesh=mesh,
-        in_specs=(
-            P(None, "ctx", None),
-            P(None, "ctx", None),
-            P(),
-            P("section", None),
-            P("section", "ctx", None, "tensor"),
-            P("section", "ctx", None),
-            P("section", "ctx", "tensor"),
-            P("section", None, "tensor"),
-            P("section", "tensor"),
-            P("section", None, None),
-            P("section", None),
-            P("section", "tensor"),
-            P("section", "tensor"),
-            P("section", "tensor"),
-            P("section", "tensor"),
-            P("section", "tensor", "ctx"),
-        ),
-        out_specs=(
-            P("section", None, "ctx", None),
-            P("section", None, "ctx", None),
-            P("section", None),
-            P("section", "ctx", None, "tensor"),
-            P("section", "ctx", None),
-            P("section", "ctx", "tensor"),
-            P("section", None, "tensor"),
-            P("section", "tensor"),
-            P("section", None, None),
-            P("section", None),
-            P("section", "tensor"),
-            P("section", "tensor"),
-            P("section", "tensor"),
-            P("section", "tensor"),
-            P("section", "tensor", "ctx"),
-        ),
-        check_vma=False,
-    )
+    def step(*args):
+        chosen = whole_micro_body if fits(dict(mesh.shape), args[0].shape[0]) else body
+        return jax.shard_map(
+            chosen,
+            mesh=mesh,
+            in_specs=(
+                P(None, "ctx", None),
+                P(None, "ctx", None),
+                P(),
+                P("section", None),
+                P("section", "ctx", None, "tensor"),
+                P("section", "ctx", None),
+                P("section", "ctx", "tensor"),
+                P("section", None, "tensor"),
+                P("section", "tensor"),
+                P("section", None, None),
+                P("section", None),
+                P("section", "tensor"),
+                P("section", "tensor"),
+                P("section", "tensor"),
+                P("section", "tensor"),
+                P("section", "tensor", "ctx"),
+            ),
+            out_specs=(
+                P("section", None, "ctx", None),
+                P("section", None, "ctx", None),
+                P("section", None),
+                P("section", "ctx", None, "tensor"),
+                P("section", "ctx", None),
+                P("section", "ctx", "tensor"),
+                P("section", None, "tensor"),
+                P("section", "tensor"),
+                P("section", None, None),
+                P("section", None),
+                P("section", "tensor"),
+                P("section", "tensor"),
+                P("section", "tensor"),
+                P("section", "tensor"),
+                P("section", "tensor", "ctx"),
+            ),
+            check_vma=False,
+        )(*args)
+
+    return step

time: 2770 us -> 661 us (0.24)
  waiting for transfers between devices: 1120 us -> 175 us
  other arithmetic: 452 us -> 25.2 us
  matrix products: 457 us -> 68.7 us
  local copies, waits for them, and re-layouts: 443 us -> 119 us
  blocking collectives: 187 us -> 0 us
  Pallas kernels: 0 us -> 139 us
  starting transfers between devices: 56.2 us -> 107 us
    psum x12 -> x0, waiting for transfers between devices: 646 us -> none  [the longest x5 248 us: body(): lax.psum(jnp.dot(gate_normed, out_full, preferred_element_type=jnp.float3...]
    dot_general x175 -> x20, matrix products: 457 us -> 68.7 us  [the longest x2 10.6 us: mix_start(): lax.dot_general(layer.normed, layer.mix_grad, transposed, preferred_eleme...]
    all_gather x12 -> x6, waiting for transfers between devices: 250 us -> 1.95 us  [the longest x5 1.95 us: gather_rows(): return lax.all_gather(half, ('ctx', 'section'), axis=0, tiled=True)]
    unnamed x30 -> x12, waiting for transfers between devices: 220 us -> 0.18 us
    ppermute x18 -> x83, waiting for transfers between devices: 2.57 us -> 170 us  [the longest x54 111 us: from_partner(): lax.ppermute(value, 'tensor', [(i, i ^ distance) for i in range(count)])]
    pallas_call x0 -> x50, Pallas kernels: none -> 139 us  [the longest x19 127 us: call(): return lambda *args: made(*held, *args)]
    another operation x92 -> x2, other arithmetic: 126 us -> 0.15 us  [the longest x1 0.08 us: token_marks(): jnp.stack(columns, axis=1)]
    all_gather x12 -> x0, blocking collectives: 111 us -> none  [the longest x10 71.8 us: prefix(): pieces = jax.tree.map(lambda part: lax.all_gather(part, axis), value)]
  transfers between devices with their start and end apart: 45 -> 94, of which waited for: 28 -> 35; matrix products, arithmetic and copies ran while one was open for 20% -> 20% of each run, Pallas kernels for 0% -> 20%
where the time goes in v1:
time: 661 us; the launch traced here: 650 us
  waiting for transfers between devices  175 us (26%)
  Pallas kernels  139 us (21%)
  local copies, waits for them, and re-layouts  119 us (18%)
  starting transfers between devices  107 us (16%)
  matrix products  68.7 us (10%)
  other arithmetic  25.2 us (4%)
  between operations  16.4 us (2%)
    pallas_call x19, Pallas kernels, call(): return lambda *args: made(*held, *args)  127 us
    ppermute x54, waiting for transfers between devices, from_partner(): lax.ppermute(value, 'tensor', [(i, i ^ distance) for i in range(count)])  111 us
    unnamed x379, local copies, waits for them, and re-layouts  81.3 us
    ppermute x54, starting transfers between devices, from_partner(): lax.ppermute(value, 'tensor', [(i, i ^ distance) for i in range(count)])  47.7 us
    ppermute x8, waiting for transfers between devices, to_owners(): pieces.append(lax.ppermute(piece, ('section', 'ctx'), route))  27.4 us
    ppermute x4, waiting for transfers between devices, to_micro(): came.append(lax.ppermute(piece, ('section', 'ctx'), route))  26.8 us
    ppermute x8, starting transfers between devices, to_owners(): pieces.append(lax.ppermute(piece, ('section', 'ctx'), route))  17.2 us
  transfers between devices with their start and end apart: 94, of which 35 were waited for; matrix products, arithmetic and copies ran while one was open for 20% of the time, Pallas kernels for 20%

profile of v1, /device:TPU:9, one launch (start us, length us, event | category | flops | bytes accessed | tf_op | source)
XLA Modules:
  0.0 650.2 jit_solution(5866538438148527543)
XLA Ops:
  27.0 14.5 %collective-permute-done = bf16[256,384]{1,0:T(8,128)(2,1)S(1)} collective-permute-done((bf16[256,384]{1,0:T(8,128)(2,1)S(1)}, bf16[256,384]{1,0:T(8,128)(2,1)S(1)}, u32[]{:S(2)}, u32[]{:S(2)}) %collective-permute-start) | collective-permute-done | bytes 196640 | tf_op jit(solution)/shard_map/ppermute | solution.py:1390
  41.5 12.3 %collective-permute-done.1 = bf16[256,384]{1,0:T(8,128)(2,1)S(1)} collective-permute-done((bf16[256,384]{1,0:T(8,128)(2,1)S(1)}, bf16[256,384]{1,0:T(8,128)(2,1)S(1)}, u32[]{:S(2)}, u32[]{:S(2)}) %collective-permute-start.1) | collective-permute-done | bytes 196640 | tf_op jit(solution)/shard_map/ppermute | solution.py:1390
  60.2 7.5 %collective-permute-done.3.refs_3_ = bf16[512,384]{1,0:T(8,128)(2,1)S(1)} collective-permute-done((bf16[512,384]{1,0:T(8,128)(2,1)S(1)}, bf16[512,384]{1,0:T(8,128)(2,1)S(1)}, u32[]{:S(2)}, u32[]{:S(2)}) %collective-permute-start.3) | collective-permute-done | bytes 393248 | tf_op jit(solution)/shard_map/ppermute | solution.py:1362
  68.4 8.5 %collective-permute-done.5.refs_5_ = bf16[512,384]{1,0:T(8,128)(2,1)S(1)} collective-permute-done((bf16[512,384]{1,0:T(8,128)(2,1)S(1)}, bf16[512,384]{1,0:T(8,128)(2,1)S(1)}, u32[]{:S(2)}, u32[]{:S(2)}) %collective-permute-start.5) | collective-permute-done | bytes 393248 | tf_op jit(solution)/shard_map/ppermute | solution.py:1362
  91.2 15.4 %scan_forward.2 = (f32[512,1024]{1,0:T(8,128)}, f32[512,768]{1,0:T(8,128)S(1)}, f32[2,128,768]{2,1,0:T(8,128)S(1)}, f32[128,768]{1,0:T(8,128)S(1)}, f32[512,768]...) custom-call(bf16[512,1024]{1,0:T(8,128)(2,1)S(1)} %copy-done.6, ...), custom_call_target="tpu_custom_call" | custom-call | bytes 45000000 | tf_op jit(solution)/shard_map/scan_forward/pallas_call | solution.py:191
  118.1 6.2 gate_forward.2
  151.5 7.6 %collective-permute-done.15 = f32[512,384]{1,0:T(8,128)S(1)} collective-permute-done((f32[512,384]{1,0:T(8,128)}, f32[512,384]{1,0:T(8,128)S(1)}, u32[]{:S(2)}, u32[]{:S(2)}) %collective-permute-start.15) | collective-permute-done | bytes 786464 | tf_op jit(solution)/shard_map/ppermute | solution.py:1362
  159.0 17.9 %collective-permute-done.14 = f32[512,384]{1,0:T(8,128)S(1)} collective-permute-done((f32[512,384]{1,0:T(8,128)}, f32[512,384]{1,0:T(8,128)S(1)}, u32[]{:S(2)}, u32[]{:S(2)}) %collective-permute-start.14) | collective-permute-done | bytes 786464 | tf_op jit(solution)/shard_map/ppermute | solution.py:1362
  181.9 6.7 %collective-permute-done.16.refs_3_ = bf16[512,384]{1,0:T(8,128)(2,1)S(1)} collective-permute-done((bf16[512,384]{1,0:T(8,128)(2,1)S(1)}, bf16[512,384]{1,0:T(8,128)(2,1)S(1)}, u32[]{:S(2)}, u32[]{:S(2)}) %collective-permute-start.16) | collective-permute-done | bytes 393248 | tf_op jit(solution)/shard_map/ppermute | solution.py:1362
  189.4 8.6 %collective-permute-done.18.refs_5_ = bf16[512,384]{1,0:T(8,128)(2,1)S(1)} collective-permute-done((bf16[512,384]{1,0:T(8,128)(2,1)S(1)}, bf16[512,384]{1,0:T(8,128)(2,1)S(1)}, u32[]{:S(2)}, u32[]{:S(2)}) %collective-permute-start.18) | collective-permute-done | bytes 393248 | tf_op jit(solution)/shard_map/ppermute | solution.py:1362
  199.9 5.2 fusion.14.refs_0_.refs_1_.refs_17_.refs_5_
  213.1 15.4 %scan_forward.3 = (f32[512,1024]{1,0:T(8,128)}, f32[512,768]{1,0:T(8,128)S(1)}, f32[2,128,768]{2,1,0:T(8,128)S(1)}, f32[128,768]{1,0:T(8,128)}, f32[512,768]{1,0...) custom-call(bf16[512,1024]{1,0:T(8,128)(2,1)S(1)} %copy-done.12, ...), custom_call_target="tpu_custom_call" | custom-call | bytes 45000000 | tf_op jit(solution)/shard_map/scan_forward/pallas_call | solution.py:191
  243.6 6.8 %gate_forward.3 = (f32[512,768]{1,0:T(8,128)S(1)}, f32[512,768]{1,0:T(8,128)S(1)}, f32[2,128,768]{2,1,0:T(8,128)S(1)}, f32[8,512]{1,0:T(8,128)S(1)}) custom-call(f32[512,768]{1,0:T(8,128)} %copy-done.50, f32[512,1024]{1,0:T(8,128)} %get-tuple-element.95.refs_1_.refs_2_.refs_4_.refs_5_.refs_3_, ...), custom_call_target="tpu_custom_call" | custom-call | bytes 18000000 | tf_op jit(solution)/shard_map/gate_forward/pallas_call | solution.py:191
  263.3 7.1 %gate_backward.2 = (f32[512,768]{1,0:T(8,128)S(1)}, bf16[512,768]{1,0:T(8,128)(2,1)S(1)}, f32[2,128,768]{2,1,0:T(8,128)S(1)}, f32[128,768]{1,0:T(8,128)S(1)}, f3...) custom-call(bf16[512,1536]{1,0:T(8,128)(2,1)S(1)} %copy-done.26, ...), custom_call_target="tpu_custom_call" | custom-call | bytes 21000000 | tf_op jit(solution)/shard_map/gate_backward/pallas_call | solution.py:191
  282.4 6.7 %collective-permute-start.29 = (f32[128,768]{1,0:T(8,128)}, f32[128,768]{1,0:T(8,128)}, u32[]{:S(2)}, u32[]{:S(2)}) collective-permute-start(f32[128,768]{1,0:T(8,128)} %copy-done.144), channel_id=1, source_target_pairs={{16,0},{17,1},{18,2},{19,3},{20,4},{21,5},{22,6},{23,7},{24,8},{25... | collective-permute-start | bytes 1179656 | tf_op jit(solution)/shard_map/ppermute | solution.py:1502
  291.7 8.4 %intra_backward.2 = (f32[512,768]{1,0:T(8,128)S(1)}, f32[6,8,512]{2,1,0:T(8,128)S(1)}, f32[512,128]{1,0:T(8,128)S(1)}, f32[512,128]{1,0:T(8,128)S(1)}) custom-call(f32[512,768]{1,0:T(8,128)S(1)} %copy-done.25, f32[512,1024]{1,0:T(8,128)} %get-tuple-element.95.refs_1_.refs_2_.refs_4_.refs_5_.refs_3_, ...), custom_call_target="tpu_custom_call" | custom-call | bytes 24000000 | tf_op jit(solution)/shard_map/intra_backward/pallas_call | solution.py:191
  301.3 16.2 %scan_backward.2 = (f32[512,1024]{1,0:T(8,128)}, f32[8,1024]{1,0:T(8,128)S(1)}, f32[6,8,512]{2,1,0:T(8,128)S(1)}, f32[6,8,128]{2,1,0:T(8,128)S(1)}, f32[6,8,128]{2,1,0:T(8,128)S(1)}) custom-call(bf16[1536,1536]{1,0:T(8,128)(2,1)} %pad_maximum_fusion.refs_0_, f32[512,768]{1,0:T(8,128)S(1)} %copy-done.25, f32[512,768]{1,0:T(8,128)} %copy-done.52, ...), custom_call_target="tpu_custom_call" | custom-call | bytes 48000000 | tf_op jit(solution)/shard_map/scan_backward/pallas_call | solution.py:191
  325.1 5.2 conv_backward.2
  345.3 5.3 convolution_convert_fusion.1.refs_0_.term_ref
  375.9 17.8 %collective-permute-done.48 = f32[128,256]{1,0:T(8,128)S(1)} collective-permute-done((f32[128,256]{1,0:T(8,128)S(1)}, f32[128,256]{1,0:T(8,128)S(1)}, u32[]{:S(2)}, u32[]{:S(2)}) %collective-permute-start.48) | collective-permute-done | bytes 131104 | tf_op jit(solution)/shard_map/ppermute | solution.py:1362
  415.9 7.4 %gate_backward.3 = (f32[512,768]{1,0:T(8,128)S(1)}, bf16[512,768]{1,0:T(8,128)(2,1)S(1)}, f32[2,128,768]{2,1,0:T(8,128)S(1)}, f32[128,768]{1,0:T(8,128)}, f32[1,...) custom-call(f32[512,768]{1,0:T(8,128)S(1)} %get-tuple-element.307.refs_0_, ...), custom_call_target="tpu_custom_call" | custom-call | bytes 21000000 | tf_op jit(solution)/shard_map/gate_backward/pallas_call | solution.py:191
  427.2 5.6 collective-permute-start.53
  439.1 8.4 %intra_backward.3 = (f32[512,768]{1,0:T(8,128)S(1)}, f32[6,8,512]{2,1,0:T(8,128)S(1)}, f32[512,128]{1,0:T(8,128)S(1)}, f32[512,128]{1,0:T(8,128)S(1)}) custom-call(bf16[1536,1152]{1,0:T(8,128)(2,1)} %place_maps.2.refs_0_, f32[512,768]{1,0:T(8,128)S(1)} %copy-done.19, f32[512,1024]{1,0:T(8,128)} %get-tuple-element.87.refs_1_.refs_2_.refs_3_.refs_4_, ...), custom_call_target="tpu_custom_call" | custom-call | bytes 24000000 | tf_op jit(solution)/shard_map/intra_backward/pallas_call | solution.py:191
  448.8 16.2 %scan_backward.3 = (f32[512,1024]{1,0:T(8,128)}, f32[8,1024]{1,0:T(8,128)S(1)}, f32[6,8,512]{2,1,0:T(8,128)S(1)}, f32[6,8,128]{2,1,0:T(8,128)S(1)}, f32[6,8,128]{2,1,0:T(8,128)S(1)}) custom-call(f32[512,768]{1,0:T(8,128)S(1)} %copy-done.19, f32[512,768]{1,0:T(8,128)} %copy-done.51, f32[512,1024]{1,0:T(8,128)} %get-tuple-element.87.refs_1_.refs_2_.refs_3_.refs_4_, ...), custom_call_target="tpu_custom_call" | custom-call | bytes 48000000 | tf_op jit(solution)/shard_map/scan_backward/pallas_call | solution.py:191
  484.8 7.2 %conv_backward.3 = (bf16[512,1152]{1,0:T(8,128)(2,1)S(1)}, f32[512,256]{1,0:T(8,128)S(1)}, f32[8,512]{1,0:T(8,128)S(1)}) custom-call(bf16[192,1536]{1,0:T(8,128)(2,1)S(1)} %copy-done.4, bf16[192,1152]{1,0:T(8,128)(2,1)S(1)} %copy-done.32, bf16[1536,1536]{1,0:T(8,128)(2,1)} %pad_maximum_fusion.1.refs_2_, f32[512,1024]{1,0:T(8,128)} %get-tuple-element.135.refs_1_.refs_3_, ...), custom_call_target="tpu_custom_call" | custom-call | bytes 18000000 | tf_op jit(solution)/shard_map/conv_backward/pallas_call | solution.py:191
  505.3 5.3 convolution_convert_fusion.term_ref
  517.2 5.6 collective-permute-done.60.refs_9_
  540.4 9.6 %collective-permute-done.62 = bf16[256,384]{1,0:T(8,128)(2,1)S(1)} collective-permute-done((bf16[256,384]{1,0:T(8,128)(2,1)S(1)}, bf16[256,384]{1,0:T(8,128)(2,1)S(1)}, u32[]{:S(2)}, u32[]{:S(2)}) %collective-permute-start.62) | collective-permute-done | bytes 196640 | tf_op jit(solution)/shard_map/ppermute | solution.py:1405
  550.2 10.2 %collective-permute-done.63 = bf16[256,384]{1,0:T(8,128)(2,1)S(1)} collective-permute-done((bf16[256,384]{1,0:T(8,128)(2,1)S(1)}, bf16[256,384]{1,0:T(8,128)(2,1)S(1)}, u32[]{:S(2)}, u32[]{:S(2)}) %collective-permute-start.63) | collective-permute-done | bytes 196640 | tf_op jit(solution)/shard_map/ppermute | solution.py:1405
  586.8 9.9 %collective-permute-done.65.refs_2_.refs_1_ = bf16[1024,384]{1,0:T(8,128)(2,1)S(1)} collective-permute-done((bf16[1024,384]{1,0:T(8,128)(2,1)S(1)}, bf16[1024,384]{1,0:T(8,128)(2,1)S(1)}, u32[]{:S(2)}, u32[]{:S(2)}) %collective-permute-start.65) | collective-permute-done | bytes 786464 | tf_op jit(solution)/shard_map/ppermute | solution.py:1362
  608.4 10.0 %collective-permute-done.66.refs_3_ = bf16[1024,384]{1,0:T(8,128)(2,1)} collective-permute-done((bf16[1024,384]{1,0:T(8,128)(2,1)S(1)}, bf16[1024,384]{1,0:T(8,128)(2,1)}, u32[]{:S(2)}, u32[]{:S(2)}) %collective-permute-start.66) | collective-permute-done | bytes 786464 | tf_op jit(solution)/shard_map/ppermute | solution.py:1362
  618.4 5.3 join_micro.1
  (784 shorter events, 333.7 us)
Async XLA Ops:
  7.2 72.8 %all-gather.8.cloned.1.call-start = ((), (), s32[]{:S(2)}) async-start(), calls=%async_computation.5 | async-start | bytes 3981312 | tf_op jit(solution)/shard_map/all_gather | solution.py:1555
  20.7 93.1 %all-gather.10.cloned.1.call-start = ((), (), s32[]{:S(2)}) async-start(), calls=%async_computation.6 | async-start | bytes 2654208 | tf_op jit(solution)/shard_map/all_gather | solution.py:1555
  21.1 33.6 %collective-permute-start.9 = (bf16[192,1536]{1,0:T(8,128)(2,1)S(1)}, bf16[192,1536]{1,0:T(8,128)(2,1)S(1)}, u32[]{:S(2)}, u32[]{:S(2)}) collective-permute-start(bf16[192,1536]{1,0:T(8,128)(2,1)S(1)} %fusion.19), channel_id=1, source_target_pairs={{0,16},{16,0},{1,17},{17,1},{2,18},{18,2},{3,19},{19,3},{4,20},{20... | collective-permute-start | bytes 1769480 | tf_op jit(solution)/shard_map/ppermute | solution.py:1357
  26.9 26.9 %collective-permute-start.1 = (bf16[256,384]{1,0:T(8,128)(2,1)S(1)}, bf16[256,384]{1,0:T(8,128)(2,1)S(1)}, u32[]{:S(2)}, u32[]{:S(2)}) collective-permute-start(bf16[256,384]{1,0:T(8,128)(2,1)S(1)} %get-tuple-element.239), channel_id=1, source_target_pairs={{0,4},{4,0},{8,20},{12,16},{16,12},{20,8},{24,28},{28,24},{1,5},{5... | collective-permute-start | bytes 589832 | tf_op jit(solution)/shard_map/ppermute | solution.py:1390
  56.8 77.0 %all-gather.12.cloned.1.call-start = ((), (), s32[]{:S(2)}) async-start(), calls=%async_computation.7 | async-start | bytes 2654208 | tf_op jit(solution)/shard_map/all_gather | solution.py:1555
  79.9 119.9 %all-gather.14.cloned.1.call-start = ((), (), s32[]{:S(2)}) async-start(), calls=%async_computation.8 | async-start | bytes 3981312 | tf_op jit(solution)/shard_map/all_gather | solution.py:1555
  86.0 150.7 %all-gather.16.cloned.1.call-start = ((), (), s32[]{:S(2)}) async-start(), calls=%async_computation.9 | async-start | bytes 5308416 | tf_op jit(solution)/shard_map/all_gather | solution.py:1555
  111.1 211.0 %reduce-scatter.16.cloned.1.call-start = ((), (), s32[]{:S(2)}) async-start(), calls=%async_computation.15 | async-start | bytes 1966080
  141.4 35.4 %collective-permute-start.14 = (f32[512,384]{1,0:T(8,128)}, f32[512,384]{1,0:T(8,128)S(1)}, u32[]{:S(2)}, u32[]{:S(2)}) collective-permute-start(f32[512,384]{1,0:T(8,128)} %get-tuple-element.237), channel_id=1, source_target_pairs={{0,2},{1,3},{2,0},{3,1},{4,6},{5,7},{6,4},{7,5},{8,10},{9,11},{10,... | collective-permute-start | bytes 2359304 | tf_op jit(solution)/shard_map/ppermute | solution.py:1362
  141.7 35.2 %collective-permute-start.13 = (f32[512,384]{1,0:T(8,128)}, f32[512,384]{1,0:T(8,128)S(1)}, u32[]{:S(2)}, u32[]{:S(2)}) collective-permute-start(f32[512,384]{1,0:T(8,128)} %get-tuple-element.235), channel_id=1, source_target_pairs={{0,1},{1,0},{2,3},{3,2},{4,5},{5,4},{6,7},{7,6},{8,9},{9,8},{10,11... | collective-permute-start | bytes 2359304 | tf_op jit(solution)/shard_map/ppermute | solution.py:1362
  143.7 37.2 %collective-permute-start.21 = (bf16[256,384]{1,0:T(8,128)(2,1)S(1)}, bf16[256,384]{1,0:T(8,128)(2,1)S(1)}, u32[]{:S(2)}, u32[]{:S(2)}) collective-permute-start(bf16[256,384]{1,0:T(8,128)(2,1)S(1)} %get-tuple-element.233), channel_id=1, source_target_pairs={{0,0},{4,4},{8,16},{12,20},{16,8},{20,12},{24,24},{28,28},{1,1},{5... | collective-permute-start | bytes 589832 | tf_op jit(solution)/shard_map/ppermute | solution.py:1390
  147.5 33.5 %collective-permute-start.22 = (bf16[256,384]{1,0:T(8,128)(2,1)S(1)}, bf16[256,384]{1,0:T(8,128)(2,1)S(1)}, u32[]{:S(2)}, u32[]{:S(2)}) collective-permute-start(bf16[256,384]{1,0:T(8,128)(2,1)S(1)} %get-tuple-element.234), channel_id=1, source_target_pairs={{0,4},{4,0},{8,20},{12,16},{16,12},{20,8},{24,28},{28,24},{1,5},{5... | collective-permute-start | bytes 589832 | tf_op jit(solution)/shard_map/ppermute | solution.py:1390
  205.1 29.0 %collective-permute-start.23 = (bf16[512,384]{1,0:T(8,128)(2,1)}, bf16[512,384]{1,0:T(8,128)(2,1)}, u32[]{:S(2)}, u32[]{:S(2)}) collective-permute-start(bf16[512,384]{1,0:T(8,128)(2,1)} %ordered.32.refs_1_), channel_id=1, source_target_pairs={{0,1},{1,0},{2,3},{3,2},{4,5},{5,4},{6,7},{7,6},{8,9},{9,8},{10,11... | collective-permute-start | bytes 1179656 | tf_op jit(solution)/shard_map/ppermute | solution.py:1362
  205.1 29.0 %collective-permute-start.24 = (bf16[512,384]{1,0:T(8,128)(2,1)}, bf16[512,384]{1,0:T(8,128)(2,1)}, u32[]{:S(2)}, u32[]{:S(2)}) collective-permute-start(bf16[512,384]{1,0:T(8,128)(2,1)} %ordered.32.refs_1_), channel_id=1, source_target_pairs={{0,2},{1,3},{2,0},{3,1},{4,6},{5,7},{6,4},{7,5},{8,10},{9,11},{10,... | collective-permute-start | bytes 1179656 | tf_op jit(solution)/shard_map/ppermute | solution.py:1362
  206.5 27.5 %collective-permute-start.25 = (bf16[512,384]{1,0:T(8,128)(2,1)}, bf16[512,384]{1,0:T(8,128)(2,1)}, u32[]{:S(2)}, u32[]{:S(2)}) collective-permute-start(bf16[512,384]{1,0:T(8,128)(2,1)} %ordered.32.refs_1_), channel_id=1, source_target_pairs={{0,3},{1,2},{2,1},{3,0},{4,7},{5,6},{6,5},{7,4},{8,11},{9,10},{10,... | collective-permute-start | bytes 1179656 | tf_op jit(solution)/shard_map/ppermute | solution.py:1362
  261.8 138.1 %reduce-scatter.8.cloned.1.call-start = ((), (), s32[]{:S(2)}) async-start(), calls=%async_computation.10 | async-start | bytes 5308416 | tf_op jit(solution)/shard_map/reduce_scatter | solution.py:1532
  282.4 198.8 %reduce-scatter.10.cloned.1.call-start = ((), (), s32[]{:S(2)}) async-start(), calls=%async_computation.11 | async-start | bytes 3981312 | tf_op jit(solution)/shard_map/reduce_scatter | solution.py:1532
  370.3 25.8 %collective-permute-start.41 = (bf16[512,384]{1,0:T(8,128)(2,1)S(1)}, bf16[512,384]{1,0:T(8,128)(2,1)S(1)}, u32[]{:S(2)}, u32[]{:S(2)}) collective-permute-start(bf16[512,384]{1,0:T(8,128)(2,1)S(1)} %get-tuple-element.120.refs_3_.refs_4_), channel_id=1, source_target_pairs={{0,1},{1,0},{2,3},{3,2},{4,5},{5,4},{6,7},{7,6},{8,9},{9,8},{10,11... | collective-permute-start | bytes 1179656 | tf_op jit(solution)/shard_map/ppermute | solution.py:1362
  371.6 25.8 %collective-permute-start.42 = (bf16[512,384]{1,0:T(8,128)(2,1)S(1)}, bf16[512,384]{1,0:T(8,128)(2,1)S(1)}, u32[]{:S(2)}, u32[]{:S(2)}) collective-permute-start(bf16[512,384]{1,0:T(8,128)(2,1)S(1)} %get-tuple-element.120.refs_3_.refs_4_), channel_id=1, source_target_pairs={{0,2},{1,3},{2,0},{3,1},{4,6},{5,7},{6,4},{7,5},{8,10},{9,11},{10,... | collective-permute-start | bytes 1179656 | tf_op jit(solution)/shard_map/ppermute | solution.py:1362
  371.9 25.6 %collective-permute-start.43 = (bf16[512,384]{1,0:T(8,128)(2,1)S(1)}, bf16[512,384]{1,0:T(8,128)(2,1)S(1)}, u32[]{:S(2)}, u32[]{:S(2)}) collective-permute-start(bf16[512,384]{1,0:T(8,128)(2,1)S(1)} %get-tuple-element.120.refs_3_.refs_4_), channel_id=1, source_target_pairs={{0,3},{1,2},{2,1},{3,0},{4,7},{5,6},{6,5},{7,4},{8,11},{9,10},{10,... | collective-permute-start | bytes 1179656 | tf_op jit(solution)/shard_map/ppermute | solution.py:1362
  405.7 111.5 %all-gather.18.cloned.1.call-start = ((), (), s32[]{:S(2)}) async-start(), calls=%async_computation.14 | async-start | bytes 3932160 | tf_op jit(solution)/shard_map/all_gather | solution.py:1685
  427.2 141.7 %reduce-scatter.12.cloned.1.call-start = ((), (), s32[]{:S(2)}) async-start(), calls=%async_computation.12 | async-start | bytes 5308416 | tf_op jit(solution)/shard_map/reduce_scatter | solution.py:1532
  427.2 21.5 %collective-permute-start.53 = (f32[128,768]{1,0:T(8,128)}, f32[128,768]{1,0:T(8,128)}, u32[]{:S(2)}, u32[]{:S(2)}) collective-permute-start(f32[128,768]{1,0:T(8,128)} %get-tuple-element.132), channel_id=1, source_target_pairs={{16,0},{17,1},{18,2},{19,3},{20,4},{21,5},{22,6},{23,7},{24,8},{25... | collective-permute-start | bytes 1179656 | tf_op jit(solution)/shard_map/ppermute | solution.py:1502
  474.2 158.6 %reduce-scatter.14.cloned.1.call-start = ((), (), s32[]{:S(2)}) async-start(), calls=%async_computation.13 | async-start | bytes 3981312 | tf_op jit(solution)/shard_map/reduce_scatter | solution.py:1532
  531.6 28.8 %collective-permute-start.63 = (bf16[256,384]{1,0:T(8,128)(2,1)S(1)}, bf16[256,384]{1,0:T(8,128)(2,1)S(1)}, u32[]{:S(2)}, u32[]{:S(2)}) collective-permute-start(bf16[256,384]{1,0:T(8,128)(2,1)S(1)} %get-tuple-element.257), channel_id=1, source_target_pairs={{0,0},{4,4},{8,16},{12,20},{16,8},{20,12},{24,24},{28,28},{1,1},{5... | collective-permute-start | bytes 589832 | tf_op jit(solution)/shard_map/ppermute | solution.py:1405
  535.0 30.6 %collective-permute-start.64 = (bf16[256,384]{1,0:T(8,128)(2,1)S(1)}, bf16[256,384]{1,0:T(8,128)(2,1)S(1)}, u32[]{:S(2)}, u32[]{:S(2)}) collective-permute-start(bf16[256,384]{1,0:T(8,128)(2,1)S(1)} %get-tuple-element.256), channel_id=1, source_target_pairs={{0,20},{4,16},{8,4},{12,0},{16,28},{20,24},{24,12},{28,8},{1,21},{... | collective-permute-start | bytes 589832 | tf_op jit(solution)/shard_map/ppermute | solution.py:1405
  536.1 33.4 %collective-permute-start.81 = (bf16[128,256]{1,0:T(8,128)(2,1)S(1)}, bf16[128,256]{1,0:T(8,128)(2,1)S(1)}, u32[]{:S(2)}, u32[]{:S(2)}) collective-permute-start(bf16[128,256]{1,0:T(8,128)(2,1)S(1)} %add_convert_fusion.2.refs_0_), channel_id=1, source_target_pairs={{0,3},{1,2},{2,1},{3,0},{4,7},{5,6},{6,5},{7,4},{8,11},{9,10},{10,... | collective-permute-start | bytes 196616 | tf_op jit(solution)/shard_map/ppermute | solution.py:1362
  540.4 28.5 %collective-permute-start.80 = (bf16[128,256]{1,0:T(8,128)(2,1)S(1)}, bf16[128,256]{1,0:T(8,128)(2,1)S(1)}, u32[]{:S(2)}, u32[]{:S(2)}) collective-permute-start(bf16[128,256]{1,0:T(8,128)(2,1)S(1)} %add_convert_fusion.2.refs_0_), channel_id=1, source_target_pairs={{0,2},{1,3},{2,0},{3,1},{4,6},{5,7},{6,4},{7,5},{8,10},{9,11},{10,... | collective-permute-start | bytes 196616 | tf_op jit(solution)/shard_map/ppermute | solution.py:1362
  583.0 35.4 %collective-permute-start.66 = (bf16[1024,384]{1,0:T(8,128)(2,1)S(1)}, bf16[1024,384]{1,0:T(8,128)(2,1)}, u32[]{:S(2)}, u32[]{:S(2)}) collective-permute-start(bf16[1024,384]{1,0:T(8,128)(2,1)S(1)} %copy-done.5), channel_id=1, source_target_pairs={{0,2},{1,3},{2,0},{3,1},{4,6},{5,7},{6,4},{7,5},{8,10},{9,11},{10,... | collective-permute-start | bytes 2359304 | tf_op jit(solution)/shard_map/ppermute | solution.py:1362
  584.2 34.2 %collective-permute-start.67 = (bf16[1024,384]{1,0:T(8,128)(2,1)S(1)}, bf16[1024,384]{1,0:T(8,128)(2,1)}, u32[]{:S(2)}, u32[]{:S(2)}) collective-permute-start(bf16[1024,384]{1,0:T(8,128)(2,1)S(1)} %copy-done.5), channel_id=1, source_target_pairs={{0,3},{1,2},{2,1},{3,0},{4,7},{5,6},{6,5},{7,4},{8,11},{9,10},{10,... | collective-permute-start | bytes 2359304 | tf_op jit(solution)/shard_map/ppermute | solution.py:1362
  601.8 21.9 %collective-permute-start.71 = (f32[16,1024]{1,0:T(8,128)S(1)}, f32[16,1024]{1,0:T(8,128)S(1)}, u32[]{:S(2)}, u32[]{:S(2)}) collective-permute-start(f32[16,1024]{1,0:T(8,128)S(1)} %select_add_fusion), channel_id=1, source_target_pairs={{0,12},{4,0},{8,4},{12,8},{1,13},{5,1},{9,5},{13,9},{2,14},{6,2},{... | collective-permute-start | bytes 196616 | tf_op jit(solution)/shard_map/ppermute | solution.py:1714
  601.8 21.9 %collective-permute-start.70 = (f32[16,1024]{1,0:T(8,128)S(1)}, f32[16,1024]{1,0:T(8,128)S(1)}, u32[]{:S(2)}, u32[]{:S(2)}) collective-permute-start(f32[16,1024]{1,0:T(8,128)S(1)} %select_add_fusion), channel_id=1, source_target_pairs={{0,8},{4,12},{8,0},{12,4},{1,9},{5,13},{9,1},{13,5},{2,10},{6,14},... | collective-permute-start | bytes 196616 | tf_op jit(solution)/shard_map/ppermute | solution.py:1714
  (243 other events, 1920.2 us)
Sparse Core Ops, SparseCore 0:
  20.8 44.2 all-gather.7
  67.3 34.0 all-gather.9
  103.0 30.7 all-gather.11
  135.3 46.3 all-gather.13
  183.2 52.1 all-gather.15
  261.9 34.0 reduce-scatter.15
  298.9 53.5 reduce-scatter.7
  405.8 42.9 reduce-scatter.9
  450.7 44.1 all-gather.17
  497.7 71.1 reduce-scatter.11
  577.6 47.0 reduce-scatter.13

commit v2 on v1

--- a/solution.py
+++ b/solution.py
@@ -17,7 +17,7 @@
 DI = 3072
 HALO = 16
 LANES = 128
-VMEM_BYTES = 48 * 1024 * 1024
+VMEM_BYTES = 60 * 1024 * 1024
 
 M_FWD, M_BWD, M_ENTER, M_LEAVE, M_SEG = 0, 4, 8, 9, 10
 
@@ -59,18 +59,29 @@
     return jnp.concatenate([high, high, low], axis=axis)
 
 
+def thirds(v):
+    high = v.astype(bf16)
+    rest = v - high.astype(f32)
+    middle = rest.astype(bf16)
+    return high, middle, (rest - middle.astype(f32)).astype(bf16)
+
+
+def left_exact(a):
+    high, middle, low = thirds(a)
+    return jnp.concatenate([high, middle, high, middle, low, high], axis=1)
+
+
+def right_exact(b, axis):
+    high, middle, low = thirds(b)
+    return jnp.concatenate([high, high, middle, middle, high, low], axis=axis)
+
+
 def precise_nt(a, b):
     return mm_nt(left_parts(a), right_parts(b, 1))
 
 
 def precise_mm(a, b):
     return mm(left_parts(a), right_parts(b, 0))
-
-
-def head_selector(head_size):
-    row = lax.broadcasted_iota(jnp.int32, (8, LANES), 0)
-    lane = lax.broadcasted_iota(jnp.int32, (8, LANES), 1)
-    return (row == lane // head_size).astype(bf16)
 
 
 def iota2(shape):
@@ -88,6 +99,11 @@
 def fill_padded(padded, halo_ref, pre_ref, rows):
     padded[pl.ds(0, HALO), :] = halo_ref[...].astype(f32)
     padded[pl.ds(HALO, rows), :] = pre_ref[...].astype(f32)
+
+
+def spread_marks(wide, marks_ref, first):
+    for k in range(KC - 1):
+        wide[k] = jnp.broadcast_to(marks_ref[:, first + k : first + k + 1], wide.shape[1:])
 
 
 def conv_tile(padded, taps_ref, marks, start, count):
@@ -97,7 +113,7 @@
         if k == KC - 1:
             total = total + taps_ref[k : k + 1, :] * shifted
         else:
-            total = total + taps_ref[k : k + 1, :] * (shifted * marks[start : start + count, M_FWD + k : M_FWD + k + 1])
+            total = total + taps_ref[k : k + 1, :] * (shifted * marks[k, pl.ds(start, count), :])
     return total
 
 
@@ -107,13 +123,18 @@
 def scan_forward_kernel(
     head_size, rows, pre_ref, halo_ref, taps_ref, marks_ref, seg_ref, step_ref, bias_ref, decay_ref,
     conv_ref, y_ref, own_state_ref, last_state_ref, cum_ref, rate_ref, cum_rows_ref, step_rows_ref,
-    padded, b_all, b_turned, scores, cum_all, rate_all, step_all,
+    padded, b_all, b_turned, scores, cum_all, rate_all, step_all, cum_turned, step_turned, wide_marks,
 ):
     i = pl.program_id(0)
     chunks = rows // CH
     fill_padded(padded, halo_ref, pre_ref, rows)
+
+    @pl.when(i == 0)
+    def _():
+        spread_marks(wide_marks, marks_ref, M_FWD)
+
     for start in range(0, rows, TILE):
-        value = conv_tile(padded, taps_ref, marks_ref, start, TILE)
+        value = conv_tile(padded, taps_ref, wide_marks, start, TILE)
         conv_ref[pl.ds(start, TILE), :] = value / (1.0 + jnp.exp(-value))
 
     @pl.when(i == 0)
@@ -138,8 +159,13 @@
         for n in range(chunks):
             here = pl.ds(n * CH, CH)
             same = marks_ref[here, M_SEG : M_SEG + 1] == seg_ref[0:1, here]
-            value = precise_nt(conv_ref[here, :], b_all[here, :])
+            value = mm_nt(left_exact(conv_ref[here, :]), right_exact(b_all[here, :], 1))
             scores[n] = jnp.where((r >= c) & same, value, 0.0)
+        per = LANES // head_size
+        for turned, values in ((cum_turned, cum_all), (step_turned, step_all)):
+            rows_all = values[...].T
+            for j in range(turned.shape[0]):
+                turned[j, 0:per, :] = rows_all[per * j : per * (j + 1), :]
 
     @pl.when(i >= 2)
     def _():
@@ -149,11 +175,9 @@
         widen = (row == per * j + lane // head_size).astype(f32)
         cum = lax.dot_general(cum_all[...], widen, (((1,), (0,)), ((), ())), preferred_element_type=f32, precision=precise)
         rate = lax.dot_general(rate_all[...], widen, (((1,), (0,)), ((), ())), preferred_element_type=f32, precision=precise)
-        row8, lane8 = iota2((8, LANES))
-        pick = ((lane8 == per * j + row8) & (row8 < per)).astype(f32)
-        cum_rows = mm_nt(pick, cum_all[...], precise)
+        cum_rows = cum_turned[j]
         cum_rows_ref[0] = cum_rows
-        step_rows_ref[0] = mm_nt(pick, step_all[...], precise)
+        step_rows_ref[0] = step_turned[j]
         cum_ref[...] = cum
         rate_ref[...] = rate
         lane_c = lax.broadcasted_iota(jnp.int32, (CH, LANES), 1)
@@ -162,15 +186,19 @@
             here = pl.ds(n * CH, CH)
             span = slice(n * CH, (n + 1) * CH)
             scaled = rate[span] * conv_ref[here, :]
-            scaled_parts = right_parts(scaled, 0)
             out = jnp.zeros((CH, LANES), f32)
             for h in range(per):
-                spread = cum[span, h * head_size : h * head_size + 1] - cum_rows[h : h + 1, span]
-                value = mm(left_parts(scores[n] * jnp.exp(jnp.minimum(spread, 0.0))), scaled_parts)
+                column = cum[span, h * head_size : h * head_size + 1]
+                value = []
+                for first, past in ((0, CH // 2), (CH // 2, CH)):
+                    spread = column[first:past] - cum_rows[h : h + 1, n * CH : n * CH + past]
+                    weights = scores[n, first:past, :past] * jnp.exp(jnp.minimum(spread, 0.0))
+                    value.append(mm(left_exact(weights), right_exact(scaled[:past], 0)))
+                value = jnp.concatenate(value, axis=0)
                 out = value if per == 1 else jnp.where(lane_c // head_size == h, value, out)
             y_ref[here, :] = out
             leave = jnp.exp(cum[(n + 1) * CH - 1 : (n + 1) * CH, :] - cum[span]) * marks_ref[here, M_LEAVE : M_LEAVE + 1]
-            state = precise_mm(b_turned[:, here], scaled * leave)
+            state = mm(left_exact(b_turned[:, here]), right_exact(scaled * leave, 0))
             own_state_ref[n] = state
             states.append(state)
         total = states[0]
@@ -266,6 +294,9 @@
             pltpu.VMEM((rows, LANES), f32),
             pltpu.VMEM((rows, LANES), f32),
             pltpu.VMEM((rows, LANES), f32),
+            pltpu.VMEM((pairs, 8, rows), f32),
+            pltpu.VMEM((pairs, 8, rows), f32),
+            pltpu.VMEM((KC - 1, rows, LANES), f32),
         ],
         compiler_params=params(),
         cost_estimate=cost(15),
@@ -278,10 +309,15 @@
     *rest,
 ):
     if with_grad:
-        grad_ref, ssm_ref, gated_ref, entering_ref, sums_ref = rest
+        grad_ref, ssm_ref, gated_ref, entering_ref, sums_ref, c_parts, squares, products = rest
     else:
-        ssm_ref, gated_ref, entering_ref, sums_ref = rest
+        ssm_ref, gated_ref, entering_ref, sums_ref, c_parts, squares = rest
     i = pl.program_id(0)
+
+    @pl.when(i == 0)
+    def _():
+        c_parts[...] = left_exact(c_ref[...])
+
     state = state_ref[...]
     for n in range(chunks):
         here = pl.ds(n * CH, CH)
@@ -289,7 +325,7 @@
         enter = jnp.exp(cum_ref[here, :]) * marks_ref[here, M_ENTER : M_ENTER + 1]
         ssm_ref[here, :] = (
             y_ref[here, :]
-            + enter * precise_mm(c_ref[here, :], state)
+            + enter * mm(c_parts[here, :], right_exact(state, 0))
             + skip_ref[...] * conv_ref[here, :]
         )
         state = enter[CH - 1 : CH, :] * state + own_state_ref[n]
@@ -297,18 +333,23 @@
     gated = ssm_ref[...] * (gate * sigmoid(gate))
     scaled = gated * gain_ref[...]
     gated_ref[...] = scaled
-    row = lax.broadcasted_iota(jnp.int32, (8, LANES), 0)
-    sums = rows_of((row == 0).astype(bf16), gated * gated)
-    if with_grad:
-        sums = sums + rows_of((row == 1).astype(bf16), scaled * grad_ref[...])
+    totals = [(squares, gated * gated)] + ([(products, scaled * grad_ref[...])] if with_grad else [])
 
     @pl.when(i == 0)
     def _():
-        sums_ref[...] = sums
+        for total, value in totals:
+            total[...] = value
 
     @pl.when(i > 0)
     def _():
-        sums_ref[...] += sums
+        for total, value in totals:
+            total[...] += value
+
+    @pl.when(i == pl.num_programs(0) - 1)
+    def _():
+        row = lax.broadcasted_iota(jnp.int32, (8, LANES), 0)
+        sums = [rows_of((row == n).astype(bf16), total[...]) for n, (total, _) in enumerate(totals)]
+        sums_ref[...] = sum(sums[1:], sums[0])
 
 
 def gate_forward(y, conv, cum, marks, own_state, state_in, gate, skip, gain, grad=None, held=()):
@@ -339,6 +380,7 @@
             jax.ShapeDtypeStruct((chunks, N, inner), f32),
             jax.ShapeDtypeStruct((8, rows), f32),
         ],
+        scratch_shapes=[pltpu.VMEM((rows, 6 * N), bf16)] + [pltpu.VMEM((rows, LANES), f32)] * (1 if grad is None else 2),
         compiler_params=params(),
         cost_estimate=cost(6),
         name="gate_forward",
@@ -348,7 +390,7 @@
 def gate_backward_kernel(
     chunks, channels, grad_ref, gate_ref, ssm_ref, conv_ref, c_ref, cum_ref, marks_ref, sums_ref, gain_ref,
     out_grad_ref, gate_grad_ref, pulled_ref, first_ref, gain_grad_ref, skip_grad_ref, dots_ref,
-    scale_all, shift_all, c_turned,
+    scale_all, shift_all, c_turned, products,
 ):
     i = pl.program_id(0)
 
@@ -359,7 +401,8 @@
         rows = scale.shape[1]
         scale_all[...] = jnp.broadcast_to(scale, (LANES, rows)).T
         shift_all[...] = jnp.broadcast_to(shift, (LANES, rows)).T
-        c_turned[...] = c_ref[...].T
+        for n in range(chunks):
+            c_turned[n] = left_parts(c_ref[pl.ds(n * CH, CH), :].T)
 
     gate = gate_ref[...]
     sig = sigmoid(gate)
@@ -375,13 +418,12 @@
     skip_grad_ref[...] = jnp.sum(out_grad * conv_ref[...], axis=0, keepdims=True)
     gate_grad = gated_grad * ssm * (sig * (1.0 + gate * (1.0 - sig)))
     gate_grad_ref[...] = gate_grad.astype(bf16)
-    row = lax.broadcasted_iota(jnp.int32, (8, LANES), 0)
-    dots = rows_of((row == 0).astype(bf16), gate_grad * gate)
+    dots = gate_grad * gate
     kept = []
     for n in range(chunks):
         here = pl.ds(n * CH, CH)
         enter = jnp.exp(cum_ref[here, :]) * marks_ref[here, M_ENTER : M_ENTER + 1]
-        pulled = precise_mm(c_turned[:, here], out_grad_ref[here, :] * enter)
+        pulled = mm(c_turned[n], right_parts(out_grad_ref[here, :] * enter, 0))
         pulled_ref[n] = pulled
         kept.append((enter[CH - 1 : CH, :], pulled))
     first = kept[-1][1]
@@ -391,11 +433,16 @@
 
     @pl.when(i == 0)
     def _():
-        dots_ref[...] = dots
+        products[...] = dots
 
     @pl.when(i > 0)
     def _():
-        dots_ref[...] += dots
+        products[...] += dots
+
+    @pl.when(i == pl.num_programs(0) - 1)
+    def _():
+        row = lax.broadcasted_iota(jnp.int32, (8, LANES), 0)
+        dots_ref[...] = rows_of((row == 0).astype(bf16), products[...])
 
 
 def gate_backward(grad, gate, ssm, conv, cum, marks, sums, gain, channels, held=()):
@@ -424,7 +471,10 @@
             jax.ShapeDtypeStruct((1, inner), f32),
             jax.ShapeDtypeStruct((8, rows), f32),
         ],
-        scratch_shapes=[pltpu.VMEM((rows, LANES), f32), pltpu.VMEM((rows, LANES), f32), pltpu.VMEM((N, rows), f32)],
+        scratch_shapes=[
+            pltpu.VMEM((rows, LANES), f32), pltpu.VMEM((rows, LANES), f32), pltpu.VMEM((chunks, N, 3 * CH), bf16),
+            pltpu.VMEM((rows, LANES), f32),
+        ],
         compiler_params=params(),
         cost_estimate=cost(7),
         name="gate_backward",
@@ -450,6 +500,7 @@
             scores_grad[n] = jnp.zeros((CH, CH), f32)
 
     from_row = (r >= c).astype(bf16)
+    from_row = jnp.concatenate([from_row, from_row], axis=0)
     lane_c = lax.broadcasted_iota(jnp.int32, (CH, LANES), 1)
     rate_rows_ref[...] = jnp.zeros(rate_rows_ref.shape, f32)
     for n in range(chunks):
@@ -467,7 +518,7 @@
             out = jnp.where(mine, value, out)
             weights_grad = mm_nt(left_parts(jnp.where(mine, scaled, 0.0)), grad_parts)
             scores_grad[n] += decay * weights_grad
-            flow = mm((weights * weights_grad).astype(bf16), from_row)
+            flow = mm(jnp.concatenate(split(weights * weights_grad), axis=1), from_row)
             rate_rows_ref[0, h : h + 1, here] = jnp.sum(jnp.where(r < c, flow, 0.0), axis=0, keepdims=True)
         scaled_grad_ref[here, :] = out
 
@@ -505,7 +556,7 @@
         ],
         scratch_shapes=[pltpu.VMEM((chunks, CH, CH), f32), pltpu.VMEM((chunks, CH, CH), f32)],
         compiler_params=params(),
-        cost_estimate=cost(8),
+        cost_estimate=cost(3),
         name="intra_backward",
     )(out_grad, conv, conv, conv, cum, rate, cum_rows, marks, seg_row)
 
@@ -514,27 +565,28 @@
     head_size, rows, pairs, out_grad_ref, scaled_grad_ref, conv_ref, b_ref, c_ref, cum_ref, rate_ref, rate_rows_ref, step_rows_ref,
     entering_ref, pulled_ref, after_ref, skip_ref, decay_ref, b_intra_ref, c_intra_ref, pre_ref, halo_ref, taps_ref, marks_ref,
     conv_grad_ref, taps_grad_ref, step_grad_ref, log_grad_ref, bias_grad_ref,
-    padded, b_total, c_total, current,
+    padded, b_total, c_total, current, head_sums, wide_marks,
 ):
     i = pl.program_id(0)
     chunks = rows // CH
     fill_padded(padded, halo_ref, pre_ref, rows)
 
+    per = LANES // head_size
+
     @pl.when(i == 0)
     def _():
         b_total[...] = b_intra_ref[...]
         c_total[...] = c_intra_ref[...]
+        head_sums[...] = jnp.zeros(head_sums.shape, f32)
+        spread_marks(wide_marks, marks_ref, M_FWD)
 
     @pl.when(i < pairs)
     def _():
-        selector = head_selector(head_size)
-        r, c = iota2((CH, CH))
-        from_row = (r >= c).astype(bf16)
-        before = (r < c).astype(bf16)
         after = after_ref[...]
-        log_total = jnp.zeros((8, 1), f32)
-        bias_total = jnp.zeros((8, 1), f32)
-        decay = decay_ref[0, :, 0:1]
+        row, lane = iota2((6 * LANES, LANES))
+        quantity = (row // LANES) % 3
+        selector = (lane == 8 * i + per * quantity + (row % LANES) // head_size).astype(bf16)
+        last_row = lax.broadcasted_iota(jnp.int32, (CH, LANES), 0) == CH - 1
         for n in reversed(range(chunks)):
             here = pl.ds(n * CH, CH)
             last = (n + 1) * CH - 1
@@ -548,32 +600,49 @@
             scaled = rate * conv
             out_grad = out_grad_ref[here, :]
             state = entering_ref[n]
-            state_low = state.astype(bf16)
-            after_low = after.astype(bf16)
-            left = leave * mm(b_ref[here, :].astype(bf16), after_low)
+            left = leave * precise_mm(b_ref[here, :], after)
             scaled_grad = scaled_grad_ref[here, :] + left
             b_total[here, :] += precise_nt(scaled * leave, after)
             entered = out_grad * enter
             c_total[here, :] += precise_nt(entered, state)
-            came = rows_of(selector, entered * mm(c_ref[here, :].astype(bf16), state_low))
-            gone = rows_of(selector, scaled * left)
             kept = enter[CH - 1 : CH, :]
-            through = jnp.sum(rows_of(selector, kept * (state * after)), axis=1, keepdims=True)
-            log_rate_grad = rate_rows_ref[0, :, here] + times_mask(came, from_row) + times_mask(gone, before) + through
-            direct = rows_of(selector, conv * scaled_grad)
-            shifted = step_rows_ref[0, :, here]
-            step_grad = (direct + log_rate_grad * decay) * sigmoid(shifted)
-            step_grad_ref[0, :, here] = step_grad
-            log_total = log_total + jnp.sum(log_rate_grad * softplus(shifted), axis=1, keepdims=True) * decay
-            bias_total = bias_total + jnp.sum(step_grad, axis=1, keepdims=True)
+            through = jnp.sum(kept * (state * after), axis=0, keepdims=True)
+            came = entered * precise_mm(c_ref[here, :], state) + jnp.where(last_row, through, 0.0)
+            parts = [split(value) for value in (came, scaled * left, conv * scaled_grad)]
+            stacked = jnp.concatenate([high for high, _ in parts] + [low for _, low in parts], axis=1)
+            head_sums[here, :] += mm(stacked, selector)
             current[here, :] = rate * scaled_grad + skip_ref[...] * out_grad
             after = kept * after + pulled_ref[n]
-        log_grad_ref[0] = jnp.broadcast_to(log_total, (8, LANES))
-        bias_grad_ref[0] = jnp.broadcast_to(bias_total, (8, LANES))
 
     @pl.when(i == pairs)
     def _():
         current[...] = b_total[...]
+        r, c = iota2((CH, CH))
+        from_row = (r >= c).astype(bf16)
+        before = (r < c).astype(bf16)
+        totals = [(jnp.zeros((per, 1), f32), jnp.zeros((per, 1), f32)) for _ in range(pairs)]
+        for n in range(chunks):
+            here = pl.ds(n * CH, CH)
+            turned = head_sums[here, :].T
+            came, gone = times_mask(turned, from_row), times_mask(turned, before)
+            for j in range(pairs):
+                first = 8 * j
+                log_rate_grad = (
+                    rate_rows_ref[j, 0:per, here] + came[first : first + per] + gone[first + per : first + 2 * per]
+                )
+                direct = turned[first + 2 * per : first + 3 * per]
+                shifted = step_rows_ref[j, 0:per, here]
+                decay = decay_ref[j, 0:per, 0:1]
+                step_grad = (direct + log_rate_grad * decay) * sigmoid(shifted)
+                step_grad_ref[j, 0:per, here] = step_grad
+                log_total, bias_total = totals[j]
+                totals[j] = (
+                    log_total + jnp.sum(log_rate_grad * softplus(shifted), axis=1, keepdims=True) * decay,
+                    bias_total + jnp.sum(step_grad, axis=1, keepdims=True),
+                )
+        for j, (log_total, bias_total) in enumerate(totals):
+            log_grad_ref[j, 0:per, :] = jnp.broadcast_to(log_total, (per, LANES))
+            bias_grad_ref[j, 0:per, :] = jnp.broadcast_to(bias_total, (per, LANES))
 
     @pl.when(i == pairs + 1)
     def _():
@@ -581,14 +650,14 @@
 
     sums = [jnp.zeros((1, LANES), f32) for _ in range(KC + 1)]
     for start in range(0, rows, TILE):
-        value = conv_tile(padded, taps_ref, marks_ref, start, TILE)
+        value = conv_tile(padded, taps_ref, wide_marks, start, TILE)
         sig = sigmoid(value)
         grad = current[pl.ds(start, TILE), :] * (sig * (1.0 + value * (1.0 - sig)))
         conv_grad_ref[pl.ds(start, TILE), :] = grad
         for k in range(KC):
             shifted = padded[pl.ds(start + HALO - KC + 1 + k, TILE), :]
             if k < KC - 1:
-                shifted = shifted * marks_ref[start : start + TILE, M_FWD + k : M_FWD + k + 1]
+                shifted = shifted * wide_marks[k, pl.ds(start, TILE), :]
             sums[k] = sums[k] + jnp.sum(grad * shifted, axis=0, keepdims=True)
         sums[KC] = sums[KC] + jnp.sum(grad, axis=0, keepdims=True)
     taps_grad_ref[...] = jnp.concatenate(sums + [jnp.zeros((8 - KC - 1, LANES), f32)], axis=0)
@@ -606,8 +675,7 @@
     own = lambda i: jnp.minimum(i, pairs - 1)
     block = pl.BlockSpec((rows, LANES), lambda i: (0, own(i)))
     column = lambda i: (0, i)
-    heads = pl.BlockSpec((1, 8, rows), lambda i: (own(i), 0, 0))
-    few = pl.BlockSpec((1, 8, LANES), lambda i: (own(i), 0, 0))
+    heads, few = whole((pairs, 8, rows)), whole((pairs, 8, LANES))
     states = pl.BlockSpec((chunks, N, LANES), lambda i: (0, 0, own(i)))
     return call(
         partial(scan_backward_kernel, head_size, rows, pairs),
@@ -633,9 +701,11 @@
             pltpu.VMEM((rows, N), f32),
             pltpu.VMEM((rows, N), f32),
             pltpu.VMEM((rows, LANES), f32),
+            pltpu.VMEM((rows, LANES), f32),
+            pltpu.VMEM((KC - 1, rows, LANES), f32),
         ],
         compiler_params=params(),
-        cost_estimate=cost(16),
+        cost_estimate=cost(3),
         name="scan_backward",
     )(
         out_grad, scaled_grad, conv, conv, conv, cum, rate, rate_rows, step_rows, entering, pulled, after, skip, decay_rows,
@@ -645,7 +715,7 @@
 
 def conv_backward_kernel(
     rows, pairs, per, conv_grad_ref, next_ref, taps_ref, marks_ref, pre_ref, gate_dots_ref, step_grad_ref, step_rows_ref,
-    bias_ref, out_ref, map_grad_ref, dots_ref, padded,
+    bias_ref, out_ref, map_grad_ref, dots_ref, padded, products, wide_marks,
 ):
     i = pl.program_id(0)
     row = lax.broadcasted_iota(jnp.int32, (8, LANES), 0)
@@ -653,22 +723,23 @@
     @pl.when(i == 0)
     def _():
         dots_ref[...] = gate_dots_ref[...]
+        products[...] = jnp.zeros(products.shape, f32)
+        spread_marks(wide_marks, marks_ref, M_BWD)
 
     @pl.when(i > 0)
     def _():
         padded[pl.ds(0, rows), :] = conv_grad_ref[...]
         padded[pl.ds(rows, 8), :] = next_ref[...]
-        selector = (row == 0).astype(bf16)
         for start in range(0, rows, TILE):
             total = taps_ref[KC - 1 : KC, :] * padded[pl.ds(start, TILE), :]
             for k in range(KC - 1):
                 shifted = padded[pl.ds(start + KC - 1 - k, TILE), :]
                 total = total + taps_ref[k : k + 1, :] * (
-                    shifted * marks_ref[start : start + TILE, M_BWD + k : M_BWD + k + 1]
+                    shifted * wide_marks[k, pl.ds(start, TILE), :]
                 )
             out_ref[pl.ds(start, TILE), :] = total.astype(bf16)
             map_grad_ref[pl.ds(start, TILE), :] = total
-            dots_ref[:, pl.ds(start, TILE)] += rows_of(selector, total * pre_ref[pl.ds(start, TILE), :].astype(f32))
+            products[pl.ds(start, TILE), :] += total * pre_ref[pl.ds(start, TILE), :].astype(f32)
 
     @pl.when(i == 0)
     def _():
@@ -681,6 +752,10 @@
                 step_grad_ref[j, 0:per, :] * (step_rows_ref[j, 0:per, :] - bias_ref[j, 0:per, 0:1]), axis=0, keepdims=True
             )
         dots_ref[0:1, :] += total
+
+    @pl.when(i == pl.num_programs(0) - 1)
+    def _():
+        dots_ref[...] += rows_of((row == 0).astype(bf16), products[...])
 
 
 def conv_backward(conv_grad, next_grad, taps, marks, pre, gate_dots, step_grad, step_rows, bias_rows, head_size, held=()):
@@ -708,7 +783,9 @@
             jax.ShapeDtypeStruct((rows, 2 * N), f32),
             jax.ShapeDtypeStruct((8, rows), f32),
         ],
-        scratch_shapes=[pltpu.VMEM((rows + 8, LANES), f32)],
+        scratch_shapes=[
+            pltpu.VMEM((rows + 8, LANES), f32), pltpu.VMEM((rows, LANES), f32), pltpu.VMEM((KC - 1, rows, LANES), f32),
+        ],
         compiler_params=params(),
         cost_estimate=cost(6),
         name="conv_backward",
@@ -1616,6 +1693,8 @@
     def input_terms(layer):
         total = lax.dot_general(layer.gate_grad, layer.gate_weight, across, preferred_element_type=f32)
         total = total + lax.dot_general(layer.mix_grad, layer.mix, across, preferred_element_type=f32)
+        rest = (layer.map_grad - layer.mix_grad[:, LANES + inner :].astype(f32)).astype(bf16)
+        total = total + lax.dot_general(rest, layer.mix[:, LANES + inner :], across, preferred_element_type=f32)
         return blocks_of(total, bf16)
 
     def send_terms(layer, terms):
@@ -1682,11 +1761,11 @@
     crossed = sum_over_tensor(jnp.broadcast_to(crossed[None, :], (8, rows)))
     sums_first = jnp.concatenate([sums_first[:1], crossed[:1], sums_first[2:]], axis=0)
     gate_side(first, grad_first, sums_first, marks, channels)
-    outputs = lax.all_gather(ordered(output_pieces, first.out_grad), "tensor", axis=0, tiled=False)
+    outputs = with_partners(ordered(output_pieces, first.out_grad))
     rest_terms = []
 
     def after_scan(conv_grad):
-        rest_terms.append(rest_term(first, middle, conv_grad))
+        rest_terms.append(rest_term(first, middle, conv_grad, *outputs[1:]))
         return rest_terms
 
     scan_side(
@@ -1696,12 +1775,12 @@
     terms = input_terms(first)
     sent = send_terms(first, terms)
     share(first, first.dots)
-    last_block, norm_first = input_side(first, terms[0], sent, middle_block, (outputs,))
+    last_block, norm_first = input_side(first, terms[0], sent, middle_block)
     grad_pieces = to_owners([last_block, middle_block])
     grads = with_partners(grad_pieces)
     mix_sum_first = scatter_rows(mix_term(first, mix_start(first), rest_sum_first, grad_pieces))
     places = jnp.stack([tensor, ctx]).astype(jnp.int32)
-    outputs = join_gathered(places, outputs, bf16, (last_block,))
+    outputs = join_micro(places, outputs, bf16, (last_block,))
 
     rest_sum = own_layer([rest_sum_first, rest_sum_second], section).astype(f32)
     mix_sum = own_layer([mix_sum_first, mix_sum_second], section).astype(f32)

time: 661 us -> 650 us (0.983)
  Pallas kernels: 139 us -> 176 us
  waiting for transfers between devices: 175 us -> 143 us
  local copies, waits for them, and re-layouts: 119 us -> 87.8 us
  matrix products: 68.7 us -> 77 us
    unnamed x379 -> x211, local copies, waits for them, and re-layouts: 81.3 us -> 39.5 us
    pallas_call x19, Pallas kernels: 127 us -> 158 us  [call(): return lambda *args: made(*held, *args)]
    ppermute x8, waiting for transfers between devices: 27.4 us -> 10.2 us  [to_owners(): pieces.append(lax.ppermute(piece, ('section', 'ctx'), route))]
    ppermute x54 -> x57, waiting for transfers between devices: 111 us -> 102 us  [from_partner(): lax.ppermute(value, 'tensor', [(i, i ^ distance) for i in range(count)])]
    ppermute x54 -> x57, starting transfers between devices: 47.7 us -> 52.2 us  [from_partner(): lax.ppermute(value, 'tensor', [(i, i ^ distance) for i in range(count)])]
  transfers between devices with their start and end apart: 94 -> 96, of which waited for: 35 -> 30; matrix products, arithmetic and copies ran while one was open for 20% -> 24% of each run, Pallas kernels for 20% -> 25%
where the time goes in v2:
time: 650 us; the launch traced here: 637 us
  Pallas kernels  176 us (27%)
  waiting for transfers between devices  143 us (22%)
  starting transfers between devices  109 us (17%)
  local copies, waits for them, and re-layouts  87.8 us (14%)
  matrix products  77 us (12%)
  other arithmetic  28.9 us (4%)
  between operations  16.1 us (2%)
    pallas_call x19, Pallas kernels, call(): return lambda *args: made(*held, *args)  158 us
    ppermute x57, waiting for transfers between devices, from_partner(): lax.ppermute(value, 'tensor', [(i, i ^ distance) for i in range(count)])  102 us
    ppermute x57, starting transfers between devices, from_partner(): lax.ppermute(value, 'tensor', [(i, i ^ distance) for i in range(count)])  52.2 us
    unnamed x211, local copies, waits for them, and re-layouts  39.5 us
    ppermute x4, waiting for transfers between devices, to_micro(): came.append(lax.ppermute(piece, ('section', 'ctx'), route))  26.8 us
    ppermute x8, starting transfers between devices, to_owners(): pieces.append(lax.ppermute(piece, ('section', 'ctx'), route))  15.5 us
    ppermute x4, starting transfers between devices, to_micro(): came.append(lax.ppermute(piece, ('section', 'ctx'), route))  13.8 us
  transfers between devices with their start and end apart: 96, of which 30 were waited for; matrix products, arithmetic and copies ran while one was open for 24% of the time, Pallas kernels for 25%

profile of v2, /device:TPU:9, one launch (start us, length us, event | category | flops | bytes accessed | tf_op | source)
XLA Modules:
  0.0 637.3 jit_solution(11371198207037391528)
XLA Ops:
  24.4 14.5 %collective-permute-done.1 = bf16[256,384]{1,0:T(8,128)(2,1)S(1)} collective-permute-done((bf16[256,384]{1,0:T(8,128)(2,1)S(1)}, bf16[256,384]{1,0:T(8,128)(2,1)S(1)}, u32[]{:S(2)}, u32[]{:S(2)}) %collective-permute-start.1) | collective-permute-done | bytes 196640 | tf_op jit(solution)/shard_map/ppermute | solution.py:1467
  39.0 12.3 %collective-permute-done.2 = bf16[256,384]{1,0:T(8,128)(2,1)S(1)} collective-permute-done((bf16[256,384]{1,0:T(8,128)(2,1)S(1)}, bf16[256,384]{1,0:T(8,128)(2,1)S(1)}, u32[]{:S(2)}, u32[]{:S(2)}) %collective-permute-start.2) | collective-permute-done | bytes 196640 | tf_op jit(solution)/shard_map/ppermute | solution.py:1467
  58.7 7.3 %collective-permute-done.5.refs_5_ = bf16[512,384]{1,0:T(8,128)(2,1)S(1)} collective-permute-done((bf16[512,384]{1,0:T(8,128)(2,1)S(1)}, bf16[512,384]{1,0:T(8,128)(2,1)S(1)}, u32[]{:S(2)}, u32[]{:S(2)}) %collective-permute-start.5) | collective-permute-done | bytes 393248 | tf_op jit(solution)/shard_map/ppermute | solution.py:1439
  66.0 9.2 %collective-permute-done.4.refs_4_ = bf16[512,384]{1,0:T(8,128)(2,1)S(1)} collective-permute-done((bf16[512,384]{1,0:T(8,128)(2,1)S(1)}, bf16[512,384]{1,0:T(8,128)(2,1)S(1)}, u32[]{:S(2)}, u32[]{:S(2)}) %collective-permute-start.4) | collective-permute-done | bytes 393248 | tf_op jit(solution)/shard_map/ppermute | solution.py:1439
  95.3 16.1 %scan_forward.2 = (f32[512,1024]{1,0:T(8,128)}, f32[512,768]{1,0:T(8,128)}, f32[2,128,768]{2,1,0:T(8,128)}, f32[128,768]{1,0:T(8,128)}, f32[512,768]{1,0:T(8,128...) custom-call(bf16[512,1024]{1,0:T(8,128)(2,1)} %fusion.12.refs_0_.refs_1_.refs_16_.refs_7_, ...), custom_call_target="tpu_custom_call" | custom-call | bytes 45000000 | tf_op jit(solution)/shard_map/scan_forward/pallas_call | solution.py:219
  119.4 8.1 %gate_forward.2 = (f32[512,768]{1,0:T(8,128)}, f32[512,768]{1,0:T(8,128)}, f32[2,128,768]{2,1,0:T(8,128)}, f32[8,512]{1,0:T(8,128)}) custom-call(f32[512,768]{1,0:T(8,128)} %get-tuple-element.86.refs_0_, f32[512,1024]{1,0:T(8,128)} %get-tuple-element.87.refs_1_.refs_2_.refs_3_.refs_4_, f32[512,1024]{1,0:T(8,128)} %get-tuple-element.87.refs_1_.refs_2_.refs_3_.refs_4_, ...), custom_call_target="tpu_custom_call" | custom-call | bytes 18000000 | tf_op jit(solution)/shard_map/gate_forward/pallas_call | solution.py:219
  147.3 7.6 %collective-permute-start.22 = (bf16[256,384]{1,0:T(8,128)(2,1)S(1)}, bf16[256,384]{1,0:T(8,128)(2,1)S(1)}, u32[]{:S(2)}, u32[]{:S(2)}) collective-permute-start(bf16[256,384]{1,0:T(8,128)(2,1)S(1)} %get-tuple-element.237), channel_id=1, source_target_pairs={{0,4},{4,0},{8,20},{12,16},{16,12},{20,8},{24,28},{28,24},{1,5},{5... | collective-permute-start | bytes 589832 | tf_op jit(solution)/shard_map/ppermute | solution.py:1467
  156.9 16.4 %collective-permute-done.15 = f32[512,384]{1,0:T(8,128)S(1)} collective-permute-done((f32[512,384]{1,0:T(8,128)}, f32[512,384]{1,0:T(8,128)S(1)}, u32[]{:S(2)}, u32[]{:S(2)}) %collective-permute-start.15) | collective-permute-done | bytes 786464 | tf_op jit(solution)/shard_map/ppermute | solution.py:1439
  182.5 10.8 %collective-permute-done.17.refs_4_ = bf16[512,384]{1,0:T(8,128)(2,1)S(1)} collective-permute-done((bf16[512,384]{1,0:T(8,128)(2,1)S(1)}, bf16[512,384]{1,0:T(8,128)(2,1)S(1)}, u32[]{:S(2)}, u32[]{:S(2)}) %collective-permute-start.17) | collective-permute-done | bytes 393248 | tf_op jit(solution)/shard_map/ppermute | solution.py:1439
  199.0 5.2 fusion.15.refs_0_.refs_1_.refs_17_.refs_5_
  215.4 16.1 %scan_forward.3 = (f32[512,1024]{1,0:T(8,128)}, f32[512,768]{1,0:T(8,128)}, f32[2,128,768]{2,1,0:T(8,128)}, f32[128,768]{1,0:T(8,128)}, f32[512,768]{1,0:T(8,128...) custom-call(bf16[512,1024]{1,0:T(8,128)(2,1)} %fusion.15.refs_0_.refs_1_.refs_17_.refs_5_, ...), custom_call_target="tpu_custom_call" | custom-call | bytes 45000000 | tf_op jit(solution)/shard_map/scan_forward/pallas_call | solution.py:219
  243.4 8.7 %gate_forward.3 = (f32[512,768]{1,0:T(8,128)}, f32[512,768]{1,0:T(8,128)}, f32[2,128,768]{2,1,0:T(8,128)}, f32[8,512]{1,0:T(8,128)}) custom-call(f32[512,768]{1,0:T(8,128)} %get-tuple-element.94.refs_0_, f32[512,1024]{1,0:T(8,128)} %get-tuple-element.95.refs_1_.refs_2_.refs_4_.refs_5_.refs_3_, ...), custom_call_target="tpu_custom_call" | custom-call | bytes 18000000 | tf_op jit(solution)/shard_map/gate_forward/pallas_call | solution.py:219
  266.3 8.4 %gate_backward.2 = (f32[512,768]{1,0:T(8,128)}, bf16[512,768]{1,0:T(8,128)(2,1)}, f32[2,128,768]{2,1,0:T(8,128)}, f32[128,768]{1,0:T(8,128)}, f32[1,768]{1,0:T(1...) custom-call(bf16[512,1536]{1,0:T(8,128)(2,1)} %convolution_convert_fusion.6.refs_0_, f32[512,768]{1,0:T(8,128)} %fusion.6.refs_10_.refs_1_, ...), custom_call_target="tpu_custom_call" | custom-call | bytes 21000000 | tf_op jit(solution)/shard_map/gate_backward/pallas_call | solution.py:219
  283.7 5.1 collective-permute-start.29
  288.9 13.0 %intra_backward.2 = (f32[512,768]{1,0:T(8,128)}, f32[6,8,512]{2,1,0:T(8,128)}, f32[512,128]{1,0:T(8,128)}, f32[512,128]{1,0:T(8,128)}) custom-call(f32[512,768]{1,0:T(8,128)} %get-tuple-element.103.refs_0_.refs_1_, f32[512,1024]{1,0:T(8,128)} %get-tuple-element.95.refs_1_.refs_2_.refs_4_.refs_5_.refs_3_, ...), custom_call_target="tpu_custom_call" | custom-call | bytes 9000000 | tf_op jit(solution)/shard_map/intra_backward/pallas_call | solution.py:219
  302.7 14.0 %scan_backward.2 = (f32[512,1024]{1,0:T(8,128)}, f32[8,1024]{1,0:T(8,128)}, f32[6,8,512]{2,1,0:T(8,128)}, f32[6,8,128]{2,1,0:T(8,128)}, f32[6,8,128]{2,1,0:T(8,128)}) custom-call(bf16[1536,1536]{1,0:T(8,128)(2,1)} %pad_maximum_fusion.refs_0_, f32[512,768]{1,0:T(8,128)} %get-tuple-element.103.refs_0_.refs_1_, f32[512,768]{1,0:T(8,128)} %get-tuple-element.106.refs_2_, ...), custom_call_target="tpu_custom_call" | custom-call | bytes 9000000 | tf_op jit(solution)/shard_map/scan_backward/pallas_call | solution.py:219
  322.7 7.7 %conv_backward.2 = (bf16[512,1152]{1,0:T(8,128)(2,1)}, f32[512,256]{1,0:T(8,128)}, f32[8,512]{1,0:T(8,128)}) custom-call(bf16[512,384]{1,0:T(8,128)(2,1)} %copy.128.refs_0_, f32[512,1024]{1,0:T(8,128)} %get-tuple-element.114.refs_1_, f32[8,1024]{1,0:T(8,128)} %copy-done.64, f32[8,1024]{1,0:T(8,128)} %concatenate.90.refs_2_.refs_19_.refs_3_, ...), custom_call_target="tpu_custom_call" | custom-call | bytes 18000000 | tf_op jit(solution)/shard_map/conv_backward/pallas_call | solution.py:219
  347.6 5.4 convolution_convert_fusion.1.refs_0_.term_ref
  378.0 16.3 %collective-permute-done.49 = f32[128,256]{1,0:T(8,128)S(1)} collective-permute-done((f32[128,256]{1,0:T(8,128)}, f32[128,256]{1,0:T(8,128)S(1)}, u32[]{:S(2)}, u32[]{:S(2)}) %collective-permute-start.49) | collective-permute-done | bytes 131104 | tf_op jit(solution)/shard_map/ppermute | solution.py:1439
  394.3 5.2 collective-permute-done.48
  424.3 8.4 %gate_backward.3 = (f32[512,768]{1,0:T(8,128)}, bf16[512,768]{1,0:T(8,128)(2,1)}, f32[2,128,768]{2,1,0:T(8,128)}, f32[128,768]{1,0:T(8,128)}, f32[1,768]{1,0:T(1...) custom-call(f32[512,768]{1,0:T(8,128)} %get-tuple-element.307.refs_0_, f32[512,768]{1,0:T(8,128)} %fusion.70.refs_7_.refs_1_, ...), custom_call_target="tpu_custom_call" | custom-call | bytes 21000000 | tf_op jit(solution)/shard_map/gate_backward/pallas_call | solution.py:219
  435.5 5.8 collective-permute-start.53
  446.6 13.0 %intra_backward.3 = (f32[512,768]{1,0:T(8,128)}, f32[6,8,512]{2,1,0:T(8,128)}, f32[512,128]{1,0:T(8,128)}, f32[512,128]{1,0:T(8,128)}) custom-call(bf16[1536,1152]{1,0:T(8,128)(2,1)} %place_maps.2.refs_0_, f32[512,768]{1,0:T(8,128)} %get-tuple-element.124.refs_1_.refs_0_, f32[512,1024]{1,0:T(8,128)} %get-tuple-element.87.refs_1_.refs_2_.refs_3_.refs_4_, ...), custom_call_target="tpu_custom_call" | custom-call | bytes 9000000 | tf_op jit(solution)/shard_map/intra_backward/pallas_call | solution.py:219
  460.4 14.0 %scan_backward.3 = (f32[512,1024]{1,0:T(8,128)}, f32[8,1024]{1,0:T(8,128)}, f32[6,8,512]{2,1,0:T(8,128)}, f32[6,8,128]{2,1,0:T(8,128)}, f32[6,8,128]{2,1,0:T(8,128)}) custom-call(f32[512,768]{1,0:T(8,128)} %get-tuple-element.124.refs_1_.refs_0_, f32[512,768]{1,0:T(8,128)} %get-tuple-element.127.refs_1_, ...), custom_call_target="tpu_custom_call" | custom-call | bytes 9000000 | tf_op jit(solution)/shard_map/scan_backward/pallas_call | solution.py:219
  484.4 7.7 %conv_backward.3 = (bf16[512,1152]{1,0:T(8,128)(2,1)}, f32[512,256]{1,0:T(8,128)}, f32[8,512]{1,0:T(8,128)}) custom-call(bf16[192,1536]{1,0:T(8,128)(2,1)} %reduce-scatter.8.cloned.1.call-done.refs_1_.refs_0_, bf16[192,1152]{1,0:T(8,128)(2,1)} %reduce-scatter.10.cloned.1.call-done.refs_1_, bf16[1536,1536]{1,0:T(8,128)(2,1)} %pad_maximum_fusion.1.refs_2_, ...), custom_call_target="tpu_custom_call" | custom-call | bytes 18000000 | tf_op jit(solution)/shard_map/conv_backward/pallas_call | solution.py:219
  509.0 5.4 convolution_convert_fusion.term_ref
  520.3 6.3 collective-permute-done.63.refs_8_
  532.8 5.5 collective-permute-start.67
  543.9 6.2 collective-permute-done.66
  570.4 11.3 %collective-permute-done.68.refs_2_.refs_1_ = bf16[1024,384]{1,0:T(8,128)(2,1)S(1)} collective-permute-done((bf16[1024,384]{1,0:T(8,128)(2,1)S(1)}, bf16[1024,384]{1,0:T(8,128)(2,1)S(1)}, u32[]{:S(2)}, u32[]{:S(2)}) %collective-permute-start.68) | collective-permute-done | bytes 786464 | tf_op jit(solution)/shard_map/ppermute | solution.py:1439
  597.2 5.6 collective-permute-done.69.refs_3_
  602.8 5.8 join_micro.3
  (622 shorter events, 318.7 us)
Async XLA Ops:
  7.2 73.1 %all-gather.6.cloned.1.call-start = ((), (), s32[]{:S(2)}) async-start(), calls=%async_computation.5 | async-start | bytes 3981312 | tf_op jit(solution)/shard_map/all_gather | solution.py:1632
  18.2 96.3 %all-gather.8.cloned.1.call-start = ((), (), s32[]{:S(2)}) async-start(), calls=%async_computation.6 | async-start | bytes 2654208 | tf_op jit(solution)/shard_map/all_gather | solution.py:1632
  18.6 33.5 %collective-permute-start.9 = (bf16[192,1536]{1,0:T(8,128)(2,1)S(1)}, bf16[192,1536]{1,0:T(8,128)(2,1)S(1)}, u32[]{:S(2)}, u32[]{:S(2)}) collective-permute-start(bf16[192,1536]{1,0:T(8,128)(2,1)S(1)} %fusion.23), channel_id=1, source_target_pairs={{0,16},{16,0},{1,17},{17,1},{2,18},{18,2},{3,19},{19,3},{4,20},{20... | collective-permute-start | bytes 1769480 | tf_op jit(solution)/shard_map/ppermute | solution.py:1434
  24.4 26.9 %collective-permute-start.2 = (bf16[256,384]{1,0:T(8,128)(2,1)S(1)}, bf16[256,384]{1,0:T(8,128)(2,1)S(1)}, u32[]{:S(2)}, u32[]{:S(2)}) collective-permute-start(bf16[256,384]{1,0:T(8,128)(2,1)S(1)} %get-tuple-element.239), channel_id=1, source_target_pairs={{0,4},{4,0},{8,20},{12,16},{16,12},{20,8},{24,28},{28,24},{1,5},{5... | collective-permute-start | bytes 589832 | tf_op jit(solution)/shard_map/ppermute | solution.py:1467
  54.1 80.0 %all-gather.10.cloned.1.call-start = ((), (), s32[]{:S(2)}) async-start(), calls=%async_computation.7 | async-start | bytes 2654208 | tf_op jit(solution)/shard_map/all_gather | solution.py:1632
  80.3 118.7 %all-gather.12.cloned.1.call-start = ((), (), s32[]{:S(2)}) async-start(), calls=%async_computation.8 | async-start | bytes 3981312 | tf_op jit(solution)/shard_map/all_gather | solution.py:1632
  86.4 149.4 %all-gather.14.cloned.1.call-start = ((), (), s32[]{:S(2)}) async-start(), calls=%async_computation.9 | async-start | bytes 5308416 | tf_op jit(solution)/shard_map/all_gather | solution.py:1632
  111.5 208.6 %reduce-scatter.16.cloned.1.call-start = ((), (), s32[]{:S(2)}) async-start(), calls=%async_computation.14 | async-start | bytes 1966080
  140.5 32.7 %collective-permute-start.15 = (f32[512,384]{1,0:T(8,128)}, f32[512,384]{1,0:T(8,128)S(1)}, u32[]{:S(2)}, u32[]{:S(2)}) collective-permute-start(f32[512,384]{1,0:T(8,128)} %get-tuple-element.234), channel_id=1, source_target_pairs={{0,3},{1,2},{2,1},{3,0},{4,7},{5,6},{6,5},{7,4},{8,11},{9,10},{10,... | collective-permute-start | bytes 2359304 | tf_op jit(solution)/shard_map/ppermute | solution.py:1439
  141.5 31.7 %collective-permute-start.14 = (f32[512,384]{1,0:T(8,128)}, f32[512,384]{1,0:T(8,128)}, u32[]{:S(2)}, u32[]{:S(2)}) collective-permute-start(f32[512,384]{1,0:T(8,128)} %get-tuple-element.235), channel_id=1, source_target_pairs={{0,2},{1,3},{2,0},{3,1},{4,6},{5,7},{6,4},{7,5},{8,10},{9,11},{10,... | collective-permute-start | bytes 2359304 | tf_op jit(solution)/shard_map/ppermute | solution.py:1439
  145.4 35.8 %collective-permute-start.21 = (bf16[256,384]{1,0:T(8,128)(2,1)S(1)}, bf16[256,384]{1,0:T(8,128)(2,1)S(1)}, u32[]{:S(2)}, u32[]{:S(2)}) collective-permute-start(bf16[256,384]{1,0:T(8,128)(2,1)S(1)} %get-tuple-element.236), channel_id=1, source_target_pairs={{0,0},{4,4},{8,16},{12,20},{16,8},{20,12},{24,24},{28,28},{1,1},{5... | collective-permute-start | bytes 589832 | tf_op jit(solution)/shard_map/ppermute | solution.py:1467
  147.3 33.9 %collective-permute-start.22 = (bf16[256,384]{1,0:T(8,128)(2,1)S(1)}, bf16[256,384]{1,0:T(8,128)(2,1)S(1)}, u32[]{:S(2)}, u32[]{:S(2)}) collective-permute-start(bf16[256,384]{1,0:T(8,128)(2,1)S(1)} %get-tuple-element.237), channel_id=1, source_target_pairs={{0,4},{4,0},{8,20},{12,16},{16,12},{20,8},{24,28},{28,24},{1,5},{5... | collective-permute-start | bytes 589832 | tf_op jit(solution)/shard_map/ppermute | solution.py:1467
  204.1 29.2 %collective-permute-start.25 = (bf16[512,384]{1,0:T(8,128)(2,1)}, bf16[512,384]{1,0:T(8,128)(2,1)}, u32[]{:S(2)}, u32[]{:S(2)}) collective-permute-start(bf16[512,384]{1,0:T(8,128)(2,1)} %ordered.32.refs_1_), channel_id=1, source_target_pairs={{0,3},{1,2},{2,1},{3,0},{4,7},{5,6},{6,5},{7,4},{8,11},{9,10},{10,... | collective-permute-start | bytes 1179656 | tf_op jit(solution)/shard_map/ppermute | solution.py:1439
  206.0 27.4 %collective-permute-start.24 = (bf16[512,384]{1,0:T(8,128)(2,1)}, bf16[512,384]{1,0:T(8,128)(2,1)}, u32[]{:S(2)}, u32[]{:S(2)}) collective-permute-start(bf16[512,384]{1,0:T(8,128)(2,1)} %ordered.32.refs_1_), channel_id=1, source_target_pairs={{0,2},{1,3},{2,0},{3,1},{4,6},{5,7},{6,4},{7,5},{8,10},{9,11},{10,... | collective-permute-start | bytes 1179656 | tf_op jit(solution)/shard_map/ppermute | solution.py:1439
  207.9 25.4 %collective-permute-start.23 = (bf16[512,384]{1,0:T(8,128)(2,1)}, bf16[512,384]{1,0:T(8,128)(2,1)}, u32[]{:S(2)}, u32[]{:S(2)}) collective-permute-start(bf16[512,384]{1,0:T(8,128)(2,1)} %ordered.32.refs_1_), channel_id=1, source_target_pairs={{0,1},{1,0},{2,3},{3,2},{4,5},{5,4},{6,7},{7,6},{8,9},{9,8},{10,11... | collective-permute-start | bytes 1179656 | tf_op jit(solution)/shard_map/ppermute | solution.py:1439
  266.2 142.0 %reduce-scatter.8.cloned.1.call-start = ((), (), s32[]{:S(2)}) async-start(), calls=%async_computation.10 | async-start | bytes 5308416 | tf_op jit(solution)/shard_map/reduce_scatter | solution.py:1609
  283.6 200.1 %reduce-scatter.10.cloned.1.call-start = ((), (), s32[]{:S(2)}) async-start(), calls=%async_computation.11 | async-start | bytes 3981312 | tf_op jit(solution)/shard_map/reduce_scatter | solution.py:1609
  373.3 28.6 %collective-permute-start.43 = (bf16[512,384]{1,0:T(8,128)(2,1)}, bf16[512,384]{1,0:T(8,128)(2,1)S(1)}, u32[]{:S(2)}, u32[]{:S(2)}) collective-permute-start(bf16[512,384]{1,0:T(8,128)(2,1)} %get-tuple-element.121.refs_3_), channel_id=1, source_target_pairs={{0,3},{1,2},{2,1},{3,0},{4,7},{5,6},{6,5},{7,4},{8,11},{9,10},{10,... | collective-permute-start | bytes 1179656 | tf_op jit(solution)/shard_map/ppermute | solution.py:1439
  374.6 29.6 %collective-permute-start.42 = (bf16[512,384]{1,0:T(8,128)(2,1)}, bf16[512,384]{1,0:T(8,128)(2,1)S(1)}, u32[]{:S(2)}, u32[]{:S(2)}) collective-permute-start(bf16[512,384]{1,0:T(8,128)(2,1)} %get-tuple-element.121.refs_3_), channel_id=1, source_target_pairs={{0,2},{1,3},{2,0},{3,1},{4,6},{5,7},{6,4},{7,5},{8,10},{9,11},{10,... | collective-permute-start | bytes 1179656 | tf_op jit(solution)/shard_map/ppermute | solution.py:1439
  375.2 29.0 %collective-permute-start.41 = (bf16[512,384]{1,0:T(8,128)(2,1)}, bf16[512,384]{1,0:T(8,128)(2,1)S(1)}, u32[]{:S(2)}, u32[]{:S(2)}) collective-permute-start(bf16[512,384]{1,0:T(8,128)(2,1)} %get-tuple-element.121.refs_3_), channel_id=1, source_target_pairs={{0,1},{1,0},{2,3},{3,2},{4,5},{5,4},{6,7},{7,6},{8,9},{9,8},{10,11... | collective-permute-start | bytes 1179656 | tf_op jit(solution)/shard_map/ppermute | solution.py:1439
  377.2 22.3 %collective-permute-start.48 = (f32[128,256]{1,0:T(8,128)S(1)}, f32[128,256]{1,0:T(8,128)S(1)}, u32[]{:S(2)}, u32[]{:S(2)}) collective-permute-start(f32[128,256]{1,0:T(8,128)S(1)} %get-tuple-element.275), channel_id=1, source_target_pairs={{0,2},{1,3},{2,0},{3,1},{4,6},{5,7},{6,4},{7,5},{8,10},{9,11},{10,... | collective-permute-start | bytes 393224 | tf_op jit(solution)/shard_map/ppermute | solution.py:1439
  413.7 141.8 %reduce-scatter.12.cloned.1.call-start = ((), (), s32[]{:S(2)}) async-start(), calls=%async_computation.12 | async-start | bytes 5308416 | tf_op jit(solution)/shard_map/reduce_scatter | solution.py:1609
  432.8 41.7 %collective-permute-start.56 = (bf16[1024,384]{1,0:T(8,128)(2,1)}, bf16[1024,384]{1,0:T(8,128)(2,1)}, u32[]{:S(2)}, u32[]{:S(2)}) collective-permute-start(bf16[1024,384]{1,0:T(8,128)(2,1)} %ordered.43.refs_1_), channel_id=1, source_target_pairs={{0,3},{1,2},{2,1},{3,0},{4,7},{5,6},{6,5},{7,4},{8,11},{9,10},{10,... | collective-permute-start | bytes 2359304 | tf_op jit(solution)/shard_map/ppermute | solution.py:1439
  434.3 40.2 %collective-permute-start.55 = (bf16[1024,384]{1,0:T(8,128)(2,1)}, bf16[1024,384]{1,0:T(8,128)(2,1)}, u32[]{:S(2)}, u32[]{:S(2)}) collective-permute-start(bf16[1024,384]{1,0:T(8,128)(2,1)} %ordered.43.refs_1_), channel_id=1, source_target_pairs={{0,2},{1,3},{2,0},{3,1},{4,6},{5,7},{6,4},{7,5},{8,10},{9,11},{10,... | collective-permute-start | bytes 2359304 | tf_op jit(solution)/shard_map/ppermute | solution.py:1439
  435.3 39.2 %collective-permute-start.54 = (bf16[1024,384]{1,0:T(8,128)(2,1)}, bf16[1024,384]{1,0:T(8,128)(2,1)}, u32[]{:S(2)}, u32[]{:S(2)}) collective-permute-start(bf16[1024,384]{1,0:T(8,128)(2,1)} %ordered.43.refs_1_), channel_id=1, source_target_pairs={{0,1},{1,0},{2,3},{3,2},{4,5},{5,4},{6,7},{7,6},{8,9},{9,8},{10,11... | collective-permute-start | bytes 2359304 | tf_op jit(solution)/shard_map/ppermute | solution.py:1439
  435.5 24.1 %collective-permute-start.53 = (f32[128,768]{1,0:T(8,128)}, f32[128,768]{1,0:T(8,128)S(1)}, u32[]{:S(2)}, u32[]{:S(2)}) collective-permute-start(f32[128,768]{1,0:T(8,128)} %get-tuple-element.132), channel_id=1, source_target_pairs={{16,0},{17,1},{18,2},{19,3},{20,4},{21,5},{22,6},{23,7},{24,8},{25... | collective-permute-start | bytes 1179656 | tf_op jit(solution)/shard_map/ppermute | solution.py:1579
  479.8 140.1 %reduce-scatter.14.cloned.1.call-start = ((), (), s32[]{:S(2)}) async-start(), calls=%async_computation.13 | async-start | bytes 3981312 | tf_op jit(solution)/shard_map/reduce_scatter | solution.py:1609
  517.6 22.7 %collective-permute-start.79 = (f32[128,256]{1,0:T(8,128)S(1)}, f32[128,256]{1,0:T(8,128)S(1)}, u32[]{:S(2)}, u32[]{:S(2)}) collective-permute-start(f32[128,256]{1,0:T(8,128)S(1)} %get-tuple-element.270), channel_id=1, source_target_pairs={{0,1},{1,0},{2,3},{3,2},{4,5},{5,4},{6,7},{7,6},{8,9},{9,8},{10,11... | collective-permute-start | bytes 393224 | tf_op jit(solution)/shard_map/ppermute | solution.py:1439
  519.0 22.6 %collective-permute-start.81 = (f32[128,256]{1,0:T(8,128)S(1)}, f32[128,256]{1,0:T(8,128)S(1)}, u32[]{:S(2)}, u32[]{:S(2)}) collective-permute-start(f32[128,256]{1,0:T(8,128)S(1)} %get-tuple-element.271), channel_id=1, source_target_pairs={{0,3},{1,2},{2,1},{3,0},{4,7},{5,6},{6,5},{7,4},{8,11},{9,10},{10,... | collective-permute-start | bytes 393224 | tf_op jit(solution)/shard_map/ppermute | solution.py:1439
  566.0 31.1 %collective-permute-start.70 = (bf16[1024,384]{1,0:T(8,128)(2,1)S(1)}, bf16[1024,384]{1,0:T(8,128)(2,1)S(1)}, u32[]{:S(2)}, u32[]{:S(2)}) collective-permute-start(bf16[1024,384]{1,0:T(8,128)(2,1)S(1)} %copy-done.4), channel_id=1, source_target_pairs={{0,3},{1,2},{2,1},{3,0},{4,7},{5,6},{6,5},{7,4},{8,11},{9,10},{10,... | collective-permute-start | bytes 2359304 | tf_op jit(solution)/shard_map/ppermute | solution.py:1439
  567.3 35.5 %collective-permute-start.69 = (bf16[1024,384]{1,0:T(8,128)(2,1)S(1)}, bf16[1024,384]{1,0:T(8,128)(2,1)}, u32[]{:S(2)}, u32[]{:S(2)}) collective-permute-start(bf16[1024,384]{1,0:T(8,128)(2,1)S(1)} %copy-done.4), channel_id=1, source_target_pairs={{0,2},{1,3},{2,0},{3,1},{4,6},{5,7},{6,4},{7,5},{8,10},{9,11},{10,... | collective-permute-start | bytes 2359304 | tf_op jit(solution)/shard_map/ppermute | solution.py:1439
  584.8 23.9 %collective-permute-start.74 = (f32[16,1024]{1,0:T(8,128)S(1)}, f32[16,1024]{1,0:T(8,128)S(1)}, u32[]{:S(2)}, u32[]{:S(2)}) collective-permute-start(f32[16,1024]{1,0:T(8,128)S(1)} %select_add_fusion), channel_id=1, source_target_pairs={{0,12},{4,0},{8,4},{12,8},{1,13},{5,1},{9,5},{13,9},{2,14},{6,2},{... | collective-permute-start | bytes 196616 | tf_op jit(solution)/shard_map/ppermute | solution.py:1793
  (161 other events, 1156.3 us)
Sparse Core Ops, SparseCore 0:
  18.3 44.2 all-gather.5
  64.2 34.0 all-gather.7
  99.9 30.7 all-gather.9
  132.2 46.3 all-gather.11
  180.0 52.1 all-gather.13
  266.3 34.6 reduce-scatter.15
  303.9 53.6 reduce-scatter.7
  413.8 46.2 reduce-scatter.9
  479.9 56.0 reduce-scatter.11
  561.1 48.4 reduce-scatter.13

commit v3 on v2

--- a/solution.py
+++ b/solution.py
@@ -786,7 +786,7 @@
         scratch_shapes=[
             pltpu.VMEM((rows + 8, LANES), f32), pltpu.VMEM((rows, LANES), f32), pltpu.VMEM((KC - 1, rows, LANES), f32),
         ],
-        compiler_params=params(),
+        compiler_params=params(32 * 1024 * 1024),
         cost_estimate=cost(6),
         name="conv_backward",
     )(conv_grad, next_grad, taps, marks, pre, gate_dots, step_grad, step_rows, bias_rows)
@@ -812,7 +812,7 @@
         + [pl.BlockSpec((size, width), lambda i: (i + first_row // size, 0))] * count,
         out_specs=pl.BlockSpec((size, count * width), lambda i: (i, 0)),
         out_shape=jax.ShapeDtypeStruct((rows, count * width), dtype),
-        compiler_params=params(),
+        compiler_params=params(16 * 1024 * 1024),
         cost_estimate=cost(2),
         name="join",
     )(index, *blocks)
@@ -849,7 +849,7 @@
             jax.ShapeDtypeStruct((rows, count * width), bf16),
             jax.ShapeDtypeStruct((rows, LANES), f32),
         ],
-        compiler_params=params(),
+        compiler_params=params(16 * 1024 * 1024),
         cost_estimate=cost(3),
         name="join_norm",
     )(index, gain, *blocks)
@@ -892,7 +892,7 @@
         + [part] * len(sent),
         out_specs=[part, whole((1, cols))],
         out_shape=[jax.ShapeDtypeStruct((rows, cols), bf16), jax.ShapeDtypeStruct((1, cols), f32)],
-        compiler_params=params(),
+        compiler_params=params(16 * 1024 * 1024),
         cost_estimate=cost(3),
         name="input_gradient",
     )(own, dots, block, grad, scale, gain, *sent)
@@ -919,7 +919,7 @@
             out_specs=pl.BlockSpec((size, count * width), lambda i, places: (places[1] ^ i, 0)),
         ),
         out_shape=jax.ShapeDtypeStruct((rows, count * width), dtype),
-        compiler_params=params(),
+        compiler_params=params(16 * 1024 * 1024),
         cost_estimate=cost(5),
         name="join_micro",
     )(places, *held, *blocks)
@@ -972,7 +972,7 @@
         out_specs=pl.BlockSpec((depth, LANES), lambda i: (0, i + first_column // LANES)),
         out_shape=jax.ShapeDtypeStruct(term.shape, term.dtype),
         input_output_aliases={1: 0},
-        compiler_params=params(),
+        compiler_params=params(16 * 1024 * 1024),
         cost_estimate=cost(3),
         name="place_maps",
     )(index, term, normed, *pieces)

time: 650 us -> 638 us (0.982)
  Pallas kernels: 176 us -> 149 us
  local copies, waits for them, and re-layouts: 87.8 us -> 108 us
  matrix products: 77 us -> 69 us
    unnamed x211 -> x289, local copies, waits for them, and re-layouts: 39.5 us -> 62.1 us
    pallas_call x19, Pallas kernels: 158 us -> 135 us  [call(): return lambda *args: made(*held, *args)]
  transfers between devices with their start and end apart: 96 -> 96, of which waited for: 30 -> 33; matrix products, arithmetic and copies ran while one was open for 24% -> 22% of each run, Pallas kernels for 25% -> 22%
where the time goes in v3:
time: 638 us; the launch traced here: 627 us
  Pallas kernels  149 us (23%)
  waiting for transfers between devices  147 us (23%)
  starting transfers between devices  110 us (17%)
  local copies, waits for them, and re-layouts  108 us (17%)
  matrix products  69 us (11%)
  other arithmetic  27.9 us (4%)
  between operations  16.5 us (3%)
    pallas_call x19, Pallas kernels, call(): return lambda *args: made(*held, *args)  135 us
    ppermute x57, waiting for transfers between devices, from_partner(): lax.ppermute(value, 'tensor', [(i, i ^ distance) for i in range(count)])  97.6 us
    unnamed x289, local copies, waits for them, and re-layouts  62.1 us
    ppermute x57, starting transfers between devices, from_partner(): lax.ppermute(value, 'tensor', [(i, i ^ distance) for i in range(count)])  51 us
    ppermute x4, waiting for transfers between devices, to_micro(): came.append(lax.ppermute(piece, ('section', 'ctx'), route))  28 us
    ppermute x8, starting transfers between devices, to_owners(): pieces.append(lax.ppermute(piece, ('section', 'ctx'), route))  17.9 us
    ppermute x8, waiting for transfers between devices, to_owners(): pieces.append(lax.ppermute(piece, ('section', 'ctx'), route))  15.9 us
    ppermute x4, starting transfers between devices, to_micro(): came.append(lax.ppermute(piece, ('section', 'ctx'), route))  14.1 us
  transfers between devices with their start and end apart: 96, of which 33 were waited for; matrix products, arithmetic and copies ran while one was open for 22% of the time, Pallas kernels for 22%

profile of v3, /device:TPU:9, one launch (start us, length us, event | category | flops | bytes accessed | tf_op | source)
XLA Modules:
  0.0 627.2 jit_solution(5022067536707714133)
XLA Ops:
  24.4 14.5 %collective-permute-done.1 = bf16[256,384]{1,0:T(8,128)(2,1)S(1)} collective-permute-done((bf16[256,384]{1,0:T(8,128)(2,1)S(1)}, bf16[256,384]{1,0:T(8,128)(2,1)S(1)}, u32[]{:S(2)}, u32[]{:S(2)}) %collective-permute-start.1) | collective-permute-done | bytes 196640 | tf_op jit(solution)/shard_map/ppermute | solution.py:1467
  39.0 12.3 %collective-permute-done.2 = bf16[256,384]{1,0:T(8,128)(2,1)S(1)} collective-permute-done((bf16[256,384]{1,0:T(8,128)(2,1)S(1)}, bf16[256,384]{1,0:T(8,128)(2,1)S(1)}, u32[]{:S(2)}, u32[]{:S(2)}) %collective-permute-start.2) | collective-permute-done | bytes 196640 | tf_op jit(solution)/shard_map/ppermute | solution.py:1467
  57.6 8.5 %collective-permute-done.5.refs_5_ = bf16[512,384]{1,0:T(8,128)(2,1)S(1)} collective-permute-done((bf16[512,384]{1,0:T(8,128)(2,1)S(1)}, bf16[512,384]{1,0:T(8,128)(2,1)S(1)}, u32[]{:S(2)}, u32[]{:S(2)}) %collective-permute-start.5) | collective-permute-done | bytes 393248 | tf_op jit(solution)/shard_map/ppermute | solution.py:1439
  66.1 9.2 %collective-permute-done.4.refs_4_ = bf16[512,384]{1,0:T(8,128)(2,1)S(1)} collective-permute-done((bf16[512,384]{1,0:T(8,128)(2,1)S(1)}, bf16[512,384]{1,0:T(8,128)(2,1)S(1)}, u32[]{:S(2)}, u32[]{:S(2)}) %collective-permute-start.4) | collective-permute-done | bytes 393248 | tf_op jit(solution)/shard_map/ppermute | solution.py:1439
  79.6 4.7 fusion.12.refs_0_.refs_1_.refs_16_.refs_7_
  93.2 16.1 %scan_forward.2 = (f32[512,1024]{1,0:T(8,128)}, f32[512,768]{1,0:T(8,128)}, f32[2,128,768]{2,1,0:T(8,128)}, f32[128,768]{1,0:T(8,128)}, f32[512,768]{1,0:T(8,128...) custom-call(bf16[512,1024]{1,0:T(8,128)(2,1)} %fusion.12.refs_0_.refs_1_.refs_16_.refs_7_, ...), custom_call_target="tpu_custom_call" | custom-call | bytes 45000000 | tf_op jit(solution)/shard_map/scan_forward/pallas_call | solution.py:219
  117.3 8.2 %gate_forward.2 = (f32[512,768]{1,0:T(8,128)}, f32[512,768]{1,0:T(8,128)}, f32[2,128,768]{2,1,0:T(8,128)}, f32[8,512]{1,0:T(8,128)}) custom-call(f32[512,768]{1,0:T(8,128)} %get-tuple-element.86.refs_0_, f32[512,1024]{1,0:T(8,128)} %get-tuple-element.87.refs_1_.refs_2_.refs_3_.refs_4_, f32[512,1024]{1,0:T(8,128)} %get-tuple-element.87.refs_1_.refs_2_.refs_3_.refs_4_, ...), custom_call_target="tpu_custom_call" | custom-call | bytes 18000000 | tf_op jit(solution)/shard_map/gate_forward/pallas_call | solution.py:219
  145.4 6.8 %collective-permute-start.22 = (bf16[256,384]{1,0:T(8,128)(2,1)S(1)}, bf16[256,384]{1,0:T(8,128)(2,1)S(1)}, u32[]{:S(2)}, u32[]{:S(2)}) collective-permute-start(bf16[256,384]{1,0:T(8,128)(2,1)S(1)} %get-tuple-element.237), channel_id=1, source_target_pairs={{0,4},{4,0},{8,20},{12,16},{16,12},{20,8},{24,28},{28,24},{1,5},{5... | collective-permute-start | bytes 589832 | tf_op jit(solution)/shard_map/ppermute | solution.py:1467
  154.0 17.2 %collective-permute-done.15 = f32[512,384]{1,0:T(8,128)} collective-permute-done((f32[512,384]{1,0:T(8,128)}, f32[512,384]{1,0:T(8,128)}, u32[]{:S(2)}, u32[]{:S(2)}) %collective-permute-start.15) | collective-permute-done | bytes 786464 | tf_op jit(solution)/shard_map/ppermute | solution.py:1439
  180.7 10.9 %collective-permute-done.17.refs_4_ = bf16[512,384]{1,0:T(8,128)(2,1)S(1)} collective-permute-done((bf16[512,384]{1,0:T(8,128)(2,1)S(1)}, bf16[512,384]{1,0:T(8,128)(2,1)S(1)}, u32[]{:S(2)}, u32[]{:S(2)}) %collective-permute-start.17) | collective-permute-done | bytes 393248 | tf_op jit(solution)/shard_map/ppermute | solution.py:1439
  193.4 5.2 fusion.15.refs_0_.refs_1_.refs_17_.refs_5_
  210.6 16.0 %scan_forward.3 = (f32[512,1024]{1,0:T(8,128)}, f32[512,768]{1,0:T(8,128)}, f32[2,128,768]{2,1,0:T(8,128)}, f32[128,768]{1,0:T(8,128)}, f32[512,768]{1,0:T(8,128...) custom-call(bf16[512,1024]{1,0:T(8,128)(2,1)} %fusion.15.refs_0_.refs_1_.refs_17_.refs_5_, ...), custom_call_target="tpu_custom_call" | custom-call | bytes 45000000 | tf_op jit(solution)/shard_map/scan_forward/pallas_call | solution.py:219
  239.2 8.7 %gate_forward.3 = (f32[512,768]{1,0:T(8,128)}, f32[512,768]{1,0:T(8,128)}, f32[2,128,768]{2,1,0:T(8,128)}, f32[8,512]{1,0:T(8,128)}) custom-call(f32[512,768]{1,0:T(8,128)} %get-tuple-element.94.refs_0_, f32[512,1024]{1,0:T(8,128)} %get-tuple-element.95.refs_1_.refs_2_.refs_4_.refs_5_.refs_3_, ...), custom_call_target="tpu_custom_call" | custom-call | bytes 18000000 | tf_op jit(solution)/shard_map/gate_forward/pallas_call | solution.py:219
  254.9 4.7 convolution_convert_fusion.6.refs_0_
  262.3 8.5 %gate_backward.2 = (f32[512,768]{1,0:T(8,128)}, bf16[512,768]{1,0:T(8,128)(2,1)}, f32[2,128,768]{2,1,0:T(8,128)}, f32[128,768]{1,0:T(8,128)}, f32[1,768]{1,0:T(1...) custom-call(bf16[512,1536]{1,0:T(8,128)(2,1)} %convolution_convert_fusion.6.refs_0_, f32[512,768]{1,0:T(8,128)} %fusion.6.refs_10_.refs_1_, ...), custom_call_target="tpu_custom_call" | custom-call | bytes 21000000 | tf_op jit(solution)/shard_map/gate_backward/pallas_call | solution.py:219
  285.5 13.0 %intra_backward.2 = (f32[512,768]{1,0:T(8,128)}, f32[6,8,512]{2,1,0:T(8,128)}, f32[512,128]{1,0:T(8,128)}, f32[512,128]{1,0:T(8,128)}) custom-call(f32[512,768]{1,0:T(8,128)} %get-tuple-element.103.refs_0_.refs_1_, f32[512,1024]{1,0:T(8,128)} %get-tuple-element.95.refs_1_.refs_2_.refs_4_.refs_5_.refs_3_, ...), custom_call_target="tpu_custom_call" | custom-call | bytes 9000000 | tf_op jit(solution)/shard_map/intra_backward/pallas_call | solution.py:219
  299.4 14.1 %scan_backward.2 = (f32[512,1024]{1,0:T(8,128)}, f32[8,1024]{1,0:T(8,128)}, f32[6,8,512]{2,1,0:T(8,128)}, f32[6,8,128]{2,1,0:T(8,128)}, f32[6,8,128]{2,1,0:T(8,128)}) custom-call(bf16[1536,1536]{1,0:T(8,128)(2,1)} %pad_maximum_fusion.refs_0_, f32[512,768]{1,0:T(8,128)} %get-tuple-element.103.refs_0_.refs_1_, f32[512,768]{1,0:T(8,128)} %get-tuple-element.106.refs_2_, ...), custom_call_target="tpu_custom_call" | custom-call | bytes 9000000 | tf_op jit(solution)/shard_map/scan_backward/pallas_call | solution.py:219
  337.6 5.3 convolution_convert_fusion.1.refs_0_.term_ref
  371.8 10.9 %collective-permute-done.49 = f32[128,256]{1,0:T(8,128)S(1)} collective-permute-done((f32[128,256]{1,0:T(8,128)S(1)}, f32[128,256]{1,0:T(8,128)S(1)}, u32[]{:S(2)}, u32[]{:S(2)}) %collective-permute-start.49) | collective-permute-done | bytes 131104 | tf_op jit(solution)/shard_map/ppermute | solution.py:1439
  399.8 4.6 multiply_reduce_fusion
  410.6 8.4 %gate_backward.3 = (f32[512,768]{1,0:T(8,128)}, bf16[512,768]{1,0:T(8,128)(2,1)}, f32[2,128,768]{2,1,0:T(8,128)}, f32[128,768]{1,0:T(8,128)}, f32[1,768]{1,0:T(1...) custom-call(f32[512,768]{1,0:T(8,128)} %get-tuple-element.307.refs_0_, f32[512,768]{1,0:T(8,128)} %fusion.70.refs_7_.refs_1_, ...), custom_call_target="tpu_custom_call" | custom-call | bytes 21000000 | tf_op jit(solution)/shard_map/gate_backward/pallas_call | solution.py:219
  421.8 4.9 collective-permute-start.53
  432.1 13.0 %intra_backward.3 = (f32[512,768]{1,0:T(8,128)}, f32[6,8,512]{2,1,0:T(8,128)}, f32[512,128]{1,0:T(8,128)}, f32[512,128]{1,0:T(8,128)}) custom-call(bf16[1536,1152]{1,0:T(8,128)(2,1)} %place_maps.2.refs_0_, f32[512,768]{1,0:T(8,128)} %get-tuple-element.124.refs_1_.refs_0_, f32[512,1024]{1,0:T(8,128)} %get-tuple-element.87.refs_1_.refs_2_.refs_3_.refs_4_, ...), custom_call_target="tpu_custom_call" | custom-call | bytes 9000000 | tf_op jit(solution)/shard_map/intra_backward/pallas_call | solution.py:219
  445.9 14.0 %scan_backward.3 = (f32[512,1024]{1,0:T(8,128)}, f32[8,1024]{1,0:T(8,128)}, f32[6,8,512]{2,1,0:T(8,128)}, f32[6,8,128]{2,1,0:T(8,128)}, f32[6,8,128]{2,1,0:T(8,128)}) custom-call(f32[512,768]{1,0:T(8,128)} %get-tuple-element.124.refs_1_.refs_0_, f32[512,768]{1,0:T(8,128)} %get-tuple-element.127.refs_1_, ...), custom_call_target="tpu_custom_call" | custom-call | bytes 9000000 | tf_op jit(solution)/shard_map/scan_backward/pallas_call | solution.py:219
  495.3 5.3 convolution_convert_fusion.term_ref
  507.3 5.2 collective-permute-done.63.refs_8_
  518.4 4.8 collective-permute-start.67
  530.1 6.1 collective-permute-done.66
  560.5 11.3 %collective-permute-done.68.refs_2_.refs_1_ = bf16[1024,384]{1,0:T(8,128)(2,1)S(1)} collective-permute-done((bf16[1024,384]{1,0:T(8,128)(2,1)S(1)}, bf16[1024,384]{1,0:T(8,128)(2,1)S(1)}, u32[]{:S(2)}, u32[]{:S(2)}) %collective-permute-start.68) | collective-permute-done | bytes 786464 | tf_op jit(solution)/shard_map/ppermute | solution.py:1439
  580.0 4.7 join_micro.2.refs_0_
  588.3 5.0 collective-permute-done.69.refs_3_
  595.2 5.3 join_micro.3
  (700 shorter events, 323.1 us)
Async XLA Ops:
  7.2 71.1 %all-gather.6.cloned.1.call-start = ((), (), s32[]{:S(2)}) async-start(), calls=%async_computation.5 | async-start | bytes 3981312 | tf_op jit(solution)/shard_map/all_gather | solution.py:1632
  18.2 94.2 %all-gather.8.cloned.1.call-start = ((), (), s32[]{:S(2)}) async-start(), calls=%async_computation.6 | async-start | bytes 2654208 | tf_op jit(solution)/shard_map/all_gather | solution.py:1632
  18.6 33.5 %collective-permute-start.9 = (bf16[192,1536]{1,0:T(8,128)(2,1)S(1)}, bf16[192,1536]{1,0:T(8,128)(2,1)S(1)}, u32[]{:S(2)}, u32[]{:S(2)}) collective-permute-start(bf16[192,1536]{1,0:T(8,128)(2,1)S(1)} %fusion.23), channel_id=1, source_target_pairs={{0,16},{16,0},{1,17},{17,1},{2,18},{18,2},{3,19},{19,3},{4,20},{20... | collective-permute-start | bytes 1769480 | tf_op jit(solution)/shard_map/ppermute | solution.py:1434
  24.4 26.9 %collective-permute-start.2 = (bf16[256,384]{1,0:T(8,128)(2,1)S(1)}, bf16[256,384]{1,0:T(8,128)(2,1)S(1)}, u32[]{:S(2)}, u32[]{:S(2)}) collective-permute-start(bf16[256,384]{1,0:T(8,128)(2,1)S(1)} %get-tuple-element.239), channel_id=1, source_target_pairs={{0,4},{4,0},{8,20},{12,16},{16,12},{20,8},{24,28},{28,24},{1,5},{5... | collective-permute-start | bytes 589832 | tf_op jit(solution)/shard_map/ppermute | solution.py:1467
  54.1 77.5 %all-gather.10.cloned.1.call-start = ((), (), s32[]{:S(2)}) async-start(), calls=%async_computation.7 | async-start | bytes 2654208 | tf_op jit(solution)/shard_map/all_gather | solution.py:1632
  78.2 115.2 %all-gather.12.cloned.1.call-start = ((), (), s32[]{:S(2)}) async-start(), calls=%async_computation.8 | async-start | bytes 3981312 | tf_op jit(solution)/shard_map/all_gather | solution.py:1632
  84.3 148.0 %all-gather.14.cloned.1.call-start = ((), (), s32[]{:S(2)}) async-start(), calls=%async_computation.9 | async-start | bytes 5308416 | tf_op jit(solution)/shard_map/all_gather | solution.py:1632
  109.4 207.7 %reduce-scatter.16.cloned.1.call-start = ((), (), s32[]{:S(2)}) async-start(), calls=%async_computation.14 | async-start | bytes 1966080
  138.4 32.8 %collective-permute-start.15 = (f32[512,384]{1,0:T(8,128)}, f32[512,384]{1,0:T(8,128)}, u32[]{:S(2)}, u32[]{:S(2)}) collective-permute-start(f32[512,384]{1,0:T(8,128)} %get-tuple-element.234), channel_id=1, source_target_pairs={{0,3},{1,2},{2,1},{3,0},{4,7},{5,6},{6,5},{7,4},{8,11},{9,10},{10,... | collective-permute-start | bytes 2359304 | tf_op jit(solution)/shard_map/ppermute | solution.py:1439
  139.3 31.9 %collective-permute-start.14 = (f32[512,384]{1,0:T(8,128)}, f32[512,384]{1,0:T(8,128)}, u32[]{:S(2)}, u32[]{:S(2)}) collective-permute-start(f32[512,384]{1,0:T(8,128)} %get-tuple-element.235), channel_id=1, source_target_pairs={{0,2},{1,3},{2,0},{3,1},{4,6},{5,7},{6,4},{7,5},{8,10},{9,11},{10,... | collective-permute-start | bytes 2359304 | tf_op jit(solution)/shard_map/ppermute | solution.py:1439
  142.3 34.9 %collective-permute-start.21 = (bf16[256,384]{1,0:T(8,128)(2,1)S(1)}, bf16[256,384]{1,0:T(8,128)(2,1)S(1)}, u32[]{:S(2)}, u32[]{:S(2)}) collective-permute-start(bf16[256,384]{1,0:T(8,128)(2,1)S(1)} %get-tuple-element.236), channel_id=1, source_target_pairs={{0,0},{4,4},{8,16},{12,20},{16,8},{20,12},{24,24},{28,28},{1,1},{5... | collective-permute-start | bytes 589832 | tf_op jit(solution)/shard_map/ppermute | solution.py:1467
  145.4 33.0 %collective-permute-start.22 = (bf16[256,384]{1,0:T(8,128)(2,1)S(1)}, bf16[256,384]{1,0:T(8,128)(2,1)S(1)}, u32[]{:S(2)}, u32[]{:S(2)}) collective-permute-start(bf16[256,384]{1,0:T(8,128)(2,1)S(1)} %get-tuple-element.237), channel_id=1, source_target_pairs={{0,4},{4,0},{8,20},{12,16},{16,12},{20,8},{24,28},{28,24},{1,5},{5... | collective-permute-start | bytes 589832 | tf_op jit(solution)/shard_map/ppermute | solution.py:1467
  198.7 29.8 %collective-permute-start.25 = (bf16[512,384]{1,0:T(8,128)(2,1)}, bf16[512,384]{1,0:T(8,128)(2,1)}, u32[]{:S(2)}, u32[]{:S(2)}) collective-permute-start(bf16[512,384]{1,0:T(8,128)(2,1)} %ordered.32.refs_1_), channel_id=1, source_target_pairs={{0,3},{1,2},{2,1},{3,0},{4,7},{5,6},{6,5},{7,4},{8,11},{9,10},{10,... | collective-permute-start | bytes 1179656 | tf_op jit(solution)/shard_map/ppermute | solution.py:1439
  200.4 28.1 %collective-permute-start.24 = (bf16[512,384]{1,0:T(8,128)(2,1)}, bf16[512,384]{1,0:T(8,128)(2,1)}, u32[]{:S(2)}, u32[]{:S(2)}) collective-permute-start(bf16[512,384]{1,0:T(8,128)(2,1)} %ordered.32.refs_1_), channel_id=1, source_target_pairs={{0,2},{1,3},{2,0},{3,1},{4,6},{5,7},{6,4},{7,5},{8,10},{9,11},{10,... | collective-permute-start | bytes 1179656 | tf_op jit(solution)/shard_map/ppermute | solution.py:1439
  201.1 27.4 %collective-permute-start.23 = (bf16[512,384]{1,0:T(8,128)(2,1)}, bf16[512,384]{1,0:T(8,128)(2,1)}, u32[]{:S(2)}, u32[]{:S(2)}) collective-permute-start(bf16[512,384]{1,0:T(8,128)(2,1)} %ordered.32.refs_1_), channel_id=1, source_target_pairs={{0,1},{1,0},{2,3},{3,2},{4,5},{5,4},{6,7},{7,6},{8,9},{9,8},{10,11... | collective-permute-start | bytes 1179656 | tf_op jit(solution)/shard_map/ppermute | solution.py:1439
  262.2 129.9 %reduce-scatter.8.cloned.1.call-start = ((), (), s32[]{:S(2)}) async-start(), calls=%async_computation.10 | async-start | bytes 5308416 | tf_op jit(solution)/shard_map/reduce_scatter | solution.py:1609
  279.8 192.6 %reduce-scatter.10.cloned.1.call-start = ((), (), s32[]{:S(2)}) async-start(), calls=%async_computation.11 | async-start | bytes 3981312 | tf_op jit(solution)/shard_map/reduce_scatter | solution.py:1609
  360.2 29.6 %collective-permute-start.43 = (bf16[512,384]{1,0:T(8,128)(2,1)S(1)}, bf16[512,384]{1,0:T(8,128)(2,1)S(1)}, u32[]{:S(2)}, u32[]{:S(2)}) collective-permute-start(bf16[512,384]{1,0:T(8,128)(2,1)S(1)} %get-tuple-element.121.refs_3_), channel_id=1, source_target_pairs={{0,3},{1,2},{2,1},{3,0},{4,7},{5,6},{6,5},{7,4},{8,11},{9,10},{10,... | collective-permute-start | bytes 1179656 | tf_op jit(solution)/shard_map/ppermute | solution.py:1439
  363.5 26.6 %collective-permute-start.42 = (bf16[512,384]{1,0:T(8,128)(2,1)S(1)}, bf16[512,384]{1,0:T(8,128)(2,1)S(1)}, u32[]{:S(2)}, u32[]{:S(2)}) collective-permute-start(bf16[512,384]{1,0:T(8,128)(2,1)S(1)} %get-tuple-element.121.refs_3_), channel_id=1, source_target_pairs={{0,2},{1,3},{2,0},{3,1},{4,6},{5,7},{6,4},{7,5},{8,10},{9,11},{10,... | collective-permute-start | bytes 1179656 | tf_op jit(solution)/shard_map/ppermute | solution.py:1439
  367.8 22.3 %collective-permute-start.41 = (bf16[512,384]{1,0:T(8,128)(2,1)S(1)}, bf16[512,384]{1,0:T(8,128)(2,1)S(1)}, u32[]{:S(2)}, u32[]{:S(2)}) collective-permute-start(bf16[512,384]{1,0:T(8,128)(2,1)S(1)} %get-tuple-element.121.refs_3_), channel_id=1, source_target_pairs={{0,1},{1,0},{2,3},{3,2},{4,5},{5,4},{6,7},{7,6},{8,9},{9,8},{10,11... | collective-permute-start | bytes 1179656 | tf_op jit(solution)/shard_map/ppermute | solution.py:1439
  398.4 143.5 %reduce-scatter.12.cloned.1.call-start = ((), (), s32[]{:S(2)}) async-start(), calls=%async_computation.12 | async-start | bytes 5308416 | tf_op jit(solution)/shard_map/reduce_scatter | solution.py:1609
  419.1 40.9 %collective-permute-start.56 = (bf16[1024,384]{1,0:T(8,128)(2,1)}, bf16[1024,384]{1,0:T(8,128)(2,1)}, u32[]{:S(2)}, u32[]{:S(2)}) collective-permute-start(bf16[1024,384]{1,0:T(8,128)(2,1)} %ordered.43.refs_1_), channel_id=1, source_target_pairs={{0,3},{1,2},{2,1},{3,0},{4,7},{5,6},{6,5},{7,4},{8,11},{9,10},{10,... | collective-permute-start | bytes 2359304 | tf_op jit(solution)/shard_map/ppermute | solution.py:1439
  420.2 39.8 %collective-permute-start.55 = (bf16[1024,384]{1,0:T(8,128)(2,1)}, bf16[1024,384]{1,0:T(8,128)(2,1)}, u32[]{:S(2)}, u32[]{:S(2)}) collective-permute-start(bf16[1024,384]{1,0:T(8,128)(2,1)} %ordered.43.refs_1_), channel_id=1, source_target_pairs={{0,2},{1,3},{2,0},{3,1},{4,6},{5,7},{6,4},{7,5},{8,10},{9,11},{10,... | collective-permute-start | bytes 2359304 | tf_op jit(solution)/shard_map/ppermute | solution.py:1439
  420.3 39.7 %collective-permute-start.54 = (bf16[1024,384]{1,0:T(8,128)(2,1)}, bf16[1024,384]{1,0:T(8,128)(2,1)}, u32[]{:S(2)}, u32[]{:S(2)}) collective-permute-start(bf16[1024,384]{1,0:T(8,128)(2,1)} %ordered.43.refs_1_), channel_id=1, source_target_pairs={{0,1},{1,0},{2,3},{3,2},{4,5},{5,4},{6,7},{7,6},{8,9},{9,8},{10,11... | collective-permute-start | bytes 2359304 | tf_op jit(solution)/shard_map/ppermute | solution.py:1439
  421.8 23.3 %collective-permute-start.53 = (f32[128,768]{1,0:T(8,128)}, f32[128,768]{1,0:T(8,128)S(1)}, u32[]{:S(2)}, u32[]{:S(2)}) collective-permute-start(f32[128,768]{1,0:T(8,128)} %get-tuple-element.132), channel_id=1, source_target_pairs={{16,0},{17,1},{18,2},{19,3},{20,4},{21,5},{22,6},{23,7},{24,8},{25... | collective-permute-start | bytes 1179656 | tf_op jit(solution)/shard_map/ppermute | solution.py:1579
  465.3 143.4 %reduce-scatter.14.cloned.1.call-start = ((), (), s32[]{:S(2)}) async-start(), calls=%async_computation.13 | async-start | bytes 3981312 | tf_op jit(solution)/shard_map/reduce_scatter | solution.py:1609
  503.8 22.9 %collective-permute-start.79 = (f32[128,256]{1,0:T(8,128)S(1)}, f32[128,256]{1,0:T(8,128)S(1)}, u32[]{:S(2)}, u32[]{:S(2)}) collective-permute-start(f32[128,256]{1,0:T(8,128)S(1)} %get-tuple-element.270), channel_id=1, source_target_pairs={{0,1},{1,0},{2,3},{3,2},{4,5},{5,4},{6,7},{7,6},{8,9},{9,8},{10,11... | collective-permute-start | bytes 393224 | tf_op jit(solution)/shard_map/ppermute | solution.py:1439
  504.2 22.7 %collective-permute-start.81 = (f32[128,256]{1,0:T(8,128)S(1)}, f32[128,256]{1,0:T(8,128)S(1)}, u32[]{:S(2)}, u32[]{:S(2)}) collective-permute-start(f32[128,256]{1,0:T(8,128)S(1)} %get-tuple-element.271), channel_id=1, source_target_pairs={{0,3},{1,2},{2,1},{3,0},{4,7},{5,6},{6,5},{7,4},{8,11},{9,10},{10,... | collective-permute-start | bytes 393224 | tf_op jit(solution)/shard_map/ppermute | solution.py:1439
  555.9 32.4 %collective-permute-start.70 = (bf16[1024,384]{1,0:T(8,128)(2,1)S(1)}, bf16[1024,384]{1,0:T(8,128)(2,1)}, u32[]{:S(2)}, u32[]{:S(2)}) collective-permute-start(bf16[1024,384]{1,0:T(8,128)(2,1)S(1)} %copy-done.8), channel_id=1, source_target_pairs={{0,3},{1,2},{2,1},{3,0},{4,7},{5,6},{6,5},{7,4},{8,11},{9,10},{10,... | collective-permute-start | bytes 2359304 | tf_op jit(solution)/shard_map/ppermute | solution.py:1439
  557.0 36.3 %collective-permute-start.69 = (bf16[1024,384]{1,0:T(8,128)(2,1)S(1)}, bf16[1024,384]{1,0:T(8,128)(2,1)}, u32[]{:S(2)}, u32[]{:S(2)}) collective-permute-start(bf16[1024,384]{1,0:T(8,128)(2,1)S(1)} %copy-done.8), channel_id=1, source_target_pairs={{0,2},{1,3},{2,0},{3,1},{4,6},{5,7},{6,4},{7,5},{8,10},{9,11},{10,... | collective-permute-start | bytes 2359304 | tf_op jit(solution)/shard_map/ppermute | solution.py:1439
  574.8 25.7 %collective-permute-start.74 = (f32[16,1024]{1,0:T(8,128)S(1)}, f32[16,1024]{1,0:T(8,128)S(1)}, u32[]{:S(2)}, u32[]{:S(2)}) collective-permute-start(f32[16,1024]{1,0:T(8,128)S(1)} %select_add_fusion), channel_id=1, source_target_pairs={{0,12},{4,0},{8,4},{12,8},{1,13},{5,1},{9,5},{13,9},{2,14},{6,2},{... | collective-permute-start | bytes 196616 | tf_op jit(solution)/shard_map/ppermute | solution.py:1793
  578.5 22.1 %collective-permute-start.72 = (f32[16,1024]{1,0:T(8,128)S(1)}, f32[16,1024]{1,0:T(8,128)S(1)}, u32[]{:S(2)}, u32[]{:S(2)}) collective-permute-start(f32[16,1024]{1,0:T(8,128)S(1)} %select_add_fusion), channel_id=1, source_target_pairs={{0,4},{4,8},{8,12},{12,0},{1,5},{5,9},{9,13},{13,1},{2,6},{6,10},{... | collective-permute-start | bytes 196616 | tf_op jit(solution)/shard_map/ppermute | solution.py:1793
  (200 other events, 1599.9 us)
Sparse Core Ops, SparseCore 0:
  18.3 44.2 all-gather.5
  64.2 34.0 all-gather.7
  99.9 30.7 all-gather.9
  132.2 46.3 all-gather.11
  180.1 52.1 all-gather.13
  262.3 34.8 reduce-scatter.15
  300.1 54.4 reduce-scatter.7
  398.5 46.5 reduce-scatter.9
  465.4 55.8 reduce-scatter.11
  551.2 48.2 reduce-scatter.13

commit v4 on v3

--- a/solution.py
+++ b/solution.py
@@ -381,7 +381,7 @@
             jax.ShapeDtypeStruct((8, rows), f32),
         ],
         scratch_shapes=[pltpu.VMEM((rows, 6 * N), bf16)] + [pltpu.VMEM((rows, LANES), f32)] * (1 if grad is None else 2),
-        compiler_params=params(),
+        compiler_params=params(48 * 1024 * 1024),
         cost_estimate=cost(6),
         name="gate_forward",
     )(*args)
@@ -475,7 +475,7 @@
             pltpu.VMEM((rows, LANES), f32), pltpu.VMEM((rows, LANES), f32), pltpu.VMEM((chunks, N, 3 * CH), bf16),
             pltpu.VMEM((rows, LANES), f32),
         ],
-        compiler_params=params(),
+        compiler_params=params(48 * 1024 * 1024),
         cost_estimate=cost(7),
         name="gate_backward",
     )(grad, gate, ssm, conv, conv, cum, marks, sums, gain)

time: 638 us -> 637 us (level)
  Pallas kernels: 149 us -> 142 us
    unnamed x289 -> x321, local copies, waits for them, and re-layouts: 62.1 us -> 73.9 us
    pallas_call x19, Pallas kernels: 135 us -> 128 us  [call(): return lambda *args: made(*held, *args)]
  transfers between devices with their start and end apart: 96 -> 96, of which waited for: 33 -> 33; matrix products, arithmetic and copies ran while one was open for 22% -> 21% of each run, Pallas kernels for 22% -> 21%
where the time goes in v4:
time: 637 us; the launch traced here: 624 us
  waiting for transfers between devices  148 us (23%)
  Pallas kernels  142 us (22%)
  local copies, waits for them, and re-layouts  114 us (18%)
  starting transfers between devices  110 us (17%)
  matrix products  67.8 us (11%)
  other arithmetic  25.8 us (4%)
  between operations  16.6 us (3%)
    pallas_call x19, Pallas kernels, call(): return lambda *args: made(*held, *args)  128 us
    ppermute x57, waiting for transfers between devices, from_partner(): lax.ppermute(value, 'tensor', [(i, i ^ distance) for i in range(count)])  102 us
    unnamed x321, local copies, waits for them, and re-layouts  73.9 us
    ppermute x57, starting transfers between devices, from_partner(): lax.ppermute(value, 'tensor', [(i, i ^ distance) for i in range(count)])  52.1 us
    ppermute x4, waiting for transfers between devices, to_micro(): came.append(lax.ppermute(piece, ('section', 'ctx'), route))  28.1 us
    ppermute x8, starting transfers between devices, to_owners(): pieces.append(lax.ppermute(piece, ('section', 'ctx'), route))  17.4 us
    ppermute x4, starting transfers between devices, to_micro(): came.append(lax.ppermute(piece, ('section', 'ctx'), route))  13.5 us
  transfers between devices with their start and end apart: 96, of which 33 were waited for; matrix products, arithmetic and copies ran while one was open for 21% of the time, Pallas kernels for 21%

profile of v4, /device:TPU:9, one launch (start us, length us, event | category | flops | bytes accessed | tf_op | source)
XLA Modules:
  0.0 624.5 jit_solution(14466538594140549101)
XLA Ops:
  24.4 14.5 %collective-permute-done.1 = bf16[256,384]{1,0:T(8,128)(2,1)S(1)} collective-permute-done((bf16[256,384]{1,0:T(8,128)(2,1)S(1)}, bf16[256,384]{1,0:T(8,128)(2,1)S(1)}, u32[]{:S(2)}, u32[]{:S(2)}) %collective-permute-start.1) | collective-permute-done | bytes 196640 | tf_op jit(solution)/shard_map/ppermute | solution.py:1467
  39.0 12.3 %collective-permute-done.2 = bf16[256,384]{1,0:T(8,128)(2,1)S(1)} collective-permute-done((bf16[256,384]{1,0:T(8,128)(2,1)S(1)}, bf16[256,384]{1,0:T(8,128)(2,1)S(1)}, u32[]{:S(2)}, u32[]{:S(2)}) %collective-permute-start.2) | collective-permute-done | bytes 196640 | tf_op jit(solution)/shard_map/ppermute | solution.py:1467
  57.6 8.5 %collective-permute-done.5.refs_5_ = bf16[512,384]{1,0:T(8,128)(2,1)S(1)} collective-permute-done((bf16[512,384]{1,0:T(8,128)(2,1)S(1)}, bf16[512,384]{1,0:T(8,128)(2,1)S(1)}, u32[]{:S(2)}, u32[]{:S(2)}) %collective-permute-start.5) | collective-permute-done | bytes 393248 | tf_op jit(solution)/shard_map/ppermute | solution.py:1439
  66.1 9.2 %collective-permute-done.4.refs_4_ = bf16[512,384]{1,0:T(8,128)(2,1)S(1)} collective-permute-done((bf16[512,384]{1,0:T(8,128)(2,1)S(1)}, bf16[512,384]{1,0:T(8,128)(2,1)S(1)}, u32[]{:S(2)}, u32[]{:S(2)}) %collective-permute-start.4) | collective-permute-done | bytes 393248 | tf_op jit(solution)/shard_map/ppermute | solution.py:1439
  79.7 4.7 fusion.12.refs_0_.refs_1_.refs_16_.refs_7_
  93.3 16.1 %scan_forward.2 = (f32[512,1024]{1,0:T(8,128)}, f32[512,768]{1,0:T(8,128)}, f32[2,128,768]{2,1,0:T(8,128)}, f32[128,768]{1,0:T(8,128)}, f32[512,768]{1,0:T(8,128...) custom-call(bf16[512,1024]{1,0:T(8,128)(2,1)} %fusion.12.refs_0_.refs_1_.refs_16_.refs_7_, ...), custom_call_target="tpu_custom_call" | custom-call | bytes 45000000 | tf_op jit(solution)/shard_map/scan_forward/pallas_call | solution.py:219
  115.6 6.1 gate_forward.2
  144.4 6.2 collective-permute-start.22
  154.3 17.2 %collective-permute-done.15 = f32[512,384]{1,0:T(8,128)} collective-permute-done((f32[512,384]{1,0:T(8,128)}, f32[512,384]{1,0:T(8,128)}, u32[]{:S(2)}, u32[]{:S(2)}) %collective-permute-start.15) | collective-permute-done | bytes 786464 | tf_op jit(solution)/shard_map/ppermute | solution.py:1439
  181.0 11.6 %collective-permute-done.17.refs_4_ = bf16[512,384]{1,0:T(8,128)(2,1)S(1)} collective-permute-done((bf16[512,384]{1,0:T(8,128)(2,1)S(1)}, bf16[512,384]{1,0:T(8,128)(2,1)S(1)}, u32[]{:S(2)}, u32[]{:S(2)}) %collective-permute-start.17) | collective-permute-done | bytes 393248 | tf_op jit(solution)/shard_map/ppermute | solution.py:1439
  195.5 5.1 fusion.15.refs_0_.refs_1_.refs_17_.refs_5_
  210.6 16.0 %scan_forward.3 = (f32[512,1024]{1,0:T(8,128)}, f32[512,768]{1,0:T(8,128)}, f32[2,128,768]{2,1,0:T(8,128)}, f32[128,768]{1,0:T(8,128)}, f32[512,768]{1,0:T(8,128...) custom-call(bf16[512,1024]{1,0:T(8,128)(2,1)} %fusion.15.refs_0_.refs_1_.refs_17_.refs_5_, ...), custom_call_target="tpu_custom_call" | custom-call | bytes 45000000 | tf_op jit(solution)/shard_map/scan_forward/pallas_call | solution.py:219
  232.3 4.9 fusion.9.refs_7_.refs_2_
  239.7 6.5 %gate_forward.3 = (f32[512,768]{1,0:T(8,128)S(1)}, f32[512,768]{1,0:T(8,128)S(1)}, f32[2,128,768]{2,1,0:T(8,128)S(1)}, f32[8,512]{1,0:T(8,128)S(1)}) custom-call(f32[512,768]{1,0:T(8,128)} %get-tuple-element.94.refs_0_, f32[512,1024]{1,0:T(8,128)} %get-tuple-element.95.refs_1_.refs_2_.refs_4_.refs_5_.refs_3_, ...), custom_call_target="tpu_custom_call" | custom-call | bytes 18000000 | tf_op jit(solution)/shard_map/gate_forward/pallas_call | solution.py:219
  260.2 7.2 %gate_backward.2 = (f32[512,768]{1,0:T(8,128)S(1)}, bf16[512,768]{1,0:T(8,128)(2,1)S(1)}, f32[2,128,768]{2,1,0:T(8,128)S(1)}, f32[128,768]{1,0:T(8,128)S(1)}, f3...) custom-call(bf16[512,1536]{1,0:T(8,128)(2,1)S(1)} %copy-done.27, ...), custom_call_target="tpu_custom_call" | custom-call | bytes 21000000 | tf_op jit(solution)/shard_map/gate_backward/pallas_call | solution.py:219
  283.9 13.0 %intra_backward.2 = (f32[512,768]{1,0:T(8,128)}, f32[6,8,512]{2,1,0:T(8,128)}, f32[512,128]{1,0:T(8,128)}, f32[512,128]{1,0:T(8,128)}) custom-call(f32[512,768]{1,0:T(8,128)} %copy-done.26, f32[512,1024]{1,0:T(8,128)} %get-tuple-element.95.refs_1_.refs_2_.refs_4_.refs_5_.refs_3_, f32[512,1024]{1,0:T(8,128)} %get-tuple-element.95.refs_1_.refs_2_.refs_4_.refs_5_.refs_3_, ...), custom_call_target="tpu_custom_call" | custom-call | bytes 9000000 | tf_op jit(solution)/shard_map/intra_backward/pallas_call | solution.py:219
  297.6 14.1 %scan_backward.2 = (f32[512,1024]{1,0:T(8,128)}, f32[8,1024]{1,0:T(8,128)}, f32[6,8,512]{2,1,0:T(8,128)}, f32[6,8,128]{2,1,0:T(8,128)}, f32[6,8,128]{2,1,0:T(8,128)}) custom-call(bf16[1536,1536]{1,0:T(8,128)(2,1)} %pad_maximum_fusion.refs_0_, f32[512,768]{1,0:T(8,128)} %copy-done.26, f32[512,768]{1,0:T(8,128)} %get-tuple-element.106.refs_2_, ...), custom_call_target="tpu_custom_call" | custom-call | bytes 9000000 | tf_op jit(solution)/shard_map/scan_backward/pallas_call | solution.py:219
  334.4 5.9 convolution_convert_fusion.1.refs_0_.term_ref
  345.6 5.2 collective-permute-start.36
  368.0 11.1 %collective-permute-done.49 = f32[128,256]{1,0:T(8,128)S(1)} collective-permute-done((f32[128,256]{1,0:T(8,128)S(1)}, f32[128,256]{1,0:T(8,128)S(1)}, u32[]{:S(2)}, u32[]{:S(2)}) %collective-permute-start.49) | collective-permute-done | bytes 131104 | tf_op jit(solution)/shard_map/ppermute | solution.py:1439
  379.1 5.0 collective-permute-done.48
  407.2 6.9 %gate_backward.3 = (f32[512,768]{1,0:T(8,128)S(1)}, bf16[512,768]{1,0:T(8,128)(2,1)S(1)}, f32[2,128,768]{2,1,0:T(8,128)S(1)}, f32[128,768]{1,0:T(8,128)S(1)}, f3...) custom-call(f32[512,768]{1,0:T(8,128)S(1)} %get-tuple-element.307.refs_0_, ...), custom_call_target="tpu_custom_call" | custom-call | bytes 21000000 | tf_op jit(solution)/shard_map/gate_backward/pallas_call | solution.py:219
  421.7 5.9 collective-permute-start.53
  432.9 13.0 %intra_backward.3 = (f32[512,768]{1,0:T(8,128)}, f32[6,8,512]{2,1,0:T(8,128)}, f32[512,128]{1,0:T(8,128)}, f32[512,128]{1,0:T(8,128)}) custom-call(bf16[1536,1152]{1,0:T(8,128)(2,1)} %place_maps.2.refs_0_, f32[512,768]{1,0:T(8,128)} %copy-done.17, f32[512,1024]{1,0:T(8,128)} %get-tuple-element.87.refs_1_.refs_2_.refs_3_.refs_4_, ...), custom_call_target="tpu_custom_call" | custom-call | bytes 9000000 | tf_op jit(solution)/shard_map/intra_backward/pallas_call | solution.py:219
  446.6 14.0 %scan_backward.3 = (f32[512,1024]{1,0:T(8,128)}, f32[8,1024]{1,0:T(8,128)}, f32[6,8,512]{2,1,0:T(8,128)}, f32[6,8,128]{2,1,0:T(8,128)}, f32[6,8,128]{2,1,0:T(8,128)}) custom-call(f32[512,768]{1,0:T(8,128)} %copy-done.17, f32[512,768]{1,0:T(8,128)} %get-tuple-element.127.refs_1_, f32[512,1024]{1,0:T(8,128)} %get-tuple-element.87.refs_1_.refs_2_.refs_3_.refs_4_, ...), custom_call_target="tpu_custom_call" | custom-call | bytes 9000000 | tf_op jit(solution)/shard_map/scan_backward/pallas_call | solution.py:219
  496.0 5.3 convolution_convert_fusion.term_ref
  507.3 6.7 %collective-permute-done.62.refs_7_ = bf16[512,384]{1,0:T(8,128)(2,1)} collective-permute-done((bf16[512,384]{1,0:T(8,128)(2,1)}, bf16[512,384]{1,0:T(8,128)(2,1)}, u32[]{:S(2)}, u32[]{:S(2)}) %collective-permute-start.62) | collective-permute-done | bytes 393248 | tf_op jit(solution)/shard_map/ppermute | solution.py:1439
  530.9 5.2 collective-permute-done.66
  560.0 11.4 %collective-permute-done.68.refs_2_.refs_1_ = bf16[1024,384]{1,0:T(8,128)(2,1)S(1)} collective-permute-done((bf16[1024,384]{1,0:T(8,128)(2,1)S(1)}, bf16[1024,384]{1,0:T(8,128)(2,1)S(1)}, u32[]{:S(2)}, u32[]{:S(2)}) %collective-permute-start.68) | collective-permute-done | bytes 786464 | tf_op jit(solution)/shard_map/ppermute | solution.py:1439
  579.9 4.7 join_micro.2.refs_0_
  587.2 5.5 collective-permute-done.69.refs_3_
  594.7 5.3 join_micro.3
  (732 shorter events, 323.6 us)
Async XLA Ops:
  7.2 71.1 %all-gather.6.cloned.1.call-start = ((), (), s32[]{:S(2)}) async-start(), calls=%async_computation.5 | async-start | bytes 3981312 | tf_op jit(solution)/shard_map/all_gather | solution.py:1632
  18.2 93.3 %all-gather.8.cloned.1.call-start = ((), (), s32[]{:S(2)}) async-start(), calls=%async_computation.6 | async-start | bytes 2654208 | tf_op jit(solution)/shard_map/all_gather | solution.py:1632
  18.6 33.5 %collective-permute-start.9 = (bf16[192,1536]{1,0:T(8,128)(2,1)S(1)}, bf16[192,1536]{1,0:T(8,128)(2,1)S(1)}, u32[]{:S(2)}, u32[]{:S(2)}) collective-permute-start(bf16[192,1536]{1,0:T(8,128)(2,1)S(1)} %fusion.23), channel_id=1, source_target_pairs={{0,16},{16,0},{1,17},{17,1},{2,18},{18,2},{3,19},{19,3},{4,20},{20... | collective-permute-start | bytes 1769480 | tf_op jit(solution)/shard_map/ppermute | solution.py:1434
  24.4 26.9 %collective-permute-start.2 = (bf16[256,384]{1,0:T(8,128)(2,1)S(1)}, bf16[256,384]{1,0:T(8,128)(2,1)S(1)}, u32[]{:S(2)}, u32[]{:S(2)}) collective-permute-start(bf16[256,384]{1,0:T(8,128)(2,1)S(1)} %get-tuple-element.239), channel_id=1, source_target_pairs={{0,4},{4,0},{8,20},{12,16},{16,12},{20,8},{24,28},{28,24},{1,5},{5... | collective-permute-start | bytes 589832 | tf_op jit(solution)/shard_map/ppermute | solution.py:1467
  54.2 77.2 %all-gather.10.cloned.1.call-start = ((), (), s32[]{:S(2)}) async-start(), calls=%async_computation.7 | async-start | bytes 2654208 | tf_op jit(solution)/shard_map/all_gather | solution.py:1632
  78.3 117.3 %all-gather.12.cloned.1.call-start = ((), (), s32[]{:S(2)}) async-start(), calls=%async_computation.8 | async-start | bytes 3981312 | tf_op jit(solution)/shard_map/all_gather | solution.py:1632
  84.3 147.9 %all-gather.14.cloned.1.call-start = ((), (), s32[]{:S(2)}) async-start(), calls=%async_computation.9 | async-start | bytes 5308416 | tf_op jit(solution)/shard_map/all_gather | solution.py:1632
  109.4 204.5 %reduce-scatter.16.cloned.1.call-start = ((), (), s32[]{:S(2)}) async-start(), calls=%async_computation.14 | async-start | bytes 1966080
  137.9 33.6 %collective-permute-start.15 = (f32[512,384]{1,0:T(8,128)}, f32[512,384]{1,0:T(8,128)}, u32[]{:S(2)}, u32[]{:S(2)}) collective-permute-start(f32[512,384]{1,0:T(8,128)} %get-tuple-element.234), channel_id=1, source_target_pairs={{0,3},{1,2},{2,1},{3,0},{4,7},{5,6},{6,5},{7,4},{8,11},{9,10},{10,... | collective-permute-start | bytes 2359304 | tf_op jit(solution)/shard_map/ppermute | solution.py:1439
  139.1 32.4 %collective-permute-start.14 = (f32[512,384]{1,0:T(8,128)}, f32[512,384]{1,0:T(8,128)}, u32[]{:S(2)}, u32[]{:S(2)}) collective-permute-start(f32[512,384]{1,0:T(8,128)} %get-tuple-element.235), channel_id=1, source_target_pairs={{0,2},{1,3},{2,0},{3,1},{4,6},{5,7},{6,4},{7,5},{8,10},{9,11},{10,... | collective-permute-start | bytes 2359304 | tf_op jit(solution)/shard_map/ppermute | solution.py:1439
  141.3 35.3 %collective-permute-start.21 = (bf16[256,384]{1,0:T(8,128)(2,1)S(1)}, bf16[256,384]{1,0:T(8,128)(2,1)S(1)}, u32[]{:S(2)}, u32[]{:S(2)}) collective-permute-start(bf16[256,384]{1,0:T(8,128)(2,1)S(1)} %get-tuple-element.236), channel_id=1, source_target_pairs={{0,0},{4,4},{8,16},{12,20},{16,8},{20,12},{24,24},{28,28},{1,1},{5... | collective-permute-start | bytes 589832 | tf_op jit(solution)/shard_map/ppermute | solution.py:1467
  144.4 33.6 %collective-permute-start.22 = (bf16[256,384]{1,0:T(8,128)(2,1)S(1)}, bf16[256,384]{1,0:T(8,128)(2,1)S(1)}, u32[]{:S(2)}, u32[]{:S(2)}) collective-permute-start(bf16[256,384]{1,0:T(8,128)(2,1)S(1)} %get-tuple-element.237), channel_id=1, source_target_pairs={{0,4},{4,0},{8,20},{12,16},{16,12},{20,8},{24,28},{28,24},{1,5},{5... | collective-permute-start | bytes 589832 | tf_op jit(solution)/shard_map/ppermute | solution.py:1467
  200.7 27.8 %collective-permute-start.25 = (bf16[512,384]{1,0:T(8,128)(2,1)}, bf16[512,384]{1,0:T(8,128)(2,1)S(1)}, u32[]{:S(2)}, u32[]{:S(2)}) collective-permute-start(bf16[512,384]{1,0:T(8,128)(2,1)} %ordered.32.refs_1_), channel_id=1, source_target_pairs={{0,3},{1,2},{2,1},{3,0},{4,7},{5,6},{6,5},{7,4},{8,11},{9,10},{10,... | collective-permute-start | bytes 1179656 | tf_op jit(solution)/shard_map/ppermute | solution.py:1439
  201.6 26.9 %collective-permute-start.24 = (bf16[512,384]{1,0:T(8,128)(2,1)}, bf16[512,384]{1,0:T(8,128)(2,1)}, u32[]{:S(2)}, u32[]{:S(2)}) collective-permute-start(bf16[512,384]{1,0:T(8,128)(2,1)} %ordered.32.refs_1_), channel_id=1, source_target_pairs={{0,2},{1,3},{2,0},{3,1},{4,6},{5,7},{6,4},{7,5},{8,10},{9,11},{10,... | collective-permute-start | bytes 1179656 | tf_op jit(solution)/shard_map/ppermute | solution.py:1439
  203.0 25.5 %collective-permute-start.23 = (bf16[512,384]{1,0:T(8,128)(2,1)}, bf16[512,384]{1,0:T(8,128)(2,1)}, u32[]{:S(2)}, u32[]{:S(2)}) collective-permute-start(bf16[512,384]{1,0:T(8,128)(2,1)} %ordered.32.refs_1_), channel_id=1, source_target_pairs={{0,1},{1,0},{2,3},{3,2},{4,5},{5,4},{6,7},{7,6},{8,9},{9,8},{10,11... | collective-permute-start | bytes 1179656 | tf_op jit(solution)/shard_map/ppermute | solution.py:1439
  258.7 131.1 %reduce-scatter.8.cloned.1.call-start = ((), (), s32[]{:S(2)}) async-start(), calls=%async_computation.10 | async-start | bytes 5308416 | tf_op jit(solution)/shard_map/reduce_scatter | solution.py:1609
  279.2 193.9 %reduce-scatter.10.cloned.1.call-start = ((), (), s32[]{:S(2)}) async-start(), calls=%async_computation.11 | async-start | bytes 3981312 | tf_op jit(solution)/shard_map/reduce_scatter | solution.py:1609
  358.1 28.8 %collective-permute-start.43 = (bf16[512,384]{1,0:T(8,128)(2,1)S(1)}, bf16[512,384]{1,0:T(8,128)(2,1)S(1)}, u32[]{:S(2)}, u32[]{:S(2)}) collective-permute-start(bf16[512,384]{1,0:T(8,128)(2,1)S(1)} %get-tuple-element.121.refs_3_), channel_id=1, source_target_pairs={{0,3},{1,2},{2,1},{3,0},{4,7},{5,6},{6,5},{7,4},{8,11},{9,10},{10,... | collective-permute-start | bytes 1179656 | tf_op jit(solution)/shard_map/ppermute | solution.py:1439
  359.4 28.5 %collective-permute-start.42 = (bf16[512,384]{1,0:T(8,128)(2,1)S(1)}, bf16[512,384]{1,0:T(8,128)(2,1)S(1)}, u32[]{:S(2)}, u32[]{:S(2)}) collective-permute-start(bf16[512,384]{1,0:T(8,128)(2,1)S(1)} %get-tuple-element.121.refs_3_), channel_id=1, source_target_pairs={{0,2},{1,3},{2,0},{3,1},{4,6},{5,7},{6,4},{7,5},{8,10},{9,11},{10,... | collective-permute-start | bytes 1179656 | tf_op jit(solution)/shard_map/ppermute | solution.py:1439
  364.0 23.9 %collective-permute-start.41 = (bf16[512,384]{1,0:T(8,128)(2,1)S(1)}, bf16[512,384]{1,0:T(8,128)(2,1)S(1)}, u32[]{:S(2)}, u32[]{:S(2)}) collective-permute-start(bf16[512,384]{1,0:T(8,128)(2,1)S(1)} %get-tuple-element.121.refs_3_), channel_id=1, source_target_pairs={{0,1},{1,0},{2,3},{3,2},{4,5},{5,4},{6,7},{7,6},{8,9},{9,8},{10,11... | collective-permute-start | bytes 1179656 | tf_op jit(solution)/shard_map/ppermute | solution.py:1439
  397.9 143.5 %reduce-scatter.12.cloned.1.call-start = ((), (), s32[]{:S(2)}) async-start(), calls=%async_computation.12 | async-start | bytes 5308416 | tf_op jit(solution)/shard_map/reduce_scatter | solution.py:1609
  419.0 41.6 %collective-permute-start.56 = (bf16[1024,384]{1,0:T(8,128)(2,1)}, bf16[1024,384]{1,0:T(8,128)(2,1)}, u32[]{:S(2)}, u32[]{:S(2)}) collective-permute-start(bf16[1024,384]{1,0:T(8,128)(2,1)} %ordered.43.refs_1_), channel_id=1, source_target_pairs={{0,3},{1,2},{2,1},{3,0},{4,7},{5,6},{6,5},{7,4},{8,11},{9,10},{10,... | collective-permute-start | bytes 2359304 | tf_op jit(solution)/shard_map/ppermute | solution.py:1439
  420.2 40.5 %collective-permute-start.55 = (bf16[1024,384]{1,0:T(8,128)(2,1)}, bf16[1024,384]{1,0:T(8,128)(2,1)}, u32[]{:S(2)}, u32[]{:S(2)}) collective-permute-start(bf16[1024,384]{1,0:T(8,128)(2,1)} %ordered.43.refs_1_), channel_id=1, source_target_pairs={{0,2},{1,3},{2,0},{3,1},{4,6},{5,7},{6,4},{7,5},{8,10},{9,11},{10,... | collective-permute-start | bytes 2359304 | tf_op jit(solution)/shard_map/ppermute | solution.py:1439
  421.2 39.4 %collective-permute-start.54 = (bf16[1024,384]{1,0:T(8,128)(2,1)}, bf16[1024,384]{1,0:T(8,128)(2,1)}, u32[]{:S(2)}, u32[]{:S(2)}) collective-permute-start(bf16[1024,384]{1,0:T(8,128)(2,1)} %ordered.43.refs_1_), channel_id=1, source_target_pairs={{0,1},{1,0},{2,3},{3,2},{4,5},{5,4},{6,7},{7,6},{8,9},{9,8},{10,11... | collective-permute-start | bytes 2359304 | tf_op jit(solution)/shard_map/ppermute | solution.py:1439
  421.7 24.2 %collective-permute-start.53 = (f32[128,768]{1,0:T(8,128)}, f32[128,768]{1,0:T(8,128)}, u32[]{:S(2)}, u32[]{:S(2)}) collective-permute-start(f32[128,768]{1,0:T(8,128)} %copy-done.113), channel_id=1, source_target_pairs={{16,0},{17,1},{18,2},{19,3},{20,4},{21,5},{22,6},{23,7},{24,8},{25... | collective-permute-start | bytes 1179656 | tf_op jit(solution)/shard_map/ppermute | solution.py:1579
  466.0 140.9 %reduce-scatter.14.cloned.1.call-start = ((), (), s32[]{:S(2)}) async-start(), calls=%async_computation.13 | async-start | bytes 3981312 | tf_op jit(solution)/shard_map/reduce_scatter | solution.py:1609
  505.5 21.8 %collective-permute-start.81 = (f32[128,256]{1,0:T(8,128)S(1)}, f32[128,256]{1,0:T(8,128)S(1)}, u32[]{:S(2)}, u32[]{:S(2)}) collective-permute-start(f32[128,256]{1,0:T(8,128)S(1)} %get-tuple-element.271), channel_id=1, source_target_pairs={{0,3},{1,2},{2,1},{3,0},{4,7},{5,6},{6,5},{7,4},{8,11},{9,10},{10,... | collective-permute-start | bytes 393224 | tf_op jit(solution)/shard_map/ppermute | solution.py:1439
  556.1 31.1 %collective-permute-start.70 = (bf16[1024,384]{1,0:T(8,128)(2,1)S(1)}, bf16[1024,384]{1,0:T(8,128)(2,1)}, u32[]{:S(2)}, u32[]{:S(2)}) collective-permute-start(bf16[1024,384]{1,0:T(8,128)(2,1)S(1)} %copy-done.10), channel_id=1, source_target_pairs={{0,3},{1,2},{2,1},{3,0},{4,7},{5,6},{6,5},{7,4},{8,11},{9,10},{10,... | collective-permute-start | bytes 2359304 | tf_op jit(solution)/shard_map/ppermute | solution.py:1439
  557.3 35.5 %collective-permute-start.69 = (bf16[1024,384]{1,0:T(8,128)(2,1)S(1)}, bf16[1024,384]{1,0:T(8,128)(2,1)}, u32[]{:S(2)}, u32[]{:S(2)}) collective-permute-start(bf16[1024,384]{1,0:T(8,128)(2,1)S(1)} %copy-done.10), channel_id=1, source_target_pairs={{0,2},{1,3},{2,0},{3,1},{4,6},{5,7},{6,4},{7,5},{8,10},{9,11},{10,... | collective-permute-start | bytes 2359304 | tf_op jit(solution)/shard_map/ppermute | solution.py:1439
  574.5 25.6 %collective-permute-start.74 = (f32[16,1024]{1,0:T(8,128)S(1)}, f32[16,1024]{1,0:T(8,128)S(1)}, u32[]{:S(2)}, u32[]{:S(2)}) collective-permute-start(f32[16,1024]{1,0:T(8,128)S(1)} %select_add_fusion), channel_id=1, source_target_pairs={{0,12},{4,0},{8,4},{12,8},{1,13},{5,1},{9,5},{13,9},{2,14},{6,2},{... | collective-permute-start | bytes 196616 | tf_op jit(solution)/shard_map/ppermute | solution.py:1793
  577.4 22.6 %collective-permute-start.73 = (f32[16,1024]{1,0:T(8,128)S(1)}, f32[16,1024]{1,0:T(8,128)S(1)}, u32[]{:S(2)}, u32[]{:S(2)}) collective-permute-start(f32[16,1024]{1,0:T(8,128)S(1)} %select_add_fusion), channel_id=1, source_target_pairs={{0,8},{4,12},{8,0},{12,4},{1,9},{5,13},{9,1},{13,5},{2,10},{6,14},... | collective-permute-start | bytes 196616 | tf_op jit(solution)/shard_map/ppermute | solution.py:1793
  577.4 22.6 %collective-permute-start.72 = (f32[16,1024]{1,0:T(8,128)S(1)}, f32[16,1024]{1,0:T(8,128)S(1)}, u32[]{:S(2)}, u32[]{:S(2)}) collective-permute-start(f32[16,1024]{1,0:T(8,128)S(1)} %select_add_fusion), channel_id=1, source_target_pairs={{0,4},{4,8},{8,12},{12,0},{1,5},{5,9},{9,13},{13,1},{2,6},{6,10},{... | collective-permute-start | bytes 196616 | tf_op jit(solution)/shard_map/ppermute | solution.py:1793
  (216 other events, 1509.7 us)
Sparse Core Ops, SparseCore 0:
  18.3 44.2 all-gather.5
  64.2 34.0 all-gather.7
  99.9 30.7 all-gather.9
  132.2 46.3 all-gather.11
  180.1 52.1 all-gather.13
  258.9 33.7 reduce-scatter.15
  295.5 53.7 reduce-scatter.7
  398.0 45.0 reduce-scatter.9
  466.1 56.0 reduce-scatter.11
  550.8 48.5 reduce-scatter.13
